TPU v7x, 32 devices: a whole 2x2x4 slice. The times are simulated.
32 devices in a mesh: tile: 8 (over z, y), chan: 4 (over x, core).
Axes of the slice: x: 2, y: 2, z: 4, core: 2. Of those that a mesh axis runs over, the one named last changes fastest.
Arguments:
- seq_grad: bfloat16 [9216, 1536], P('tile', 'chan'), may hold values from -6 to 6
- token_slot: int32 [4608], P('tile'), may hold values from 0 to 9215, as said below
- pixels: bfloat16 [4608, 1536], P('tile', 'chan'), may hold values from -6 to 6
- dw_kernel: float32 [49, 1536], P(None, 'chan'), may hold values from -0.875 to 0.875
- ln_gain: float32 [1536], P('chan'), may hold values from 0.5 to 2
- ln_bias: float32 [1536], P('chan'), may hold values from -3 to 3
- w_in: bfloat16 [1536, 6144], P(None, 'chan'), may hold values from -0.15625 to 0.15625
- b_in: float32 [6144], P('chan'), may hold values from -3 to 3
- w_out: bfloat16 [6144, 1536], P('chan'), may hold values from -0.078125 to 0.078125
- layer_scale: float32 [1536], replicated, may hold values from 0.3 to 1.5
Outputs:
- grad_input: bfloat16 [4608, 1536], P('tile', 'chan')
- grad_w_in: float32 [1536, 6144], P('tile', 'chan')
- grad_w_out: float32 [6144, 1536], P('chan', 'tile')
- grad_kernel: float32 [49, 1536], P(None, 'chan')
Inputs may be any that keep to these rules, and one draw needn't show every extreme that they name: No two visual tokens name the same slot. Slot s belongs to sequence shard s // 1152. The 576 tokens of one device (an aligned block of token_slot) take at most 144 slots of any one shard, and exactly 144 from some shard in every block.
All inputs are finite; a program needn't handle non-finite values.
Results may differ from a plain program's by a relative error of at most 0.015.
Values may be sent and summed in bfloat16 or wider, within the bound.
A program may use at most 128 MiB of HBM per device.

v0:
```python
import math

import jax
import jax.numpy as jnp
from jax import lax
from jax.sharding import PartitionSpec as P

C = 1536
KSIZE = 7
PAGE_SIDE = 48


EPS = 1e-06


def extended_2(value, sides, width):
    for axis, dim in sides:
        peers, length = (lax.axis_size(axis), value.shape[dim])
        up = [(i, (i + 1) % peers) for i in range(peers)]
        down = [(j, i) for i, j in up]
        last = lax.slice_in_dim(value, length - width, length, axis=dim)
        first = lax.slice_in_dim(value, 0, width, axis=dim)
        before = lax.ppermute(last, axis, up)
        after = lax.ppermute(first, axis, down)
        value = jnp.concatenate([before, value, after], axis=dim)
    return value


def gelu_parts(preact):
    normal_cdf = 0.5 * (1.0 + jax.scipy.special.erf(preact * 0.7071067811865476))
    density = jnp.exp(-0.5 * preact * preact) * 0.3989422804014327
    return (preact * normal_cdf, normal_cdf + preact * density)


def depthwise(padded, kernel, rows, cols):
    total = jnp.zeros((rows, cols, padded.shape[2]), jnp.float32)
    for row_off in range(KSIZE):
        for col_off in range(KSIZE):
            window = padded[row_off : row_off + rows, col_off : col_off + cols, :]
            total = total + kernel[row_off * KSIZE + col_off] * window
    return total


def page_edges(extended, band_index, tiles_page, reach):
    height = extended.shape[0]
    row_ids = lax.broadcasted_iota(jnp.int32, (height, 1, 1), 0)
    first = band_index % tiles_page == 0
    final = band_index % tiles_page == tiles_page - 1
    dropped = (row_ids < reach) & first | (row_ids >= height - reach) & final
    kept = jnp.where(dropped, jnp.zeros_like(extended), extended)
    return jnp.pad(kept, ((0, 0), (reach, reach), (0, 0)))


def shards(
    seq_grad, token_slot, pixels, dw_kernel, ln_gain, ln_bias, w_in, b_in, w_out, layer_scale
):
    tiles = lax.axis_size("tile")
    position = lax.axis_index("tile")
    band_index = (position + 1) % tiles
    slots = seq_grad.shape[0]
    capacity = slots // tiles
    tok_dev, chan_dev = pixels.shape
    reach = KSIZE // 2
    source = token_slot // slots
    local_slot = token_slot % slots
    onehot = (source[:, None] == jnp.arange(tiles, dtype=jnp.int32)[None, :]).astype(jnp.int32)
    ranks = jnp.sum((jnp.cumsum(onehot, axis=0) - onehot) * onehot, axis=1)
    seat = source * capacity + ranks
    request = (
        jnp.zeros((tiles * capacity,), jnp.int32).at[seat].set(local_slot).reshape(tiles, capacity)
    )
    found = jnp.take(
        seq_grad, lax.all_to_all(request, "tile", split_axis=0, concat_axis=0, tiled=True), axis=0
    )
    arrived = lax.all_to_all(found, "tile", split_axis=0, concat_axis=0, tiled=True)
    upstream = jnp.take(arrived.reshape(tiles * capacity, chan_dev), seat, axis=0)
    rows = tok_dev // PAGE_SIDE
    tiles_page = PAGE_SIDE // rows
    grid = pixels.reshape(rows, PAGE_SIDE, chan_dev)
    extended = extended_2(grid, (("tile", 0),), reach)
    padded = page_edges(extended.astype(jnp.float32), band_index, tiles_page, reach)
    mixed = depthwise(padded, dw_kernel, rows, PAGE_SIDE).reshape(tok_dev, chan_dev)
    total = lax.psum(jnp.sum(mixed, axis=1), "chan")
    center = mixed - (total / C)[:, None]
    spread = lax.psum(jnp.sum(center * center, axis=1), "chan")
    inv_std = lax.rsqrt(spread / C + EPS)[:, None]
    normed = center * inv_std
    ln_part = (normed * ln_gain + ln_bias).astype(jnp.bfloat16)
    ln_out, upstream_all = (
        lax.all_gather(ln_part, "chan", axis=1, tiled=True),
        lax.all_gather(upstream, "chan", axis=1, tiled=True),
    )
    scaled = (upstream_all.astype(jnp.float32) * layer_scale).astype(jnp.bfloat16)
    preact = jnp.dot(ln_out, w_in, preferred_element_type=jnp.float32) + b_in
    act_val, act_slope = gelu_parts(preact)
    hidden = act_val.astype(jnp.bfloat16)
    back_hidden = lax.dot_general(
        scaled, w_out, (((1,), (1,)), ((), ())), preferred_element_type=jnp.float32
    )
    back_pre = (back_hidden * act_slope).astype(jnp.bfloat16)
    factor = 1.0 / math.sqrt(tok_dev * tiles)
    columns = ln_out
    grad_w_in = lax.psum_scatter(
        lax.dot_general(
            columns, back_pre, (((0,), (0,)), ((), ())), preferred_element_type=jnp.float32
        )
        * factor,
        "tile",
        scatter_dimension=0,
        tiled=True,
    )
    columns = scaled
    grad_w_out = lax.psum_scatter(
        lax.dot_general(
            columns, hidden, (((0,), (0,)), ((), ())), preferred_element_type=jnp.float32
        )
        * factor,
        "tile",
        scatter_dimension=0,
        tiled=True,
    ).T
    partial_sum = lax.dot_general(
        back_pre, w_in, (((1,), (1,)), ((), ())), preferred_element_type=jnp.float32
    )
    back_norm = lax.psum_scatter(
        partial_sum.astype(jnp.bfloat16), "chan", scatter_dimension=1, tiled=True
    ).astype(jnp.float32)
    grad_normed = back_norm * ln_gain
    sum_grad, sum_cross = lax.psum(
        (jnp.sum(grad_normed, axis=1), jnp.sum(grad_normed * normed, axis=1)), "chan"
    )
    grad_mixed = inv_std * (
        grad_normed - (sum_grad / C)[:, None] - normed * (sum_cross / C)[:, None]
    )
    grad_grid = grad_mixed.reshape(rows, PAGE_SIDE, chan_dev)
    grad_ext = extended_2(grad_grid.astype(jnp.bfloat16), (("tile", 0),), reach).astype(
        grad_grid.dtype
    )
    grad_pad = page_edges(grad_ext, band_index, tiles_page, reach)
    back_conv = depthwise(grad_pad, dw_kernel[::-1], rows, PAGE_SIDE).reshape(tok_dev, chan_dev)
    grad_input = (upstream.astype(jnp.float32) + back_conv).astype(jnp.bfloat16)
    taps = []
    for row_off in range(KSIZE):
        for col_off in range(KSIZE):
            window = padded[row_off : row_off + rows, col_off : col_off + PAGE_SIDE, :]
            taps.append(jnp.sum(window * grad_grid, axis=(0, 1)))
    grad_kernel = lax.psum(jnp.stack(taps) * factor, "tile")
    return (grad_input, grad_w_in, grad_w_out, grad_kernel)


def solution(mesh):
    placed = (
        P("tile", "chan"),
        P("tile"),
        P("tile", "chan"),
        P(None, "chan"),
        P("chan"),
        P("chan"),
        P(None, "chan"),
        P("chan"),
        P("chan", None),
        P(),
    )
    return jax.shard_map(
        shards,
        mesh=mesh,
        in_specs=placed,
        out_specs=(P("tile", "chan"), P("tile", "chan"), P("chan", "tile"), P(None, "chan")),
        check_vma=False,
    )
```

profile of v0, /device:TPU:0, one launch (start us, length us, event | category | flops | bytes accessed | tf_op | source)
XLA Modules:
  0.0 597.6 jit_solution(6697986136220048852)
XLA Ops:
  7.2 1.0 fusion.108
  8.3 6.1 %collective-permute-start.1 = (bf16[3,48,384]{2,1,0:T(8,128)(2,1)S(1)}, bf16[3,48,384]{2,1,0:T(8,128)(2,1)S(1)}, u32[]{:S(2)}, u32[]{:S(2)}) collective-permute-start(bf16[3,48,384]{2,1,0:T(8,128)(2,1)S(1)} %bitcast.50), channel_id=1, source_target_pairs={{4,0},{8,4},{12,8},{16,12},{20,16},{24,20},{28,24},{0,28},{5,1},{9... | collective-permute-start | bytes 331784 | tf_op jit(solution)/shard_map/ppermute | solution.py:24
  14.3 1.0 slice_reduce_fusion.46
  15.4 1.9 slice_reduce_fusion.48
  17.4 1.9 slice_reduce_fusion.47
  19.3 1.3 add_select_fusion
  20.6 1.4 reduce-window.6
  23.5 1.2 convert_select_fusion.1
  25.0 6.5 %fusion.106 = (f32[12,48]{1,0:T(8,128)S(1)}, f32[12,48,384]{2,1,0:T(8,128)S(1)}) fusion(f32[384]{0:T(512)S(1)} %get-tuple-element.55, f32[384]{0:T(512)S(1)} %get-tuple-element.102, f32[384]{0:T(512)S(1)} %get-tuple-element.103, f32[18,48,384]{2,1,0:T(8,128)S(1)} %convert_select_fusion.1, f32[384]{0:T(512)S(1)} %get-tuple-element.56, ...), kind=kLoop, calls=%fused_computation.339 | loop fusion | flops 21675456 | bytes 8507648 | tf_op jit(solution)/shard_map/reduce_sum | solution.py:83
  31.8 6.3 %psum.35 = f32[576]{0:T(1024)S(1)} all-reduce(f32[576]{0:T(1024)S(1)} %reduce_sum.492), channel_id=1, replica_groups=mesh['tile'=8,'chan'=4] {'chan'}, use_global_device_ids=true, to_apply=%region_5.6 | all-reduce | flops 576 | bytes 4608 | tf_op jit(solution)/shard_map/psum | solution.py:83
  38.5 6.0 psum.36
  44.5 1.3 add_convert_fusion
  46.4 4.3 scatter_custom_fusion
  50.8 12.3 %all_to_all.20 = s32[8,1,144]{2,1,0:T(1,128)S(1)} all-to-all(s32[8,1,144]{2,1,0:T(1,128)S(1)} %all_to_all.13), channel_id=1, replica_groups=mesh['tile'=8,'chan'=4] {'tile'}, dimensions={0} | all-to-all | bytes 9216 | tf_op jit(solution)/shard_map/all_to_all | solution.py:73
  63.2 4.3 gather_fusion
  67.5 1.1 broadcast_select_fusion
  68.7 3.6 all-to-all-start.1
  72.9 20.0 %all-to-all-done.1 = bf16[8,144,384]{2,1,0:T(8,128)(2,1)S(1)} async-done(((bf16[8,144,384]{2,1,0:T(8,128)(2,1)}), bf16[8,144,384]{2,1,0:T(8,128)(2,1)S(1)}, u32[]{:S(2)}, u32[]{:S(2)}) %all-to-all-start.1) | async-done | bytes 884768 | tf_op jit(solution)/shard_map/all_to_all | solution.py:75
  92.9 2.9 gather_fusion.1
  95.8 1.5 broadcast_select_fusion.1
  97.6 7.6 %convolution_add_fusion = f32[576,1536]{1,0:T(8,128)} fusion(bf16[576,1536]{1,0:T(8,128)(2,1)} %all-gather.5.cloned.1.call-done, bf16[1536,1536]{1,0:T(8,128)(2,1)} %param.16, f32[1536]{0:T(1024)} %param.17), kind=kOutput, calls=%fused_computation.15 | convolution fusion | flops 2718793728 | bytes 10033152 | tf_op jit(solution)/shard_map/dot_general | solution.py:94
  105.2 11.7 %all-gather.3.cloned.1.call-done = bf16[576,1536]{1,0:T(8,128)(2,1)} async-done(((bf16[576,384]{1,0:T(8,128)(2,1)}), bf16[576,1536]{1,0:T(8,128)(2,1)}) %all-gather.3.cloned.1.call-update) | async-done | bytes 1769488 | tf_op jit(solution)/shard_map/all_gather | solution.py:91
  117.0 6.5 %fusion.5 = bf16[576,1536]{1,0:T(8,128)(2,1)S(1)} fusion(f32[576,1536]{1,0:T(8,128)} %convolution_add_fusion, bf16[1536,1536]{1,0:T(8,128)(2,1)} %param.18, bf16[576,1536]{1,0:T(8,128)(2,1)} %all-gather.3.cloned.1.call-done, f32[1536]{0:T(1024)S(1)} %copy-done.94), kind=kOutput, calls=%fused_computation.11 | convolution fusion | flops 2729410560 | bytes 11802624 | tf_op jit(solution)/shard_map/dot_general | solution.py:97
  123.5 1.2 copy-done.95
  124.7 6.5 %convolution_convert_fusion = bf16[576,1536]{1,0:T(8,128)(2,1)} fusion(bf16[576,1536]{1,0:T(8,128)(2,1)S(1)} %fusion.5, bf16[1536,1536]{1,0:T(8,128)(2,1)} %param.16), kind=kOutput, calls=%fused_computation.16 | convolution fusion | flops 2718793728 | bytes 8257536 | tf_op jit(solution)/shard_map/dot_general | solution.py:122
  131.2 3.9 copy.20
  135.2 30.8 %reduce-scatter.10.cloned.1.call-done = bf16[384,576]{1,0:T(8,128)(2,1)} async-done(((bf16[1536,576]{1,0:T(8,128)(2,1)}), bf16[384,576]{1,0:T(8,128)(2,1)}) %reduce-scatter.10.cloned.1.call-update) | async-done | bytes 442384
  165.9 2.0 copy.21
  167.9 1.9 fusion.98
  169.8 6.0 all-reduce.3
  175.8 1.6 subtract_multiply_fusion
  177.3 1.5 multiply_reduce_fusion.36
  178.9 2.1 multiply_reduce_fusion.18
  181.0 2.0 multiply_reduce_fusion
  183.7 0.7 broadcast_multiply_fusion
  184.7 10.1 %convolution_multiply_fusion = f32[1536,1536]{1,0:T(8,128)} fusion(f32[576,1536]{1,0:T(8,128)} %convolution_add_fusion, bf16[576,1536]{1,0:T(8,128)(2,1)} %all-gather.3.cloned.1.call-done, f32[1536]{0:T(1024)} %param.19), kind=kOutput, calls=%fused_computation.3 | convolution fusion | flops 2727346176 | bytes 14751744 | tf_op jit(solution)/shard_map/dot_general | solution.py:114
  194.9 9.6 %convolution_multiply_fusion.1 = f32[1536,1536]{1,0:T(8,128)} fusion(bf16[576,1536]{1,0:T(8,128)(2,1)} %all-gather.5.cloned.1.call-done, bf16[576,1536]{1,0:T(8,128)(2,1)} %copy-done.95), kind=kOutput, calls=%fused_computation.4 | convolution fusion | flops 2720268288 | bytes 12976128 | tf_op jit(solution)/shard_map/dot_general | solution.py:104
  204.9 1.8 collective-permute-start.2
  206.7 3.0 collective-permute-start.3
  209.7 2.9 collective-permute-done.2
  212.6 1.0 collective-permute-done.3
  213.6 0.8 convert_select_fusion
  214.8 7.2 %fusion.92 = f32[12,48,384]{2,1,0:T(8,128)S(1)} fusion(f32[18,48,384]{2,1,0:T(8,128)S(1)} %convert_select_fusion, f32[384]{0:T(512)S(1)} %copy-done.18, f32[384]{0:T(512)S(1)} %copy-done.20, f32[384]{0:T(512)S(1)} %copy-done.24, f32[384]{0:T(512)S(1)} %copy-done.26, f32[384]{0:T(512)S(1)} %copy-done.28, f32[384]{0:T(512)S(1)} %copy-done.30, ...), kind=kLoop, calls=%fused_computation.189 | loop fusion | flops 21454848 | bytes 8501760 | tf_op jit(solution)/shard_map/add | solution.py:40
  222.0 1.6 fusion.96
  223.6 30.9 %all-reduce.6.cloned.1.call-done = f32[49,384]{1,0:T(8,128)} async-done(((f32[49,384]{1,0:T(8,128)}), f32[49,384]{1,0:T(8,128)}) %all-reduce.6.cloned.1.call-update) | async-done | bytes 75280 | tf_op jit(solution)/shard_map/psum | solution.py:147
  254.5 167.6 %reduce-scatter.8.cloned.1.call-done = f32[192,1536]{1,0:T(8,128)} async-done(((f32[1536,1536]{1,0:T(8,128)}), f32[192,1536]{1,0:T(8,128)}) %reduce-scatter.8.cloned.1.call-update) | async-done | bytes 1179664 | tf_op jit(solution)/shard_map/reduce_scatter | solution.py:113
  422.1 167.0 %reduce-scatter.6.cloned.1.call-done = f32[192,1536]{1,0:T(8,128)} async-done(((f32[1536,1536]{1,0:T(8,128)}), f32[192,1536]{1,0:T(8,128)}) %reduce-scatter.6.cloned.1.call-update) | async-done | bytes 1179664 | tf_op jit(solution)/shard_map/reduce_scatter | solution.py:103
  589.2 1.5 copy.27
  (282 shorter events, 4.7 us)
Async XLA Ops:
  7.2 56.0 %copy-start = (bf16[1152,384]{1,0:T(8,128)(2,1)S(1)}, bf16[1152,384]{1,0:T(8,128)(2,1)}, u32[]{:S(2)}) copy-start(bf16[1152,384]{1,0:T(8,128)(2,1)} %param.10) | copy-start | bytes 2654212
  7.2 90.4 %all-gather.5.cloned.1.call-start = ((), (), s32[]{:S(2)}) async-start(), calls=%async_computation.6 | async-start | bytes 2211840 | tf_op jit(solution)/shard_map/all_gather | solution.py:90
  8.3 15.2 %collective-permute-start.1 = (bf16[3,48,384]{2,1,0:T(8,128)(2,1)S(1)}, bf16[3,48,384]{2,1,0:T(8,128)(2,1)S(1)}, u32[]{:S(2)}, u32[]{:S(2)}) collective-permute-start(bf16[3,48,384]{2,1,0:T(8,128)(2,1)S(1)} %bitcast.50), channel_id=1, source_target_pairs={{4,0},{8,4},{12,8},{16,12},{20,16},{24,20},{28,24},{0,28},{5,1},{9... | collective-permute-start | bytes 331784 | tf_op jit(solution)/shard_map/ppermute | solution.py:24
  14.3 9.1 %collective-permute-start = (bf16[3,48,384]{2,1,0:T(8,128)(2,1)S(1)}, bf16[3,48,384]{2,1,0:T(8,128)(2,1)S(1)}, u32[]{:S(2)}, u32[]{:S(2)}) collective-permute-start(bf16[3,48,384]{2,1,0:T(8,128)(2,1)S(1)} %bitcast.49), channel_id=1, source_target_pairs={{0,4},{4,8},{8,12},{12,16},{16,20},{20,24},{24,28},{28,0},{1,5},{5... | collective-permute-start | bytes 331784 | tf_op jit(solution)/shard_map/ppermute | solution.py:23
  15.4 16.2 %copy-start.3 = (f32[384]{0:T(512)}, f32[384]{0:T(512)S(1)}, u32[]{:S(2)}) copy-start(f32[384]{0:T(512)S(1)} %get-tuple-element.95) | copy-start | bytes 4612
  15.4 16.2 %copy-start.5 = (f32[384]{0:T(512)}, f32[384]{0:T(512)S(1)}, u32[]{:S(2)}) copy-start(f32[384]{0:T(512)S(1)} %get-tuple-element.96) | copy-start | bytes 4612
  15.4 16.2 %copy-start.7 = (f32[384]{0:T(512)}, f32[384]{0:T(512)S(1)}, u32[]{:S(2)}) copy-start(f32[384]{0:T(512)S(1)} %get-tuple-element.97) | copy-start | bytes 4612
  15.4 16.2 %copy-start.9 = (f32[384]{0:T(512)}, f32[384]{0:T(512)S(1)}, u32[]{:S(2)}) copy-start(f32[384]{0:T(512)S(1)} %get-tuple-element.98) | copy-start | bytes 4612
  15.4 16.2 %copy-start.11 = (f32[384]{0:T(512)}, f32[384]{0:T(512)S(1)}, u32[]{:S(2)}) copy-start(f32[384]{0:T(512)S(1)} %get-tuple-element.99) | copy-start | bytes 4612
  15.4 16.2 %copy-start.13 = (f32[384]{0:T(512)}, f32[384]{0:T(512)S(1)}, u32[]{:S(2)}) copy-start(f32[384]{0:T(512)S(1)} %get-tuple-element.100) | copy-start | bytes 4612
  15.4 16.2 %copy-start.15 = (f32[384]{0:T(512)}, f32[384]{0:T(512)S(1)}, u32[]{:S(2)}) copy-start(f32[384]{0:T(512)S(1)} %get-tuple-element.101) | copy-start | bytes 4612
  15.4 16.2 %copy-start.17 = (f32[384]{0:T(512)}, f32[384]{0:T(512)S(1)}, u32[]{:S(2)}) copy-start(f32[384]{0:T(512)S(1)} %get-tuple-element.102) | copy-start | bytes 4612
  15.4 16.2 %copy-start.19 = (f32[384]{0:T(512)}, f32[384]{0:T(512)S(1)}, u32[]{:S(2)}) copy-start(f32[384]{0:T(512)S(1)} %get-tuple-element.103) | copy-start | bytes 4612
  17.3 14.3 %copy-start.21 = (f32[384]{0:T(512)}, f32[384]{0:T(512)S(1)}, u32[]{:S(2)}) copy-start(f32[384]{0:T(512)S(1)} %get-tuple-element.55) | copy-start | bytes 4612
  17.3 14.3 %copy-start.23 = (f32[384]{0:T(512)}, f32[384]{0:T(512)S(1)}, u32[]{:S(2)}) copy-start(f32[384]{0:T(512)S(1)} %get-tuple-element.56) | copy-start | bytes 4612
  17.3 14.3 %copy-start.25 = (f32[384]{0:T(512)}, f32[384]{0:T(512)S(1)}, u32[]{:S(2)}) copy-start(f32[384]{0:T(512)S(1)} %get-tuple-element.57) | copy-start | bytes 4612
  17.3 14.3 %copy-start.27 = (f32[384]{0:T(512)}, f32[384]{0:T(512)S(1)}, u32[]{:S(2)}) copy-start(f32[384]{0:T(512)S(1)} %get-tuple-element.58) | copy-start | bytes 4612
  17.3 14.3 %copy-start.29 = (f32[384]{0:T(512)}, f32[384]{0:T(512)S(1)}, u32[]{:S(2)}) copy-start(f32[384]{0:T(512)S(1)} %get-tuple-element.59) | copy-start | bytes 4612
  17.4 14.3 %copy-start.31 = (f32[384]{0:T(512)}, f32[384]{0:T(512)S(1)}, u32[]{:S(2)}) copy-start(f32[384]{0:T(512)S(1)} %get-tuple-element.60) | copy-start | bytes 4612
  17.4 14.3 %copy-start.33 = (f32[384]{0:T(512)}, f32[384]{0:T(512)S(1)}, u32[]{:S(2)}) copy-start(f32[384]{0:T(512)S(1)} %get-tuple-element.61) | copy-start | bytes 4612
  17.4 14.3 %copy-start.35 = (f32[384]{0:T(512)}, f32[384]{0:T(512)S(1)}, u32[]{:S(2)}) copy-start(f32[384]{0:T(512)S(1)} %get-tuple-element.62) | copy-start | bytes 4612
  25.0 19.5 %copy-start.2 = (f32[384]{0:T(512)S(1)}, f32[384]{0:T(512)}, u32[]{:S(2)}) copy-start(f32[384]{0:T(512)} %param.14) | copy-start | bytes 4612
  25.0 19.5 %copy-start.93 = (f32[384]{0:T(512)S(1)}, f32[384]{0:T(512)}, u32[]{:S(2)}) copy-start(f32[384]{0:T(512)} %param.15) | copy-start | bytes 4612
  68.7 24.2 %all-to-all-start.1 = ((bf16[8,144,384]{2,1,0:T(8,128)(2,1)}), bf16[8,144,384]{2,1,0:T(8,128)(2,1)S(1)}, u32[]{:S(2)}, u32[]{:S(2)}) async-start(bf16[8,144,384]{2,1,0:T(8,128)(2,1)} %broadcast_select_fusion), calls=%async_computation.1 | async-start | bytes 1769472 | tf_op jit(solution)/shard_map/all_to_all | solution.py:75
  72.2 44.7 %all-gather.3.cloned.1.call-start = ((), (), s32[]{:S(2)}) async-start(), calls=%async_computation.5 | async-start | bytes 2211840 | tf_op jit(solution)/shard_map/all_gather | solution.py:91
  97.4 19.6 %copy-start.94 = (f32[1536]{0:T(1024)S(1)}, f32[1536]{0:T(1024)}, u32[]{:S(2)}) copy-start(f32[1536]{0:T(1024)} %param.19) | copy-start | bytes 18436
  97.4 68.5 %reduce-scatter.10.cloned.1.call-start = ((), (), s32[]{:S(2)}) async-start(), calls=%async_computation.10 | async-start | bytes 2457600
  135.1 32.8 %copy-start.1 = (f32[576,384]{1,0:T(8,128)S(1)}, f32[576,384]{1,0:T(8,128)}, u32[]{:S(2)}) copy-start(f32[576,384]{1,0:T(8,128)} %get-tuple-element.109) | copy-start | bytes 2654212
  135.1 119.4 %all-reduce.6.cloned.1.call-start = ((), (), s32[]{:S(2)}) async-start(), calls=%async_computation.9 | async-start | bytes 172032 | tf_op jit(solution)/shard_map/psum | solution.py:147
  184.4 237.8 %reduce-scatter.8.cloned.1.call-start = ((), (), s32[]{:S(2)}) async-start(), calls=%async_computation.8 | async-start | bytes 10616832 | tf_op jit(solution)/shard_map/reduce_scatter | solution.py:113
  194.8 394.4 %reduce-scatter.6.cloned.1.call-start = ((), (), s32[]{:S(2)}) async-start(), calls=%async_computation.7 | async-start | bytes 10616832 | tf_op jit(solution)/shard_map/reduce_scatter | solution.py:103
  204.5 9.9 %copy-start.4 = (f32[384]{0:T(512)S(1)}, f32[384]{0:T(512)}, u32[]{:S(2)}) copy-start(f32[384]{0:T(512)} %copy-done.3) | copy-start | bytes 4612
  204.5 9.9 %copy-start.6 = (f32[384]{0:T(512)S(1)}, f32[384]{0:T(512)}, u32[]{:S(2)}) copy-start(f32[384]{0:T(512)} %copy-done.5) | copy-start | bytes 4612
  204.5 9.9 %copy-start.8 = (f32[384]{0:T(512)S(1)}, f32[384]{0:T(512)}, u32[]{:S(2)}) copy-start(f32[384]{0:T(512)} %copy-done.7) | copy-start | bytes 4612
  204.5 9.9 %copy-start.10 = (f32[384]{0:T(512)S(1)}, f32[384]{0:T(512)}, u32[]{:S(2)}) copy-start(f32[384]{0:T(512)} %copy-done.9) | copy-start | bytes 4612
  204.5 9.9 %copy-start.12 = (f32[384]{0:T(512)S(1)}, f32[384]{0:T(512)}, u32[]{:S(2)}) copy-start(f32[384]{0:T(512)} %copy-done.11) | copy-start | bytes 4612
  204.5 9.9 %copy-start.14 = (f32[384]{0:T(512)S(1)}, f32[384]{0:T(512)}, u32[]{:S(2)}) copy-start(f32[384]{0:T(512)} %copy-done.13) | copy-start | bytes 4612
  204.5 9.9 %copy-start.16 = (f32[384]{0:T(512)S(1)}, f32[384]{0:T(512)}, u32[]{:S(2)}) copy-start(f32[384]{0:T(512)} %copy-done.15) | copy-start | bytes 4612
  204.5 9.9 %copy-start.18 = (f32[384]{0:T(512)S(1)}, f32[384]{0:T(512)}, u32[]{:S(2)}) copy-start(f32[384]{0:T(512)} %copy-done.17) | copy-start | bytes 4612
  204.5 9.9 %copy-start.20 = (f32[384]{0:T(512)S(1)}, f32[384]{0:T(512)}, u32[]{:S(2)}) copy-start(f32[384]{0:T(512)} %copy-done.19) | copy-start | bytes 4612
  204.5 9.9 %copy-start.22 = (f32[384]{0:T(512)S(1)}, f32[384]{0:T(512)}, u32[]{:S(2)}) copy-start(f32[384]{0:T(512)} %copy-done.21) | copy-start | bytes 4612
  204.6 9.9 %copy-start.24 = (f32[384]{0:T(512)S(1)}, f32[384]{0:T(512)}, u32[]{:S(2)}) copy-start(f32[384]{0:T(512)} %copy-done.23) | copy-start | bytes 4612
  204.6 9.9 %copy-start.26 = (f32[384]{0:T(512)S(1)}, f32[384]{0:T(512)}, u32[]{:S(2)}) copy-start(f32[384]{0:T(512)} %copy-done.25) | copy-start | bytes 4612
  204.6 9.9 %copy-start.28 = (f32[384]{0:T(512)S(1)}, f32[384]{0:T(512)}, u32[]{:S(2)}) copy-start(f32[384]{0:T(512)} %copy-done.27) | copy-start | bytes 4612
  204.6 9.9 %copy-start.30 = (f32[384]{0:T(512)S(1)}, f32[384]{0:T(512)}, u32[]{:S(2)}) copy-start(f32[384]{0:T(512)} %copy-done.29) | copy-start | bytes 4612
  204.6 9.9 %copy-start.32 = (f32[384]{0:T(512)S(1)}, f32[384]{0:T(512)}, u32[]{:S(2)}) copy-start(f32[384]{0:T(512)} %copy-done.31) | copy-start | bytes 4612
  204.9 7.7 %collective-permute-start.2 = (bf16[3,48,384]{2,1,0:T(8,128)(2,1)S(1)}, bf16[3,48,384]{2,1,0:T(8,128)(2,1)S(1)}, u32[]{:S(2)}, u32[]{:S(2)}) collective-permute-start(bf16[3,48,384]{2,1,0:T(8,128)(2,1)S(1)} %get-tuple-element.112), channel_id=1, source_target_pairs={{0,4},{4,8},{8,12},{12,16},{16,20},{20,24},{24,28},{28,0},{1,5},{5... | collective-permute-start | bytes 331784 | tf_op jit(solution)/shard_map/ppermute | solution.py:23
  206.7 6.9 %collective-permute-start.3 = (bf16[3,48,384]{2,1,0:T(8,128)(2,1)S(1)}, bf16[3,48,384]{2,1,0:T(8,128)(2,1)S(1)}, u32[]{:S(2)}, u32[]{:S(2)}) collective-permute-start(bf16[3,48,384]{2,1,0:T(8,128)(2,1)S(1)} %get-tuple-element.113), channel_id=1, source_target_pairs={{4,0},{8,4},{12,8},{16,12},{20,16},{24,20},{28,24},{0,28},{5,1},{9... | collective-permute-start | bytes 331784 | tf_op jit(solution)/shard_map/ppermute | solution.py:24
  (59 other events, 333.2 us)
Sparse Core Ops, SparseCore 0:
  46.0 21.4 all-gather.4
  97.5 19.4 all-gather.2
  135.2 30.6 reduce-scatter.9
  184.5 69.9 all-reduce.5
  259.0 163.1 reduce-scatter.7
  426.6 162.5 reduce-scatter.5
where the time goes:
time: 599 us; the launch traced here: 598 us
  waiting for transfers between devices  432 us (72%)
  matrix products  40.2 us (7%)
  other arithmetic  36.2 us (6%)
  blocking collectives  30.5 us (5%)
  local copies, waits for them, and re-layouts  27.4 us (5%)
  between operations  16.1 us (3%)
  starting transfers between devices  15 us (3%)
    reduce_scatter x1, waiting for transfers between devices, shards(): lax.psum_scatter(lax.dot_general(columns, hidden, (((0,), (0,)), ((), ())...  168 us
    reduce_scatter x1, waiting for transfers between devices, shards(): lax.psum_scatter(lax.dot_general(columns, back_pre, (((0,), (0,)), ((), (...  167 us
    psum x1, waiting for transfers between devices, shards(): grad_kernel = lax.psum(jnp.stack(taps) * factor, 'tile')  30.9 us
    unnamed x7, waiting for transfers between devices  30.9 us
    all_to_all x1, waiting for transfers between devices, shards(): lax.all_to_all(found, 'tile', split_axis=0, concat_axis=0, tiled=True)  20 us
    all_to_all x1, blocking collectives, shards(): lax.all_to_all(request, 'tile', split_axis=0, concat_axis=0, tiled=True)  12.3 us
  transfers between devices with their start and end apart: 11, of which 8 were waited for; matrix products, arithmetic and copies ran while one was open for 10% of the time, Pallas kernels for 0%

commit v1 on v0

--- a/solution.py
+++ b/solution.py
@@ -49,6 +49,52 @@
     dropped = (row_ids < reach) & first | (row_ids >= height - reach) & final
     kept = jnp.where(dropped, jnp.zeros_like(extended), extended)
     return jnp.pad(kept, ((0, 0), (reach, reach), (0, 0)))
+
+
+def pair_products(columns, values, factor):
+    tiles = lax.axis_size("tile")
+    tokens, width = columns.shape
+    lines, rows = tiles // 2, width // tiles
+    side = lax.axis_index("tile") % 2
+    blocks = columns.reshape(tokens, lines, 2, rows)
+
+    def product(which):
+        part = lax.dynamic_index_in_dim(blocks, which, 2, keepdims=False)
+        return (
+            lax.dot_general(
+                part.reshape(tokens, lines * rows),
+                values,
+                (((0,), (0,)), ((), ())),
+                preferred_element_type=jnp.float32,
+            )
+            * factor
+        )
+
+    swap = [(i, i ^ 1) for i in range(tiles)]
+    arrived = lax.ppermute(product(1 - side).astype(jnp.bfloat16), "tile", swap)
+    total = product(side) + arrived.astype(jnp.float32)
+    return total.reshape(lines, rows, values.shape[1])
+
+
+def line_sum(parts):
+    lines = parts.shape[0]
+    tiles = lax.axis_size("tile")
+    place = lax.axis_index("tile") // 2
+    result = lax.dynamic_index_in_dim(parts, place, 0, keepdims=False)
+    ups = downs = None
+    for step in range(lines - 1):
+        up_pairs = [(i, i + 2) for i in range(2 * (step + 1))]
+        down_pairs = [(tiles - 1 - i, tiles - 1 - j) for i, j in up_pairs]
+        far = jnp.clip(lines - 1 - step + place, 0, lines - 1)
+        near = jnp.clip(step - (lines - 1 - place), 0, lines - 1)
+        up = lax.dynamic_index_in_dim(parts, far, 0, keepdims=False)
+        down = lax.dynamic_index_in_dim(parts, near, 0, keepdims=False)
+        if step:
+            up = up + ups.astype(jnp.float32)
+            down = down + downs.astype(jnp.float32)
+        ups = lax.ppermute(up.astype(jnp.bfloat16), "tile", up_pairs)
+        downs = lax.ppermute(down.astype(jnp.bfloat16), "tile", down_pairs)
+    return result + ups.astype(jnp.float32) + downs.astype(jnp.float32)
 
 
 def shards(
@@ -80,9 +126,14 @@
     extended = extended_2(grid, (("tile", 0),), reach)
     padded = page_edges(extended.astype(jnp.float32), band_index, tiles_page, reach)
     mixed = depthwise(padded, dw_kernel, rows, PAGE_SIDE).reshape(tok_dev, chan_dev)
-    total = lax.psum(jnp.sum(mixed, axis=1), "chan")
-    center = mixed - (total / C)[:, None]
-    spread = lax.psum(jnp.sum(center * center, axis=1), "chan")
+    own_mean = jnp.mean(mixed, axis=1)
+    own_center = mixed - own_mean[:, None]
+    own_spread = jnp.sum(own_center * own_center, axis=1)
+    stats = lax.all_gather(jnp.stack([own_mean, own_spread]), "chan")
+    mean = jnp.mean(stats[:, 0], axis=0)
+    shift = stats[:, 0] - mean
+    spread = jnp.sum(stats[:, 1] + chan_dev * shift * shift, axis=0)
+    center = mixed - mean[:, None]
     inv_std = lax.rsqrt(spread / C + EPS)[:, None]
     normed = center * inv_std
     ln_part = (normed * ln_gain + ln_bias).astype(jnp.bfloat16)
@@ -94,37 +145,21 @@
     preact = jnp.dot(ln_out, w_in, preferred_element_type=jnp.float32) + b_in
     act_val, act_slope = gelu_parts(preact)
     hidden = act_val.astype(jnp.bfloat16)
+    factor = 1.0 / math.sqrt(tok_dev * tiles)
+    out_parts = pair_products(scaled, hidden, factor)
     back_hidden = lax.dot_general(
         scaled, w_out, (((1,), (1,)), ((), ())), preferred_element_type=jnp.float32
     )
     back_pre = (back_hidden * act_slope).astype(jnp.bfloat16)
-    factor = 1.0 / math.sqrt(tok_dev * tiles)
-    columns = ln_out
-    grad_w_in = lax.psum_scatter(
-        lax.dot_general(
-            columns, back_pre, (((0,), (0,)), ((), ())), preferred_element_type=jnp.float32
-        )
-        * factor,
-        "tile",
-        scatter_dimension=0,
-        tiled=True,
-    )
-    columns = scaled
-    grad_w_out = lax.psum_scatter(
-        lax.dot_general(
-            columns, hidden, (((0,), (0,)), ((), ())), preferred_element_type=jnp.float32
-        )
-        * factor,
-        "tile",
-        scatter_dimension=0,
-        tiled=True,
-    ).T
     partial_sum = lax.dot_general(
         back_pre, w_in, (((1,), (1,)), ((), ())), preferred_element_type=jnp.float32
     )
     back_norm = lax.psum_scatter(
         partial_sum.astype(jnp.bfloat16), "chan", scatter_dimension=1, tiled=True
     ).astype(jnp.float32)
+    in_parts = pair_products(ln_out, back_pre, factor)
+    grad_w_out = line_sum(out_parts).T
+    grad_w_in = line_sum(in_parts)
     grad_normed = back_norm * ln_gain
     sum_grad, sum_cross = lax.psum(
         (jnp.sum(grad_normed, axis=1), jnp.sum(grad_normed * normed, axis=1)), "chan"

time: 599 us -> 354 us (0.59)
  waiting for transfers between devices: 432 us -> 146 us
  starting transfers between devices: 15 us -> 44.8 us
  other arithmetic: 36.2 us -> 51.4 us
  local copies, waits for them, and re-layouts: 27.4 us -> 41.1 us
  blocking collectives: 30.5 us -> 21.1 us
  matrix products: 40.2 us -> 32.1 us
    reduce_scatter x2 -> x0, waiting for transfers between devices: 335 us -> none  [the longest x1 168 us: shards(): lax.psum_scatter(lax.dot_general(columns, hidden, (((0,), (0,)), ((), ())...]
    ppermute x0 -> x14, waiting for transfers between devices: none -> 107 us  [the longest x2 77.3 us: pair_products(): arrived = lax.ppermute(product(1 - side).astype(jnp.bfloat16), 'tile', swap)]
    unnamed x7 -> x5, waiting for transfers between devices: 30.9 us -> 0.07 us
    ppermute x0 -> x14, starting transfers between devices: none -> 30 us  [the longest x6 21 us: line_sum(): ups = lax.ppermute(up.astype(jnp.bfloat16), 'tile', up_pairs)]
    psum x1, waiting for transfers between devices: 30.9 us -> 10.6 us  [shards(): grad_kernel = lax.psum(jnp.stack(taps) * factor, 'tile')]
    convert_element_type x0 -> x7, other arithmetic: none -> 12.6 us  [the longest x4 9.32 us: line_sum(): ups = lax.ppermute(up.astype(jnp.bfloat16), 'tile', up_pairs)]
    psum x2 -> x0, blocking collectives: 12.3 us -> none  [the longest x1 6.29 us: shards(): total = lax.psum(jnp.sum(mixed, axis=1), 'chan')]
    convert_element_type x0 -> x3, local copies, waits for them, and re-layouts: none -> 6.2 us  [the longest x1 3.89 us: shards(): (upstream_all.astype(jnp.float32) * layer_scale).astype(jnp.bfloat16)]
  transfers between devices with their start and end apart: 11 -> 23, of which waited for: 8 -> 8; matrix products, arithmetic and copies ran while one was open for 10% -> 27% of each run, Pallas kernels for 0% -> 0%
where the time goes in v1:
time: 354 us; the launch traced here: 352 us
  waiting for transfers between devices  146 us (41%)
  other arithmetic  51.4 us (15%)
  starting transfers between devices  44.8 us (13%)
  local copies, waits for them, and re-layouts  41.1 us (12%)
  matrix products  32.1 us (9%)
  blocking collectives  21.1 us (6%)
  between operations  16 us (5%)
    ppermute x2, waiting for transfers between devices, pair_products(): arrived = lax.ppermute(product(1 - side).astype(jnp.bfloat16), 'tile', swap)  77.3 us
    ppermute x6, waiting for transfers between devices, line_sum(): downs = lax.ppermute(down.astype(jnp.bfloat16), 'tile', down_pairs)  24.1 us
    all_to_all x1, waiting for transfers between devices, shards(): lax.all_to_all(found, 'tile', split_axis=0, concat_axis=0, tiled=True)  21 us
    ppermute x6, starting transfers between devices, line_sum(): ups = lax.ppermute(up.astype(jnp.bfloat16), 'tile', up_pairs)  21 us
    dot_general x4, matrix products, product(): lax.dot_general(part.reshape(tokens, lines * rows), values, (((0,), (0,))...  15 us
    psum x1, waiting for transfers between devices, shards(): grad_kernel = lax.psum(jnp.stack(taps) * factor, 'tile')  10.6 us
    all_to_all x1, blocking collectives, shards(): lax.all_to_all(request, 'tile', split_axis=0, concat_axis=0, tiled=True)  9.55 us
    convert_element_type x4, other arithmetic, line_sum(): ups = lax.ppermute(up.astype(jnp.bfloat16), 'tile', up_pairs)  9.32 us
  transfers between devices with their start and end apart: 23, of which 8 were waited for; matrix products, arithmetic and copies ran while one was open for 27% of the time, Pallas kernels for 0%

profile of v1, /device:TPU:0, one launch (start us, length us, event | category | flops | bytes accessed | tf_op | source)
XLA Modules:
  0.0 352.2 jit_solution(8791043645573910614)
XLA Ops:
  8.3 3.0 collective-permute-start
  11.3 3.1 collective-permute-start.1
  17.4 1.7 slice_reduce_fusion.46
  23.5 7.3 %fusion.124 = (f32[12,48]{1,0:T(8,128)S(1)}, f32[12,48,384]{2,1,0:T(8,128)S(1)}) fusion(f32[384]{0:T(512)S(1)} %get-tuple-element.55, f32[384]{0:T(512)} %get-tuple-element.102, f32[384]{0:T(512)} %get-tuple-element.103, f32[18,48,384]{2,1,0:T(8,128)S(1)} %convert_select_fusion.1, f32[384]{0:T(512)S(1)} %get-tuple-element.56, f32[384]{0:T(512)S(1)} %get-tuple-element.57, ...), kind=kLoop, calls=%fused_computation.382 | loop fusion | flops 21675456 | bytes 8503040 | tf_op jit(solution)/shard_map/reduce_sum | solution.py:129
  31.7 5.2 %all-gather.1 = f32[4,2,576]{2,1,0:T(2,128)S(1)} all-gather(f32[1,2,576]{2,1,0:T(2,128)S(1)} %maximum_bitcast_fusion), channel_id=2, replica_groups=mesh['tile'=8,'chan'=4] {'chan'}, dimensions={0}, use_global_device_ids=true | all-gather | bytes 23040 | tf_op jit(solution)/shard_map/all_gather | solution.py:132
  37.0 2.2 add_convert_fusion
  39.8 4.1 %scatter_custom_fusion = s32[1152]{0:T(1024)S(1)} fusion(s32[576]{0:T(1024)S(1)} %get-tuple-element.107, s32[576]{0:T(1024)S(1)} %get-tuple-element.131, s32[]{:T(128)} %constant.173.clone.1), kind=kCustom, calls=%fused_computation.322 | custom fusion | bytes 4612 | tf_op jit(solution)/shard_map/scatter | solution.py:116
  44.0 9.5 %all_to_all.20 = s32[8,1,144]{2,1,0:T(1,128)S(1)} all-to-all(s32[8,1,144]{2,1,0:T(1,128)S(1)} %all_to_all.13), channel_id=1, replica_groups=mesh['tile'=8,'chan'=4] {'tile'}, dimensions={0} | all-to-all | bytes 9216 | tf_op jit(solution)/shard_map/all_to_all | solution.py:119
  53.7 4.6 %gather_fusion = bf16[1152,384]{1,0:T(8,128)(2,1)} fusion(bf16[1152,384]{1,0:T(8,128)(2,1)S(1)} %copy-done, s32[2048]{0:T(1024)S(1)} %pad_clamp_fusion), kind=kCustom, calls=%fused_computation | custom fusion | bytes 1774080 | tf_op jit(solution)/shard_map/jit(_take)/gather | solution.py:118
  58.3 2.3 broadcast_select_fusion
  60.6 3.6 %all-to-all-start.1 = ((bf16[8,144,384]{2,1,0:T(8,128)(2,1)}), bf16[8,144,384]{2,1,0:T(8,128)(2,1)S(1)}, u32[]{:S(2)}, u32[]{:S(2)}) async-start(bf16[8,144,384]{2,1,0:T(8,128)(2,1)} %broadcast_select_fusion), calls=%async_computation.1 | async-start | bytes 1769472 | tf_op jit(solution)/shard_map/all_to_all | solution.py:121
  64.8 21.0 %all-to-all-done.1 = bf16[8,144,384]{2,1,0:T(8,128)(2,1)S(1)} async-done(((bf16[8,144,384]{2,1,0:T(8,128)(2,1)}), bf16[8,144,384]{2,1,0:T(8,128)(2,1)S(1)}, u32[]{:S(2)}, u32[]{:S(2)}) %all-to-all-start.1) | async-done | bytes 884768 | tf_op jit(solution)/shard_map/all_to_all | solution.py:121
  85.8 2.9 gather_fusion.1
  88.7 1.6 broadcast_select_fusion.1
  90.6 3.9 %copy.81 = bf16[576,1536]{0,1:T(8,128)(2,1)} copy(bf16[576,1536]{1,0:T(8,128)(2,1)} %all-gather.7.cloned.1.call-done) | data formatting | bytes 3538944 | tf_op jit(solution)/shard_map/all_gather | solution.py:141
  94.5 8.8 %multiply_convert_fusion.2 = (bf16[576,1536]{1,0:T(8,128)(2,1)}, f32[576,1536]{1,0:T(8,128)}) fusion(f32[1536]{0:T(1024)S(1)} %copy-done.84, bf16[576,1536]{1,0:T(8,128)(2,1)} %all-gather.7.cloned.1.call-done, bf16[1536,1536]{1,0:T(8,128)(2,1)} %param.16), kind=kOutput, calls=%fused_computation.14 | convolution fusion | flops 2723217408 | bytes 11802624 | tf_op jit(solution)/shard_map/dot_general | solution.py:145
  103.3 6.8 %all-gather.5.cloned.1.call-done = bf16[576,1536]{1,0:T(8,128)(2,1)} async-done(((bf16[576,384]{1,0:T(8,128)(2,1)}), bf16[576,1536]{1,0:T(8,128)(2,1)}) %all-gather.5.cloned.1.call-update) | async-done | bytes 1769488 | tf_op jit(solution)/shard_map/all_gather | solution.py:142
  110.0 3.0 multiply_convert_fusion.3
  113.1 3.9 %copy.82 = bf16[576,1536]{0,1:T(8,128)(2,1)} copy(bf16[576,1536]{1,0:T(8,128)(2,1)} %multiply_convert_fusion.3) | data formatting | bytes 3538944 | tf_op jit(solution)/shard_map/convert_element_type | solution.py:144
  117.0 3.9 %constant_dynamic-slice_fusion.1 = (bf16[576,4,1,192]{0,3,2,1:T(8,128)(2,1)}, bf16[576,4,1,192]{0,3,2,1:T(8,128)(2,1)S(1)}, bf16[576,4,1,192]{0,3,2,1:T(8,128)(2,1)S(1)}, bf16[576,4,1,192]{0,3,2,1:T(8,128)(2,1)}) fusion(bf16[576,4,2,192]{0,3,2,1:T(8,128)(2,1)} %bitcast.136, s32[]{:T(128)S(6)} %select_n.113, s32[]{:T(128)S(6)} %select_n.114, ...), kind=kLoop, calls=%fused_computation.316 | loop fusion | bytes 7077896 | tf_op jit(solution)/shard_map/jit(dynamic_index_in_dim)/dynamic_slice | solution.py:62
  120.9 3.4 multiply_convert_fusion
  125.8 4.1 %fusion.5 = bf16[576,1536]{1,0:T(8,128)(2,1)S(1)} fusion(f32[576,1536]{1,0:T(8,128)S(1)} %copy-done.88, bf16[576,1536]{1,0:T(8,128)(2,1)S(1)} %copy-done.5, bf16[1536,1536]{1,0:T(8,128)(2,1)S(1)} %bitcast.149), kind=kOutput, calls=%fused_computation.13 | convolution fusion | flops 2726756352 | bytes 11796480 | tf_op jit(solution)/shard_map/dot_general | solution.py:150
  129.9 3.4 multiply_convert_fusion.1
  133.9 4.2 %convolution_convert_fusion = bf16[576,1536]{1,0:T(8,128)(2,1)} fusion(bf16[576,1536]{1,0:T(8,128)(2,1)S(1)} %fusion.5, bf16[1536,1536]{1,0:T(8,128)(2,1)S(1)} %bitcast.151), kind=kOutput, calls=%fused_computation.18 | convolution fusion | flops 2718793728 | bytes 8257536 | tf_op jit(solution)/shard_map/dot_general | solution.py:154
  138.0 3.9 %copy.83 = bf16[576,1536]{0,1:T(8,128)(2,1)} copy(bf16[576,1536]{1,0:T(8,128)(2,1)} %convolution_convert_fusion) | data formatting | bytes 3538944
  142.0 36.6 %collective-permute-done.11 = bf16[768,1536]{1,0:T(8,128)(2,1)} collective-permute-done((bf16[768,1536]{1,0:T(8,128)(2,1)}, bf16[768,1536]{1,0:T(8,128)(2,1)}, u32[]{:S(2)}, u32[]{:S(2)}) %collective-permute-start.11) | collective-permute-done | bytes 2359328 | tf_op jit(solution)/shard_map/ppermute | solution.py:74
  178.7 4.6 %convert_add_fusion = f32[768,1536]{1,0:T(8,128)S(1)} fusion(bf16[768,1536]{1,0:T(8,128)(2,1)} %collective-permute-done.11, bf16[576,768]{0,1:T(8,128)(2,1)} %bitcast.140, bf16[576,1536]{1,0:T(8,128)(2,1)} %get-tuple-element.133), kind=kOutput, calls=%fused_computation.4 | convolution fusion | flops 1362493440 | bytes 9732096 | tf_op jit(solution)/shard_map/dot_general | solution.py:64
  184.5 3.4 collective-permute-start.12
  187.9 40.6 %collective-permute-done.4 = bf16[768,1536]{1,0:T(8,128)(2,1)} collective-permute-done((bf16[768,1536]{1,0:T(8,128)(2,1)}, bf16[768,1536]{1,0:T(8,128)(2,1)}, u32[]{:S(2)}, u32[]{:S(2)}) %collective-permute-start.4) | collective-permute-done | bytes 2359328 | tf_op jit(solution)/shard_map/ppermute | solution.py:74
  228.5 3.7 %convert_add_fusion.1 = f32[768,1536]{1,0:T(8,128)S(1)} fusion(bf16[768,1536]{1,0:T(8,128)(2,1)} %collective-permute-done.4, bf16[576,768]{0,1:T(8,128)(2,1)S(1)} %bitcast.139, bf16[576,1536]{1,0:T(8,128)(2,1)S(1)} %copy-done.87), kind=kOutput, calls=%fused_computation.6 | convolution fusion | flops 1362493440 | bytes 9732096 | tf_op jit(solution)/shard_map/dot_general | solution.py:64
  232.2 2.2 copy-done.3
  235.5 4.2 %collective-permute-start.5 = (bf16[192,1536]{1,0:T(8,128)(2,1)}, bf16[192,1536]{1,0:T(8,128)(2,1)}, u32[]{:S(2)}, u32[]{:S(2)}) collective-permute-start(bf16[192,1536]{1,0:T(8,128)(2,1)} %get-tuple-element.118), channel_id=1, source_target_pairs={{0,8},{4,12},{1,9},{5,13},{2,10},{6,14},{3,11},{7,15}} | collective-permute-start | bytes 1769480 | tf_op jit(solution)/shard_map/ppermute | solution.py:95
  242.7 2.2 fusion.8
  244.9 2.1 collective-permute-start.13
  247.0 5.9 %collective-permute-done.5 = bf16[192,1536]{1,0:T(8,128)(2,1)} collective-permute-done((bf16[192,1536]{1,0:T(8,128)(2,1)}, bf16[192,1536]{1,0:T(8,128)(2,1)}, u32[]{:S(2)}, u32[]{:S(2)}) %collective-permute-start.5) | collective-permute-done | bytes 589856 | tf_op jit(solution)/shard_map/ppermute | solution.py:95
  253.0 2.4 fusion.14
  255.4 5.2 %collective-permute-start.6 = (bf16[192,1536]{1,0:T(8,128)(2,1)}, bf16[192,1536]{1,0:T(8,128)(2,1)}, u32[]{:S(2)}, u32[]{:S(2)}) collective-permute-start(bf16[192,1536]{1,0:T(8,128)(2,1)} %fusion.14), channel_id=1, source_target_pairs={{0,8},{4,12},{8,16},{12,20},{1,9},{5,13},{9,17},{13,21},{2,10},{6,... | collective-permute-start | bytes 1769480 | tf_op jit(solution)/shard_map/ppermute | solution.py:95
  262.1 6.3 %all-reduce.3 = (f32[576]{0:T(1024)S(1)}, f32[576]{0:T(1024)S(1)}) all-reduce(f32[576]{0:T(1024)S(1)} %get-tuple-element.54, f32[576]{0:T(1024)S(1)} %get-tuple-element.53), channel_id=1, replica_groups=mesh['tile'=8,'chan'=4] {'chan'}, use_global_device_ids=true, to_apply=%region_12.13 | all-reduce | flops 1152 | bytes 9216 | tf_op jit(solution)/shard_map/psum | solution.py:164
  269.8 2.1 multiply_reduce_fusion.18
  271.9 2.0 multiply_reduce_fusion
  278.5 3.2 collective-permute-start.3
  281.7 2.3 fusion.9
  286.1 2.5 fusion.15
  289.6 4.7 %collective-permute-start.7 = (bf16[192,1536]{1,0:T(8,128)(2,1)S(1)}, bf16[192,1536]{1,0:T(8,128)(2,1)S(1)}, u32[]{:S(2)}, u32[]{:S(2)}) collective-permute-start(bf16[192,1536]{1,0:T(8,128)(2,1)S(1)} %get-tuple-element.116), channel_id=1, source_target_pairs={{0,8},{4,12},{8,16},{12,20},{16,24},{20,28},{1,9},{5,13},{9,17},{1... | collective-permute-start | bytes 1769480 | tf_op jit(solution)/shard_map/ppermute | solution.py:95
  295.6 7.5 %fusion.103 = f32[12,48,384]{2,1,0:T(8,128)S(1)} fusion(f32[18,48,384]{2,1,0:T(8,128)S(1)} %convert_select_fusion, f32[384]{0:T(512)} %get-tuple-element.102, f32[384]{0:T(512)} %get-tuple-element.103, f32[384]{0:T(512)S(1)} %get-tuple-element.56, f32[384]{0:T(512)S(1)} %copy-done.10, f32[384]{0:T(512)S(1)} %copy-done.12, f32[384]{0:T(512)S(1)} %copy-done.14, ...), kind=kLoop, calls=%fused_computation.216 | loop fusion | flops 21454848 | bytes 8498176 | tf_op jit(solution)/shard_map/add | solution.py:40
  307.0 15.3 %collective-permute-done.17 = bf16[192,1536]{1,0:T(8,128)(2,1)S(1)} collective-permute-done((bf16[192,1536]{1,0:T(8,128)(2,1)S(1)}, bf16[192,1536]{1,0:T(8,128)(2,1)S(1)}, u32[]{:S(2)}, u32[]{:S(2)}) %collective-permute-start.17) | collective-permute-done | bytes 589856 | tf_op jit(solution)/shard_map/ppermute | solution.py:96
  323.5 8.8 %collective-permute-done.10 = bf16[192,1536]{1,0:T(8,128)(2,1)S(1)} collective-permute-done((bf16[192,1536]{1,0:T(8,128)(2,1)S(1)}, bf16[192,1536]{1,0:T(8,128)(2,1)S(1)}, u32[]{:S(2)}, u32[]{:S(2)}) %collective-permute-start.10) | collective-permute-done | bytes 589856 | tf_op jit(solution)/shard_map/ppermute | solution.py:96
  333.5 10.6 %all-reduce.6.cloned.1.call-done = f32[49,384]{1,0:T(8,128)} async-done(((f32[49,384]{1,0:T(8,128)}), f32[49,384]{1,0:T(8,128)}) %all-reduce.6.cloned.1.call-update) | async-done | bytes 75280 | tf_op jit(solution)/shard_map/psum | solution.py:182
  (328 shorter events, 36.5 us)
Async XLA Ops:
  7.2 46.5 %copy-start = (bf16[1152,384]{1,0:T(8,128)(2,1)S(1)}, bf16[1152,384]{1,0:T(8,128)(2,1)}, u32[]{:S(2)}) copy-start(bf16[1152,384]{1,0:T(8,128)(2,1)} %param.10) | copy-start | bytes 2654212
  7.2 83.4 %all-gather.7.cloned.1.call-start = ((), (), s32[]{:S(2)}) async-start(), calls=%async_computation.4 | async-start | bytes 2211840 | tf_op jit(solution)/shard_map/all_gather | solution.py:141
  8.3 14.0 %collective-permute-start = (bf16[3,48,384]{2,1,0:T(8,128)(2,1)S(1)}, bf16[3,48,384]{2,1,0:T(8,128)(2,1)S(1)}, u32[]{:S(2)}, u32[]{:S(2)}) collective-permute-start(bf16[3,48,384]{2,1,0:T(8,128)(2,1)S(1)} %bitcast.145), channel_id=1, source_target_pairs={{0,4},{4,8},{8,12},{12,16},{16,20},{20,24},{24,28},{28,0},{1,5},{5... | collective-permute-start | bytes 331784 | tf_op jit(solution)/shard_map/ppermute | solution.py:23
  11.3 10.9 %collective-permute-start.1 = (bf16[3,48,384]{2,1,0:T(8,128)(2,1)S(1)}, bf16[3,48,384]{2,1,0:T(8,128)(2,1)S(1)}, u32[]{:S(2)}, u32[]{:S(2)}) collective-permute-start(bf16[3,48,384]{2,1,0:T(8,128)(2,1)S(1)} %bitcast.144), channel_id=1, source_target_pairs={{4,0},{8,4},{12,8},{16,12},{20,16},{24,20},{28,24},{0,28},{5,1},{9... | collective-permute-start | bytes 331784 | tf_op jit(solution)/shard_map/ppermute | solution.py:24
  15.7 15.1 %copy-start.9 = (f32[384]{0:T(512)}, f32[384]{0:T(512)S(1)}, u32[]{:S(2)}) copy-start(f32[384]{0:T(512)S(1)} %get-tuple-element.57) | copy-start | bytes 4612
  15.7 15.1 %copy-start.11 = (f32[384]{0:T(512)}, f32[384]{0:T(512)S(1)}, u32[]{:S(2)}) copy-start(f32[384]{0:T(512)S(1)} %get-tuple-element.58) | copy-start | bytes 4612
  15.7 15.1 %copy-start.13 = (f32[384]{0:T(512)}, f32[384]{0:T(512)S(1)}, u32[]{:S(2)}) copy-start(f32[384]{0:T(512)S(1)} %get-tuple-element.59) | copy-start | bytes 4612
  15.7 15.1 %copy-start.15 = (f32[384]{0:T(512)}, f32[384]{0:T(512)S(1)}, u32[]{:S(2)}) copy-start(f32[384]{0:T(512)S(1)} %get-tuple-element.60) | copy-start | bytes 4612
  15.7 15.1 %copy-start.17 = (f32[384]{0:T(512)}, f32[384]{0:T(512)S(1)}, u32[]{:S(2)}) copy-start(f32[384]{0:T(512)S(1)} %get-tuple-element.61) | copy-start | bytes 4612
  15.7 15.1 %copy-start.19 = (f32[384]{0:T(512)}, f32[384]{0:T(512)S(1)}, u32[]{:S(2)}) copy-start(f32[384]{0:T(512)S(1)} %get-tuple-element.62) | copy-start | bytes 4612
  15.7 15.1 %copy-start.21 = (f32[384]{0:T(512)}, f32[384]{0:T(512)S(1)}, u32[]{:S(2)}) copy-start(f32[384]{0:T(512)S(1)} %get-tuple-element.63) | copy-start | bytes 4612
  15.7 15.1 %copy-start.23 = (f32[384]{0:T(512)}, f32[384]{0:T(512)S(1)}, u32[]{:S(2)}) copy-start(f32[384]{0:T(512)S(1)} %get-tuple-element.64) | copy-start | bytes 4612
  15.8 15.1 %copy-start.25 = (f32[384]{0:T(512)}, f32[384]{0:T(512)S(1)}, u32[]{:S(2)}) copy-start(f32[384]{0:T(512)S(1)} %get-tuple-element.65) | copy-start | bytes 4612
  15.8 15.1 %copy-start.27 = (f32[384]{0:T(512)}, f32[384]{0:T(512)S(1)}, u32[]{:S(2)}) copy-start(f32[384]{0:T(512)S(1)} %get-tuple-element.66) | copy-start | bytes 4612
  15.8 15.1 %copy-start.29 = (f32[384]{0:T(512)}, f32[384]{0:T(512)S(1)}, u32[]{:S(2)}) copy-start(f32[384]{0:T(512)S(1)} %get-tuple-element.67) | copy-start | bytes 4612
  15.8 15.1 %copy-start.31 = (f32[384]{0:T(512)}, f32[384]{0:T(512)S(1)}, u32[]{:S(2)}) copy-start(f32[384]{0:T(512)S(1)} %get-tuple-element.68) | copy-start | bytes 4612
  15.8 15.1 %copy-start.33 = (f32[384]{0:T(512)}, f32[384]{0:T(512)S(1)}, u32[]{:S(2)}) copy-start(f32[384]{0:T(512)S(1)} %get-tuple-element.69) | copy-start | bytes 4612
  15.8 15.1 %copy-start.35 = (f32[384]{0:T(512)}, f32[384]{0:T(512)S(1)}, u32[]{:S(2)}) copy-start(f32[384]{0:T(512)S(1)} %get-tuple-element.70) | copy-start | bytes 4612
  15.8 15.1 %copy-start.37 = (f32[384]{0:T(512)}, f32[384]{0:T(512)S(1)}, u32[]{:S(2)}) copy-start(f32[384]{0:T(512)S(1)} %get-tuple-element.71) | copy-start | bytes 4612
  15.8 15.1 %copy-start.39 = (f32[384]{0:T(512)}, f32[384]{0:T(512)S(1)}, u32[]{:S(2)}) copy-start(f32[384]{0:T(512)S(1)} %get-tuple-element.72) | copy-start | bytes 4612
  15.8 15.1 %copy-start.41 = (f32[384]{0:T(512)}, f32[384]{0:T(512)S(1)}, u32[]{:S(2)}) copy-start(f32[384]{0:T(512)S(1)} %get-tuple-element.73) | copy-start | bytes 4612
  17.2 13.8 %copy-start.43 = (f32[384]{0:T(512)}, f32[384]{0:T(512)S(1)}, u32[]{:S(2)}) copy-start(f32[384]{0:T(512)S(1)} %get-tuple-element.74) | copy-start | bytes 4612
  60.6 25.2 %all-to-all-start.1 = ((bf16[8,144,384]{2,1,0:T(8,128)(2,1)}), bf16[8,144,384]{2,1,0:T(8,128)(2,1)S(1)}, u32[]{:S(2)}, u32[]{:S(2)}) async-start(bf16[8,144,384]{2,1,0:T(8,128)(2,1)} %broadcast_select_fusion), calls=%async_computation.1 | async-start | bytes 1769472 | tf_op jit(solution)/shard_map/all_to_all | solution.py:121
  64.1 45.9 %all-gather.5.cloned.1.call-start = ((), (), s32[]{:S(2)}) async-start(), calls=%async_computation.3 | async-start | bytes 2211840 | tf_op jit(solution)/shard_map/all_gather | solution.py:142
  90.3 170.3 %reduce-scatter.4.cloned.1.call-start = ((), (), s32[]{:S(2)}) async-start(), calls=%async_computation.6 | async-start | bytes 2457600
  94.5 15.5 %copy-start.82 = (f32[1536]{0:T(1024)S(1)}, f32[1536]{0:T(1024)}, u32[]{:S(2)}) copy-start(f32[1536]{0:T(1024)} %param.19) | copy-start | bytes 18436
  124.3 54.4 %collective-permute-start.11 = (bf16[768,1536]{1,0:T(8,128)(2,1)}, bf16[768,1536]{1,0:T(8,128)(2,1)}, u32[]{:S(2)}, u32[]{:S(2)}) collective-permute-start(bf16[768,1536]{1,0:T(8,128)(2,1)} %multiply_convert_fusion), channel_id=1, source_target_pairs={{0,4},{4,0},{8,12},{12,8},{16,20},{20,16},{24,28},{28,24},{1,5},{5... | collective-permute-start | bytes 7077896 | tf_op jit(solution)/shard_map/ppermute | solution.py:74
  133.3 95.2 %collective-permute-start.4 = (bf16[768,1536]{1,0:T(8,128)(2,1)}, bf16[768,1536]{1,0:T(8,128)(2,1)}, u32[]{:S(2)}, u32[]{:S(2)}) collective-permute-start(bf16[768,1536]{1,0:T(8,128)(2,1)} %multiply_convert_fusion.1), channel_id=1, source_target_pairs={{0,4},{4,0},{8,12},{12,8},{16,20},{20,16},{24,28},{28,24},{1,5},{5... | collective-permute-start | bytes 7077896 | tf_op jit(solution)/shard_map/ppermute | solution.py:74
  142.0 202.2 %all-reduce.6.cloned.1.call-start = ((), (), s32[]{:S(2)}) async-start(), calls=%async_computation.5 | async-start | bytes 172032 | tf_op jit(solution)/shard_map/psum | solution.py:182
  178.7 49.9 %copy-start.87 = (bf16[576,1536]{1,0:T(8,128)(2,1)S(1)}, bf16[576,1536]{1,0:T(8,128)(2,1)}, u32[]{:S(2)}) copy-start(bf16[576,1536]{1,0:T(8,128)(2,1)} %copy-done.86) | copy-start | bytes 5308420
  183.3 48.9 %copy-start.2 = (f32[768,1536]{1,0:T(8,128)}, f32[768,1536]{1,0:T(8,128)S(1)}, u32[]{:S(2)}) copy-start(f32[768,1536]{1,0:T(8,128)S(1)} %convert_add_fusion) | copy-start | bytes 14155780
  183.3 45.2 %copy-start.7 = (bf16[576,4,1,192]{0,3,2,1:T(8,128)(2,1)S(1)}, bf16[576,4,1,192]{0,3,2,1:T(8,128)(2,1)}, u32[]{:S(2)}) copy-start(bf16[576,4,1,192]{0,3,2,1:T(8,128)(2,1)} %get-tuple-element.138) | copy-start | bytes 2654212
  184.5 58.2 %collective-permute-start.12 = (bf16[192,1536]{1,0:T(8,128)(2,1)}, bf16[192,1536]{1,0:T(8,128)(2,1)S(1)}, u32[]{:S(2)}, u32[]{:S(2)}) collective-permute-start(bf16[192,1536]{1,0:T(8,128)(2,1)} %get-tuple-element.114), channel_id=1, source_target_pairs={{0,8},{4,12},{1,9},{5,13},{2,10},{6,14},{3,11},{7,15}} | collective-permute-start | bytes 1769480 | tf_op jit(solution)/shard_map/ppermute | solution.py:95
  235.5 17.5 %collective-permute-start.5 = (bf16[192,1536]{1,0:T(8,128)(2,1)}, bf16[192,1536]{1,0:T(8,128)(2,1)}, u32[]{:S(2)}, u32[]{:S(2)}) collective-permute-start(bf16[192,1536]{1,0:T(8,128)(2,1)} %get-tuple-element.118), channel_id=1, source_target_pairs={{0,8},{4,12},{1,9},{5,13},{2,10},{6,14},{3,11},{7,15}} | collective-permute-start | bytes 1769480 | tf_op jit(solution)/shard_map/ppermute | solution.py:95
  239.7 38.7 %collective-permute-start.15 = (bf16[192,1536]{1,0:T(8,128)(2,1)}, bf16[192,1536]{1,0:T(8,128)(2,1)}, u32[]{:S(2)}, u32[]{:S(2)}) collective-permute-start(bf16[192,1536]{1,0:T(8,128)(2,1)} %get-tuple-element.115), channel_id=1, source_target_pairs={{28,20},{24,16},{29,21},{25,17},{30,22},{26,18},{31,23},{27,19}} | collective-permute-start | bytes 1769480 | tf_op jit(solution)/shard_map/ppermute | solution.py:96
  241.2 43.5 %collective-permute-start.8 = (bf16[192,1536]{1,0:T(8,128)(2,1)}, bf16[192,1536]{1,0:T(8,128)(2,1)}, u32[]{:S(2)}, u32[]{:S(2)}) collective-permute-start(bf16[192,1536]{1,0:T(8,128)(2,1)} %get-tuple-element.119), channel_id=1, source_target_pairs={{28,20},{24,16},{29,21},{25,17},{30,22},{26,18},{31,23},{27,19}} | collective-permute-start | bytes 1769480 | tf_op jit(solution)/shard_map/ppermute | solution.py:96
  244.9 36.8 %collective-permute-start.13 = (bf16[192,1536]{1,0:T(8,128)(2,1)}, bf16[192,1536]{1,0:T(8,128)(2,1)}, u32[]{:S(2)}, u32[]{:S(2)}) collective-permute-start(bf16[192,1536]{1,0:T(8,128)(2,1)} %fusion.8), channel_id=1, source_target_pairs={{0,8},{4,12},{8,16},{12,20},{1,9},{5,13},{9,17},{13,21},{2,10},{6,... | collective-permute-start | bytes 1769480 | tf_op jit(solution)/shard_map/ppermute | solution.py:95
  255.4 30.7 %collective-permute-start.6 = (bf16[192,1536]{1,0:T(8,128)(2,1)}, bf16[192,1536]{1,0:T(8,128)(2,1)}, u32[]{:S(2)}, u32[]{:S(2)}) collective-permute-start(bf16[192,1536]{1,0:T(8,128)(2,1)} %fusion.14), channel_id=1, source_target_pairs={{0,8},{4,12},{8,16},{12,20},{1,9},{5,13},{9,17},{13,21},{2,10},{6,... | collective-permute-start | bytes 1769480 | tf_op jit(solution)/shard_map/ppermute | solution.py:95
  276.9 12.7 %collective-permute-start.2 = (bf16[3,48,384]{2,1,0:T(8,128)(2,1)S(1)}, bf16[3,48,384]{2,1,0:T(8,128)(2,1)S(1)}, u32[]{:S(2)}, u32[]{:S(2)}) collective-permute-start(bf16[3,48,384]{2,1,0:T(8,128)(2,1)S(1)} %get-tuple-element.124), channel_id=1, source_target_pairs={{0,4},{4,8},{8,12},{12,16},{16,20},{20,24},{24,28},{28,0},{1,5},{5... | collective-permute-start | bytes 331784 | tf_op jit(solution)/shard_map/ppermute | solution.py:23
  278.5 15.8 %collective-permute-start.3 = (bf16[3,48,384]{2,1,0:T(8,128)(2,1)S(1)}, bf16[3,48,384]{2,1,0:T(8,128)(2,1)S(1)}, u32[]{:S(2)}, u32[]{:S(2)}) collective-permute-start(bf16[3,48,384]{2,1,0:T(8,128)(2,1)S(1)} %get-tuple-element.125), channel_id=1, source_target_pairs={{4,0},{8,4},{12,8},{16,12},{20,16},{24,20},{28,24},{0,28},{5,1},{9... | collective-permute-start | bytes 331784 | tf_op jit(solution)/shard_map/ppermute | solution.py:24
  284.0 19.1 %collective-permute-start.16 = (bf16[192,1536]{1,0:T(8,128)(2,1)S(1)}, bf16[192,1536]{1,0:T(8,128)(2,1)S(1)}, u32[]{:S(2)}, u32[]{:S(2)}) collective-permute-start(bf16[192,1536]{1,0:T(8,128)(2,1)S(1)} %get-tuple-element.113), channel_id=1, source_target_pairs={{28,20},{24,16},{20,12},{16,8},{29,21},{25,17},{21,13},{17,9},{30,... | collective-permute-start | bytes 1769480 | tf_op jit(solution)/shard_map/ppermute | solution.py:96
  284.7 22.3 %collective-permute-start.14 = (bf16[192,1536]{1,0:T(8,128)(2,1)S(1)}, bf16[192,1536]{1,0:T(8,128)(2,1)S(1)}, u32[]{:S(2)}, u32[]{:S(2)}) collective-permute-start(bf16[192,1536]{1,0:T(8,128)(2,1)S(1)} %get-tuple-element.112), channel_id=1, source_target_pairs={{0,8},{4,12},{8,16},{12,20},{16,24},{20,28},{1,9},{5,13},{9,17},{1... | collective-permute-start | bytes 1769480 | tf_op jit(solution)/shard_map/ppermute | solution.py:95
  286.1 18.5 %slice-start.2 = ((s8[4718592]{0:T(1024)(128)(4,1)}), s8[4194304]{0:T(1024)(128)(4,1)S(1)}, s32[]{:S(2)}) async-start(s8[4718592]{0:T(1024)(128)(4,1)} %bitcast.130), calls=%async_computation.9 | async-start | bytes 8388608
  288.9 15.7 %collective-permute-start.9 = (bf16[192,1536]{1,0:T(8,128)(2,1)S(1)}, bf16[192,1536]{1,0:T(8,128)(2,1)S(1)}, u32[]{:S(2)}, u32[]{:S(2)}) collective-permute-start(bf16[192,1536]{1,0:T(8,128)(2,1)S(1)} %get-tuple-element.117), channel_id=1, source_target_pairs={{28,20},{24,16},{20,12},{16,8},{29,21},{25,17},{21,13},{17,9},{30,... | collective-permute-start | bytes 1769480 | tf_op jit(solution)/shard_map/ppermute | solution.py:96
  289.6 33.9 %collective-permute-start.7 = (bf16[192,1536]{1,0:T(8,128)(2,1)S(1)}, bf16[192,1536]{1,0:T(8,128)(2,1)S(1)}, u32[]{:S(2)}, u32[]{:S(2)}) collective-permute-start(bf16[192,1536]{1,0:T(8,128)(2,1)S(1)} %get-tuple-element.116), channel_id=1, source_target_pairs={{0,8},{4,12},{8,16},{12,20},{16,24},{20,28},{1,9},{5,13},{9,17},{1... | collective-permute-start | bytes 1769480 | tf_op jit(solution)/shard_map/ppermute | solution.py:95
  303.3 19.0 %collective-permute-start.17 = (bf16[192,1536]{1,0:T(8,128)(2,1)S(1)}, bf16[192,1536]{1,0:T(8,128)(2,1)S(1)}, u32[]{:S(2)}, u32[]{:S(2)}) collective-permute-start(bf16[192,1536]{1,0:T(8,128)(2,1)S(1)} %fusion.7), channel_id=1, source_target_pairs={{28,20},{24,16},{20,12},{16,8},{12,4},{8,0},{29,21},{25,17},{21,13... | collective-permute-start | bytes 1769480 | tf_op jit(solution)/shard_map/ppermute | solution.py:96
  304.8 27.6 %collective-permute-start.10 = (bf16[192,1536]{1,0:T(8,128)(2,1)S(1)}, bf16[192,1536]{1,0:T(8,128)(2,1)S(1)}, u32[]{:S(2)}, u32[]{:S(2)}) collective-permute-start(bf16[192,1536]{1,0:T(8,128)(2,1)S(1)} %fusion.13), channel_id=1, source_target_pairs={{28,20},{24,16},{20,12},{16,8},{12,4},{8,0},{29,21},{25,17},{21,13... | collective-permute-start | bytes 1769480 | tf_op jit(solution)/shard_map/ppermute | solution.py:96
  322.3 23.3 %copy-start.1 = (bf16[1152,384]{1,0:T(8,128)(2,1)S(1)}, bf16[1152,384]{1,0:T(8,128)(2,1)}, u32[]{:S(2)}) copy-start(bf16[1152,384]{1,0:T(8,128)(2,1)} %param.10) | copy-start | bytes 2654212
  (72 other events, 626.4 us)
Sparse Core Ops, SparseCore 0:
  39.3 19.3 all-gather.6
  90.4 19.5 all-gather.4
  142.1 30.6 reduce-scatter.3
  277.0 67.0 all-reduce.5

commit v2 on v1

v2 whole, which is shorter than its diff:
```python
import math

import jax
import jax.numpy as jnp
from jax import lax
from jax.sharding import PartitionSpec as P

C = 1536
KSIZE = 7
PAGE_SIDE = 48


EPS = 1e-06


def extended_2(value, sides, width):
    for axis, dim in sides:
        peers, length = (lax.axis_size(axis), value.shape[dim])
        up = [(i, (i + 1) % peers) for i in range(peers)]
        down = [(j, i) for i, j in up]
        last = lax.slice_in_dim(value, length - width, length, axis=dim)
        first = lax.slice_in_dim(value, 0, width, axis=dim)
        before = lax.ppermute(last, axis, up)
        after = lax.ppermute(first, axis, down)
        value = jnp.concatenate([before, value, after], axis=dim)
    return value


def gelu_parts(preact):
    normal_cdf = 0.5 * (1.0 + jax.scipy.special.erf(preact * 0.7071067811865476))
    density = jnp.exp(-0.5 * preact * preact) * 0.3989422804014327
    return (preact * normal_cdf, normal_cdf + preact * density)


def depthwise(padded, kernel, rows, cols):
    total = jnp.zeros((rows, cols, padded.shape[2]), jnp.float32)
    for row_off in range(KSIZE):
        for col_off in range(KSIZE):
            window = padded[row_off : row_off + rows, col_off : col_off + cols, :]
            total = total + kernel[row_off * KSIZE + col_off] * window
    return total


def page_edges(extended, band_index, tiles_page, reach):
    height = extended.shape[0]
    row_ids = lax.broadcasted_iota(jnp.int32, (height, 1, 1), 0)
    first = band_index % tiles_page == 0
    final = band_index % tiles_page == tiles_page - 1
    dropped = (row_ids < reach) & first | (row_ids >= height - reach) & final
    kept = jnp.where(dropped, jnp.zeros_like(extended), extended)
    return jnp.pad(kept, ((0, 0), (reach, reach), (0, 0)))


def after(value, *others):
    return lax.optimization_barrier((value, *others))[0]


def product(columns, values, factor):
    return (
        lax.dot_general(
            columns, values, (((0,), (0,)), ((), ())), preferred_element_type=jnp.float32
        )
        * factor
    )


def pair_swap(value):
    swap = [(i, i ^ 1) for i in range(lax.axis_size("tile"))]
    return lax.ppermute(value.astype(jnp.bfloat16), "tile", swap)


def pair_columns(columns):
    tiles = lax.axis_size("tile")
    tokens, width = columns.shape
    side = lax.axis_index("tile") % 2
    blocks = columns.reshape(tokens, tiles // 2, 2, width // tiles)
    return [
        lax.dynamic_index_in_dim(blocks, which, 2, keepdims=False).reshape(tokens, width // 2)
        for which in (side, 1 - side)
    ]


class LineSum:
    def __init__(self, parts):
        self.lines = lax.axis_size("tile") // 2
        self.parts = parts.reshape(self.lines, -1, parts.shape[-1])
        self.place = lax.axis_index("tile") // 2
        self.step = 0
        self.ups = self.downs = None

    def pick(self, index):
        return lax.dynamic_index_in_dim(self.parts, index, 0, keepdims=False)

    def advance(self, *others):
        lines, tiles, step = self.lines, 2 * self.lines, self.step
        up_pairs = [(i, i + 2) for i in range(2 * (step + 1))]
        down_pairs = [(tiles - 1 - i, tiles - 1 - j) for i, j in up_pairs]
        up = self.pick(jnp.clip(lines - 1 - step + self.place, 0, lines - 1))
        down = self.pick(jnp.clip(step - (lines - 1 - self.place), 0, lines - 1))
        if step:
            ups, downs = self.arrived(*others)
            up, down = up + ups, down + downs
        up, down = lax.optimization_barrier((up.astype(jnp.bfloat16), down.astype(jnp.bfloat16)))
        self.ups = lax.ppermute(up, "tile", up_pairs)
        self.downs = lax.ppermute(down, "tile", down_pairs)
        self.step += 1
        return up

    def arrived(self, *others):
        ups, downs = self.ups, self.downs
        if others:
            ups, downs = lax.optimization_barrier((ups, downs, *others))[:2]
        return ups.astype(jnp.float32), downs.astype(jnp.float32)

    def finish(self, *others):
        while self.step < self.lines - 1:
            self.advance(*others)
        ups, downs = self.arrived(*others)
        return self.pick(self.place) + ups + downs


def shards(
    seq_grad, token_slot, pixels, dw_kernel, ln_gain, ln_bias, w_in, b_in, w_out, layer_scale
):
    tiles = lax.axis_size("tile")
    position = lax.axis_index("tile")
    band_index = (position + 1) % tiles
    slots = seq_grad.shape[0]
    capacity = slots // tiles
    tok_dev, chan_dev = pixels.shape
    reach = KSIZE // 2
    source = token_slot // slots
    local_slot = token_slot % slots
    onehot = (source[:, None] == jnp.arange(tiles, dtype=jnp.int32)[None, :]).astype(jnp.int32)
    ranks = jnp.sum((jnp.cumsum(onehot, axis=0) - onehot) * onehot, axis=1)
    seat = source * capacity + ranks
    seats = jnp.arange(tiles * capacity, dtype=jnp.int32)
    placed = seat[:, None] == seats[None, :]
    request = jnp.sum(jnp.where(placed, local_slot[:, None], 0), axis=0).reshape(tiles, capacity)
    asked = lax.all_to_all(request, "tile", split_axis=0, concat_axis=0, tiled=True)
    wanted = asked.reshape(-1, 1) == jnp.arange(slots, dtype=jnp.int32)[None, :]
    found = jnp.dot(
        wanted.astype(jnp.bfloat16), seq_grad, preferred_element_type=jnp.float32
    ).astype(jnp.bfloat16)
    arrived = lax.all_to_all(
        found.reshape(tiles, capacity, chan_dev), "tile", split_axis=0, concat_axis=0, tiled=True
    )
    rows = tok_dev // PAGE_SIDE
    tiles_page = PAGE_SIDE // rows
    grid = pixels.reshape(rows, PAGE_SIDE, chan_dev)
    extended = extended_2(grid, (("tile", 0),), reach)
    extended = after(extended, found)
    padded = page_edges(extended.astype(jnp.float32), band_index, tiles_page, reach)
    mixed = depthwise(padded, dw_kernel, rows, PAGE_SIDE).reshape(tok_dev, chan_dev)
    own_mean = jnp.mean(mixed, axis=1)
    own_center = mixed - own_mean[:, None]
    own_spread = jnp.sum(own_center * own_center, axis=1)
    stats = lax.all_gather(jnp.stack([own_mean, own_spread]), "chan")
    mean = jnp.mean(stats[:, 0], axis=0)
    shift = stats[:, 0] - mean
    spread = jnp.sum(stats[:, 1] + chan_dev * shift * shift, axis=0)
    center = mixed - mean[:, None]
    inv_std = lax.rsqrt(spread / C + EPS)[:, None]
    normed = center * inv_std
    ln_part = (normed * ln_gain + ln_bias).astype(jnp.bfloat16)
    ln_out = lax.all_gather(ln_part, "chan", axis=1, tiled=True)
    arrived = after(arrived, ln_part)
    upstream = jnp.dot(
        placed.astype(jnp.bfloat16),
        arrived.reshape(tiles * capacity, chan_dev),
        preferred_element_type=jnp.float32,
    ).astype(jnp.bfloat16)
    upstream_all = lax.all_gather(upstream, "chan", axis=1, tiled=True)
    scaled = (upstream_all.astype(jnp.float32) * layer_scale).astype(jnp.bfloat16)
    preact = jnp.dot(ln_out, w_in, preferred_element_type=jnp.float32) + b_in
    act_val, act_slope = gelu_parts(preact)
    hidden = act_val.astype(jnp.bfloat16)
    factor = 1.0 / math.sqrt(tok_dev * tiles)
    scaled_own, scaled_other = pair_columns(scaled)
    out_send, hidden = lax.optimization_barrier(
        (product(scaled_other, hidden, factor).astype(jnp.bfloat16), hidden)
    )
    out_swap = pair_swap(out_send)
    back_hidden = lax.dot_general(
        after(scaled, out_send), w_out, (((1,), (1,)), ((), ())), preferred_element_type=jnp.float32
    )
    back_pre = (back_hidden * act_slope).astype(jnp.bfloat16)
    half = back_pre.shape[1] // 2
    lead = LineSum(product(ln_out, back_pre[:, :half], factor))
    sent = lead.advance()
    back_pre_late = after(back_pre, sent)
    partial_sum = lax.dot_general(
        back_pre_late, w_in, (((1,), (1,)), ((), ())), preferred_element_type=jnp.float32
    )
    partial_sum = partial_sum.astype(jnp.bfloat16)
    back_norm = lax.psum_scatter(partial_sum, "chan", scatter_dimension=1, tiled=True)
    ln_own, ln_other = pair_columns(ln_out)
    in_send = after(product(ln_other, back_pre[:, half:], factor).astype(jnp.bfloat16), partial_sum)
    in_swap = pair_swap(in_send)
    out_part = product(scaled_own, hidden, factor)
    in_part = product(ln_own, back_pre[:, half:], factor)
    sent = lead.advance(in_send)
    while lead.step < lead.lines - 1:
        sent = lead.advance(sent)
    back_norm = after(back_norm, sent).astype(jnp.float32)
    grad_normed = back_norm * ln_gain
    sum_grad, sum_cross = lax.psum(
        (jnp.sum(grad_normed, axis=1), jnp.sum(grad_normed * normed, axis=1)), "chan"
    )
    grad_mixed = inv_std * (
        grad_normed - (sum_grad / C)[:, None] - normed * (sum_cross / C)[:, None]
    )
    grad_grid = grad_mixed.reshape(rows, PAGE_SIDE, chan_dev)
    taps = []
    for row_off in range(KSIZE):
        for col_off in range(KSIZE):
            window = padded[row_off : row_off + rows, col_off : col_off + PAGE_SIDE, :]
            taps.append(jnp.sum(window * grad_grid, axis=(0, 1)))
    taps = jnp.stack(taps) * factor
    grad_kernel = lax.psum(taps, "tile")
    grad_ext = extended_2(grad_grid.astype(jnp.bfloat16), (("tile", 0),), reach)
    out_line = LineSum(out_part + after(out_swap, taps).astype(jnp.float32))
    sent = out_line.advance()
    lead_sum = lead.finish(sent).reshape(2, -1, half)
    side = lax.axis_index("tile") % 2
    lead_other = lax.dynamic_index_in_dim(lead_sum, 1 - side, 0, keepdims=False)
    lead_own = lax.dynamic_index_in_dim(lead_sum, side, 0, keepdims=False)
    lead_swap = pair_swap(lead_other)
    grad_pad = page_edges(
        after(grad_ext, sent).astype(jnp.float32), band_index, tiles_page, reach
    )
    back_conv = depthwise(grad_pad, dw_kernel[::-1], rows, PAGE_SIDE).reshape(tok_dev, chan_dev)
    grad_input = (upstream.astype(jnp.float32) + back_conv).astype(jnp.bfloat16)
    sent = out_line.advance(grad_input)
    in_line = LineSum(in_part + after(in_swap, sent).astype(jnp.float32))
    in_line.advance()
    out_line.advance()
    in_line.advance()
    grad_w_out = out_line.finish().T
    in_late = in_line.finish()
    in_early = lead_own + lead_swap.astype(jnp.float32)
    grad_w_in = jnp.concatenate([in_early, in_late], axis=1)
    return (grad_input, grad_w_in, grad_w_out, grad_kernel)


def solution(mesh):
    placed = (
        P("tile", "chan"),
        P("tile"),
        P("tile", "chan"),
        P(None, "chan"),
        P("chan"),
        P("chan"),
        P(None, "chan"),
        P("chan"),
        P("chan", None),
        P(),
    )
    return jax.shard_map(
        shards,
        mesh=mesh,
        in_specs=placed,
        out_specs=(P("tile", "chan"), P("tile", "chan"), P("chan", "tile"), P(None, "chan")),
        check_vma=False,
    )
```

time: 354 us -> 321 us (0.907)
  waiting for transfers between devices: 146 us -> 81.3 us
  starting transfers between devices: 44.8 us -> 67.2 us
  blocking collectives: 21.1 us -> 38.4 us
  local copies, waits for them, and re-layouts: 41.1 us -> 28.8 us
  matrix products: 32.1 us -> 39.6 us
    ppermute x14 -> x21, waiting for transfers between devices: 107 us -> 36.1 us  [the longest x9 27.9 us: advance(): self.ups = lax.ppermute(up, 'tile', up_pairs)]
    ppermute x14 -> x21, starting transfers between devices: 30 us -> 52.7 us  [the longest x9 40.8 us: advance(): self.ups = lax.ppermute(up, 'tile', up_pairs)]
    all_to_all x1, waiting for transfers between devices: 21 us -> 2.58 us  [shards(): lax.all_to_all(request, 'tile', split_axis=0, concat_axis=0, tiled=True)]
    ppermute x2, waiting for transfers between devices: 0.01 us -> 18.1 us  [extended_2(): after = lax.ppermute(first, axis, down)]
    all_to_all x1, blocking collectives: 9.55 us -> 26.9 us  [shards(): lax.all_to_all(found.reshape(tiles, capacity, chan_dev), 'tile', split_ax...]
    gather x2 -> x0, local copies, waits for them, and re-layouts: 7.49 us -> none  [the longest x1 4.59 us: shards(): jnp.take(seq_grad, lax.all_to_all(request, 'tile', split_axis=0, concat_a...]
    psum x1, waiting for transfers between devices: 10.6 us -> 18 us  [shards(): grad_kernel = lax.psum(taps, 'tile')]
    dot_general x6 -> x9, matrix products: 23.4 us -> 30.7 us  [the longest x5 18.1 us: product(): lax.dot_general(columns, values, (((0,), (0,)), ((), ())), preferred_elem...]
  transfers between devices with their start and end apart: 23 -> 30, of which waited for: 8 -> 11; matrix products, arithmetic and copies ran while one was open for 27% -> 22% of each run, Pallas kernels for 0% -> 0%
where the time goes in v2:
time: 321 us; the launch traced here: 320 us
  waiting for transfers between devices  81.3 us (25%)
  starting transfers between devices  67.2 us (21%)
  other arithmetic  48.5 us (15%)
  matrix products  39.6 us (12%)
  blocking collectives  38.4 us (12%)
  local copies, waits for them, and re-layouts  28.8 us (9%)
  between operations  15.9 us (5%)
    ppermute x9, starting transfers between devices, advance(): self.ups = lax.ppermute(up, 'tile', up_pairs)  40.8 us
    ppermute x9, waiting for transfers between devices, advance(): self.ups = lax.ppermute(up, 'tile', up_pairs)  27.9 us
    all_to_all x1, blocking collectives, shards(): lax.all_to_all(found.reshape(tiles, capacity, chan_dev), 'tile', split_ax...  26.9 us
    dot_general x5, matrix products, product(): lax.dot_general(columns, values, (((0,), (0,)), ((), ())), preferred_elem...  18.1 us
    ppermute x2, waiting for transfers between devices, extended_2(): after = lax.ppermute(first, axis, down)  18.1 us
    psum x1, waiting for transfers between devices, shards(): grad_kernel = lax.psum(taps, 'tile')  18 us
    ppermute x9, starting transfers between devices, advance(): self.downs = lax.ppermute(down, 'tile', down_pairs)  9.97 us
    dot_general x1, matrix products, shards(): preact = jnp.dot(ln_out, w_in, preferred_element_type=jnp.float32) + b_in  8.87 us
  transfers between devices with their start and end apart: 30, of which 11 were waited for; matrix products, arithmetic and copies ran while one was open for 22% of the time, Pallas kernels for 0%

profile of v2, /device:TPU:0, one launch (start us, length us, event | category | flops | bytes accessed | tf_op | source)
XLA Modules:
  0.0 319.6 jit_solution(14177762822810298282)
XLA Ops:
  8.2 6.1 %collective-permute-start.1 = (bf16[3,48,384]{2,1,0:T(8,128)(2,1)S(1)}, bf16[3,48,384]{2,1,0:T(8,128)(2,1)S(1)}, u32[]{:S(2)}, u32[]{:S(2)}) collective-permute-start(bf16[3,48,384]{2,1,0:T(8,128)(2,1)S(1)} %bitcast.168), channel_id=1, source_target_pairs={{4,0},{8,4},{12,8},{16,12},{20,16},{24,20},{28,24},{0,28},{5,1},{9... | collective-permute-start | bytes 331784 | tf_op jit(solution)/shard_map/ppermute | solution.py:24
  18.8 6.0 %all-to-all-start = ((s32[8,1,144]{2,1,0:T(1,128)}), s32[8,1,144]{2,1,0:T(1,128)S(1)}, u32[]{:S(2)}, u32[]{:S(2)}) async-start(s32[8,1,144]{2,1,0:T(1,128)} %all_to_all.9), calls=%async_computation | async-start | bytes 16384 | tf_op jit(solution)/shard_map/all_to_all | solution.py:140
  28.7 2.6 all-to-all-done
  31.4 2.6 fusion.7
  34.6 6.6 %fusion.138 = (f32[12,48]{1,0:T(8,128)S(1)}, f32[12,48,384]{2,1,0:T(8,128)S(1)}) fusion(f32[384]{0:T(512)S(1)} %get-tuple-element.176, f32[384]{0:T(512)S(1)} %get-tuple-element.177, f32[384]{0:T(512)S(1)} %get-tuple-element.130, f32[18,48,384]{2,1,0:T(8,128)S(1)} %convert_select_fusion.1, f32[384]{0:T(512)S(1)} %get-tuple-element.131, ...), kind=kLoop, calls=%fused_computation.402 | loop fusion | flops 21675456 | bytes 8507648 | tf_op jit(solution)/shard_map/reduce_sum | solution.py:155
  41.6 5.2 %all-gather.1 = f32[4,2,576]{2,1,0:T(2,128)S(1)} all-gather(f32[1,2,576]{2,1,0:T(2,128)S(1)} %maximum_bitcast_fusion), channel_id=2, replica_groups=mesh['tile'=8,'chan'=4] {'chan'}, dimensions={0}, use_global_device_ids=true | all-gather | bytes 23040 | tf_op jit(solution)/shard_map/all_gather | solution.py:158
  48.0 26.9 %all_to_all.14 = bf16[8,144,384]{2,1,0:T(8,128)(2,1)S(1)} all-to-all(bf16[8,144,384]{2,1,0:T(8,128)(2,1)} %bitcast.164), channel_id=1, replica_groups=mesh['tile'=8,'chan'=4] {'tile'}, dimensions={0} | all-to-all | bytes 1769472 | tf_op jit(solution)/shard_map/all_to_all | solution.py:145
  74.9 1.7 fusion.11
  77.0 3.9 %copy.87 = bf16[576,1536]{0,1:T(8,128)(2,1)} copy(bf16[576,1536]{1,0:T(8,128)(2,1)} %all-gather.7.cloned.1.call-done) | data formatting | bytes 3538944 | tf_op jit(solution)/shard_map/all_gather | solution.py:166
  80.9 8.9 %multiply_convert_fusion.1 = (bf16[576,1536]{1,0:T(8,128)(2,1)}, f32[576,1536]{1,0:T(8,128)}) fusion(f32[1536]{0:T(1024)S(1)} %copy-done.76, bf16[576,1536]{1,0:T(8,128)(2,1)} %all-gather.7.cloned.1.call-done, bf16[1536,1536]{1,0:T(8,128)(2,1)} %param.16), kind=kOutput, calls=%fused_computation.12 | convolution fusion | flops 2723217408 | bytes 11802624 | tf_op jit(solution)/shard_map/dot_general | solution.py:175
  89.8 6.3 %all-gather.5.cloned.1.call-done = bf16[576,1536]{1,0:T(8,128)(2,1)} async-done(((bf16[576,384]{1,0:T(8,128)(2,1)}), bf16[576,1536]{1,0:T(8,128)(2,1)}) %all-gather.5.cloned.1.call-update) | async-done | bytes 1769488 | tf_op jit(solution)/shard_map/all_gather | solution.py:173
  96.1 3.0 multiply_convert_fusion.2
  99.1 3.9 %copy.86 = bf16[576,1536]{0,1:T(8,128)(2,1)} copy(bf16[576,1536]{1,0:T(8,128)(2,1)} %multiply_convert_fusion.2) | data formatting | bytes 3538944 | tf_op jit(solution)/shard_map/convert_element_type | solution.py:174
  103.0 3.9 %constant_dynamic-slice_fusion = (bf16[576,4,1,192]{0,3,2,1:T(8,128)(2,1)}, bf16[576,4,1,192]{0,3,2,1:T(8,128)(2,1)}, bf16[576,4,1,192]{0,3,2,1:T(8,128)(2,1)S(1)}, bf16[576,4,1,192]{0,3,2,1:T(8,128)(2,1)S(1)}) fusion(bf16[576,4,2,192]{0,3,2,1:T(8,128)(2,1)} %bitcast.155, s32[]{:T(128)S(6)} %select_n.100, s32[]{:T(128)S(6)} %select_n.98, ...), kind=kLoop, calls=%fused_computation.335 | loop fusion | bytes 7077896 | tf_op jit(solution)/shard_map/jit(dynamic_index_in_dim)/dynamic_slice | solution.py:78
  106.9 3.5 %multiply_convert_fusion = bf16[768,1536]{1,0:T(8,128)(2,1)} fusion(bf16[576,768]{0,1:T(8,128)(2,1)S(1)} %bitcast.163, bf16[576,1536]{1,0:T(8,128)(2,1)S(1)} %copy-done.79), kind=kOutput, calls=%fused_computation.4 | convolution fusion | flops 1361313792 | bytes 5013504 | tf_op jit(solution)/shard_map/dot_general | solution.py:60
  110.4 4.1 %fusion.6 = bf16[576,1536]{1,0:T(8,128)(2,1)S(1)} fusion(f32[576,1536]{1,0:T(8,128)S(1)} %copy-done.81, bf16[576,1536]{1,0:T(8,128)(2,1)S(1)} %copy-done.3, bf16[1536,1536]{1,0:T(8,128)(2,1)S(1)} %bitcast.172), kind=kOutput, calls=%fused_computation.11 | convolution fusion | flops 2726756352 | bytes 11796480 | tf_op jit(solution)/shard_map/dot_general | solution.py:184
  114.6 4.2 %convolution_multiply_fusion = f32[1536,768]{1,0:T(8,128)} fusion(bf16[576,1536]{1,0:T(8,128)(2,1)S(1)} %copy-done.5, bf16[576,1536]{1,0:T(8,128)(2,1)S(1)} %fusion.6), kind=kOutput, calls=%fused_computation.5 | convolution fusion | flops 1360134144 | bytes 7372800 | tf_op jit(solution)/shard_map/dot_general | solution.py:60
  118.7 2.8 fusion.121
  121.5 4.2 %convolution_convert_fusion = bf16[576,1536]{1,0:T(8,128)(2,1)} fusion(bf16[576,1536]{1,0:T(8,128)(2,1)S(1)} %fusion.6, bf16[1536,1536]{1,0:T(8,128)(2,1)S(1)} %bitcast.174), kind=kOutput, calls=%fused_computation.16 | convolution fusion | flops 2718793728 | bytes 8257536 | tf_op jit(solution)/shard_map/dot_general | solution.py:192
  125.7 3.9 %copy.88 = bf16[576,1536]{0,1:T(8,128)(2,1)} copy(bf16[576,1536]{1,0:T(8,128)(2,1)} %convolution_convert_fusion) | data formatting | bytes 3538944
  129.7 4.2 %collective-permute-start.2 = (bf16[384,768]{1,0:T(8,128)(2,1)}, bf16[384,768]{1,0:T(8,128)(2,1)}, u32[]{:S(2)}, u32[]{:S(2)}) collective-permute-start(bf16[384,768]{1,0:T(8,128)(2,1)} %get-tuple-element.45), channel_id=1, source_target_pairs={{0,8},{4,12},{1,9},{5,13},{2,10},{6,14},{3,11},{7,15}} | collective-permute-start | bytes 1769480 | tf_op jit(solution)/shard_map/ppermute | solution.py:104
  136.8 3.8 %multiply_convert_fusion.3 = bf16[768,768]{1,0:T(8,128)(2,1)} fusion(bf16[576,768]{0,1:T(8,128)(2,1)} %bitcast.162, bf16[576,1536]{1,0:T(8,128)(2,1)} %copy-done.77), kind=kOutput, calls=%fused_computation.23 | convolution fusion | flops 680656896 | bytes 3047424 | tf_op jit(solution)/shard_map/dot_general | solution.py:60
  141.0 5.3 %collective-permute-done.2 = bf16[384,768]{1,0:T(8,128)(2,1)} collective-permute-done((bf16[384,768]{1,0:T(8,128)(2,1)}, bf16[384,768]{1,0:T(8,128)(2,1)}, u32[]{:S(2)}, u32[]{:S(2)}) %collective-permute-start.2) | collective-permute-done | bytes 589856 | tf_op jit(solution)/shard_map/ppermute | solution.py:104
  146.3 2.3 fusion.20
  148.7 4.3 %collective-permute-start.4 = (bf16[384,768]{1,0:T(8,128)(2,1)S(1)}, bf16[384,768]{1,0:T(8,128)(2,1)S(1)}, u32[]{:S(2)}, u32[]{:S(2)}) collective-permute-start(bf16[384,768]{1,0:T(8,128)(2,1)S(1)} %get-tuple-element.51), channel_id=1, source_target_pairs={{0,8},{4,12},{8,16},{12,20},{1,9},{5,13},{9,17},{13,21},{2,10},{6,... | collective-permute-start | bytes 1769480 | tf_op jit(solution)/shard_map/ppermute | solution.py:104
  153.9 2.5 fusion.117
  156.4 4.2 %fusion.141 = f32[768,1536]{1,0:T(8,128)} fusion(bf16[576,768]{0,1:T(8,128)(2,1)S(1)} %bitcast.160, bf16[576,1536]{1,0:T(8,128)(2,1)S(1)} %copy-done.80), kind=kOutput, calls=%fused_computation.405 | convolution fusion | flops 1358954496 | bytes 7372800 | tf_op jit(solution)/shard_map/dot_general | solution.py:60
  160.6 4.7 %collective-permute-done.4 = bf16[384,768]{1,0:T(8,128)(2,1)S(1)} collective-permute-done((bf16[384,768]{1,0:T(8,128)(2,1)S(1)}, bf16[384,768]{1,0:T(8,128)(2,1)S(1)}, u32[]{:S(2)}, u32[]{:S(2)}) %collective-permute-start.4) | collective-permute-done | bytes 589856 | tf_op jit(solution)/shard_map/ppermute | solution.py:104
  165.3 2.8 fusion.19
  168.1 9.6 %collective-permute-start.9 = (bf16[384,768]{1,0:T(8,128)(2,1)}, bf16[384,768]{1,0:T(8,128)(2,1)}, u32[]{:S(2)}, u32[]{:S(2)}) collective-permute-start(bf16[384,768]{1,0:T(8,128)(2,1)} %get-tuple-element.55), channel_id=1, source_target_pairs={{0,8},{4,12},{8,16},{12,20},{16,24},{20,28},{1,9},{5,13},{9,17},{1... | collective-permute-start | bytes 1769480 | tf_op jit(solution)/shard_map/ppermute | solution.py:104
  180.5 6.3 %all-reduce.3 = (f32[576]{0:T(1024)S(1)}, f32[576]{0:T(1024)S(1)}) all-reduce(f32[576]{0:T(1024)S(1)} %get-tuple-element.128, f32[576]{0:T(1024)S(1)} %get-tuple-element.127), channel_id=1, replica_groups=mesh['tile'=8,'chan'=4] {'chan'}, use_global_device_ids=true, to_apply=%region_12.13 | all-reduce | flops 1152 | bytes 9216 | tf_op jit(solution)/shard_map/psum | solution.py:207
  187.2 2.1 collective-permute-start.7
  191.0 2.1 multiply_reduce_fusion.18
  193.2 2.1 multiply_reduce_fusion
  196.4 3.8 %convert_add_fusion = f32[768,1536]{1,0:T(8,128)S(1)} fusion(bf16[768,1536]{1,0:T(8,128)(2,1)} %collective-permute-done.8, f32[768,1536]{1,0:T(8,128)} %fusion.141), kind=kLoop, calls=%fused_computation.3 | loop fusion | flops 3538944 | bytes 11796480 | tf_op jit(solution)/shard_map/add | solution.py:222
  200.6 18.1 %collective-permute-done.7 = bf16[3,48,384]{2,1,0:T(8,128)(2,1)S(1)} collective-permute-done((bf16[3,48,384]{2,1,0:T(8,128)(2,1)S(1)}, bf16[3,48,384]{2,1,0:T(8,128)(2,1)S(1)}, u32[]{:S(2)}, u32[]{:S(2)}) %collective-permute-start.7) | collective-permute-done | bytes 110624 | tf_op jit(solution)/shard_map/ppermute | solution.py:24
  221.3 6.6 %fusion.109 = f32[12,48,384]{2,1,0:T(8,128)S(1)} fusion(f32[18,48,384]{2,1,0:T(8,128)S(1)} %convert_select_fusion, f32[384]{0:T(512)S(1)} %get-tuple-element.176, f32[384]{0:T(512)S(1)} %get-tuple-element.177, f32[384]{0:T(512)S(1)} %get-tuple-element.130, f32[384]{0:T(512)S(1)} %get-tuple-element.131, f32[384]{0:T(512)S(1)} %get-tuple-element.132, ...), kind=kLoop, calls=%fused_computation.224 | loop fusion | flops 21454848 | bytes 8505344 | tf_op jit(solution)/shard_map/add | solution.py:40
  228.9 3.2 %collective-permute-done.13 = bf16[192,1536]{1,0:T(8,128)(2,1)S(1)} collective-permute-done((bf16[192,1536]{1,0:T(8,128)(2,1)S(1)}, bf16[192,1536]{1,0:T(8,128)(2,1)S(1)}, u32[]{:S(2)}, u32[]{:S(2)}) %collective-permute-start.13) | collective-permute-done | bytes 589856 | tf_op jit(solution)/shard_map/ppermute | solution.py:104
  237.7 5.1 %collective-permute-start.15 = (bf16[192,768]{1,0:T(8,128)(2,1)}, bf16[192,768]{1,0:T(8,128)(2,1)}, u32[]{:S(2)}, u32[]{:S(2)}) collective-permute-start(bf16[192,768]{1,0:T(8,128)(2,1)} %get-tuple-element.69), channel_id=1, source_target_pairs={{0,8},{4,12},{1,9},{5,13},{2,10},{6,14},{3,11},{7,15}} | collective-permute-start | bytes 884744 | tf_op jit(solution)/shard_map/ppermute | solution.py:104
  245.2 5.0 %collective-permute-done.15 = bf16[192,768]{1,0:T(8,128)(2,1)} collective-permute-done((bf16[192,768]{1,0:T(8,128)(2,1)}, bf16[192,768]{1,0:T(8,128)(2,1)}, u32[]{:S(2)}, u32[]{:S(2)}) %collective-permute-start.15) | collective-permute-done | bytes 294944 | tf_op jit(solution)/shard_map/ppermute | solution.py:104
  252.0 5.0 %collective-permute-start.17 = (bf16[192,768]{1,0:T(8,128)(2,1)S(1)}, bf16[192,768]{1,0:T(8,128)(2,1)S(1)}, u32[]{:S(2)}, u32[]{:S(2)}) collective-permute-start(bf16[192,768]{1,0:T(8,128)(2,1)S(1)} %get-tuple-element.71), channel_id=1, source_target_pairs={{0,8},{4,12},{8,16},{12,20},{1,9},{5,13},{9,17},{13,21},{2,10},{6,... | collective-permute-start | bytes 884744 | tf_op jit(solution)/shard_map/ppermute | solution.py:104
  257.0 1.8 fusion.18
  258.9 8.3 %collective-permute-done.17 = bf16[192,768]{1,0:T(8,128)(2,1)S(1)} collective-permute-done((bf16[192,768]{1,0:T(8,128)(2,1)S(1)}, bf16[192,768]{1,0:T(8,128)(2,1)S(1)}, u32[]{:S(2)}, u32[]{:S(2)}) %collective-permute-start.17) | collective-permute-done | bytes 294944 | tf_op jit(solution)/shard_map/ppermute | solution.py:104
  268.7 5.0 %collective-permute-start.19 = (bf16[192,768]{1,0:T(8,128)(2,1)S(1)}, bf16[192,768]{1,0:T(8,128)(2,1)S(1)}, u32[]{:S(2)}, u32[]{:S(2)}) collective-permute-start(bf16[192,768]{1,0:T(8,128)(2,1)S(1)} %get-tuple-element.73), channel_id=1, source_target_pairs={{0,8},{4,12},{8,16},{12,20},{16,24},{20,28},{1,9},{5,13},{9,17},{1... | collective-permute-start | bytes 884744 | tf_op jit(solution)/shard_map/ppermute | solution.py:104
  275.5 4.6 %collective-permute-start.23 = (bf16[192,1536]{1,0:T(8,128)(2,1)S(1)}, bf16[192,1536]{1,0:T(8,128)(2,1)S(1)}, u32[]{:S(2)}, u32[]{:S(2)}) collective-permute-start(bf16[192,1536]{1,0:T(8,128)(2,1)S(1)} %get-tuple-element.76), channel_id=1, source_target_pairs={{0,8},{4,12},{8,16},{12,20},{16,24},{20,28},{1,9},{5,13},{9,17},{1... | collective-permute-start | bytes 1769480 | tf_op jit(solution)/shard_map/ppermute | solution.py:104
  281.5 8.2 %collective-permute-done.24 = bf16[192,1536]{1,0:T(8,128)(2,1)S(1)} collective-permute-done((bf16[192,1536]{1,0:T(8,128)(2,1)S(1)}, bf16[192,1536]{1,0:T(8,128)(2,1)S(1)}, u32[]{:S(2)}, u32[]{:S(2)}) %collective-permute-start.24) | collective-permute-done | bytes 589856 | tf_op jit(solution)/shard_map/ppermute | solution.py:105
  291.0 2.5 fusion.15
  293.5 18.0 %all-reduce.6.cloned.1.call-done = f32[49,384]{1,0:T(8,128)} async-done(((f32[49,384]{1,0:T(8,128)}), f32[49,384]{1,0:T(8,128)}) %all-reduce.6.cloned.1.call-update) | async-done | bytes 75280 | tf_op jit(solution)/shard_map/psum | solution.py:220
  (329 shorter events, 42.2 us)
Async XLA Ops:
  7.2 24.2 %copy-start = (bf16[1152,384]{1,0:T(8,128)(2,1)S(1)}, bf16[1152,384]{1,0:T(8,128)(2,1)}, u32[]{:S(2)}) copy-start(bf16[1152,384]{1,0:T(8,128)(2,1)} %param.10) | copy-start | bytes 2654212
  8.2 25.8 %collective-permute-start.1 = (bf16[3,48,384]{2,1,0:T(8,128)(2,1)S(1)}, bf16[3,48,384]{2,1,0:T(8,128)(2,1)S(1)}, u32[]{:S(2)}, u32[]{:S(2)}) collective-permute-start(bf16[3,48,384]{2,1,0:T(8,128)(2,1)S(1)} %bitcast.168), channel_id=1, source_target_pairs={{4,0},{8,4},{12,8},{16,12},{20,16},{24,20},{28,24},{0,28},{5,1},{9... | collective-permute-start | bytes 331784 | tf_op jit(solution)/shard_map/ppermute | solution.py:24
  14.3 19.7 %collective-permute-start = (bf16[3,48,384]{2,1,0:T(8,128)(2,1)S(1)}, bf16[3,48,384]{2,1,0:T(8,128)(2,1)S(1)}, u32[]{:S(2)}, u32[]{:S(2)}) collective-permute-start(bf16[3,48,384]{2,1,0:T(8,128)(2,1)S(1)} %bitcast.167), channel_id=1, source_target_pairs={{0,4},{4,8},{8,12},{12,16},{16,20},{20,24},{24,28},{28,0},{1,5},{5... | collective-permute-start | bytes 331784 | tf_op jit(solution)/shard_map/ppermute | solution.py:23
  18.8 12.5 %all-to-all-start = ((s32[8,1,144]{2,1,0:T(1,128)}), s32[8,1,144]{2,1,0:T(1,128)S(1)}, u32[]{:S(2)}, u32[]{:S(2)}) async-start(s32[8,1,144]{2,1,0:T(1,128)} %all_to_all.9), calls=%async_computation | async-start | bytes 16384 | tf_op jit(solution)/shard_map/all_to_all | solution.py:140
  24.8 52.2 %all-gather.7.cloned.1.call-start = ((), (), s32[]{:S(2)}) async-start(), calls=%async_computation.4 | async-start | bytes 2211840 | tf_op jit(solution)/shard_map/all_gather | solution.py:166
  48.0 48.1 %all-gather.5.cloned.1.call-start = ((), (), s32[]{:S(2)}) async-start(), calls=%async_computation.3 | async-start | bytes 2211840 | tf_op jit(solution)/shard_map/all_gather | solution.py:173
  76.7 102.3 %reduce-scatter.4.cloned.1.call-start = ((), (), s32[]{:S(2)}) async-start(), calls=%async_computation.6 | async-start | bytes 2457600
  129.6 181.9 %all-reduce.6.cloned.1.call-start = ((), (), s32[]{:S(2)}) async-start(), calls=%async_computation.5 | async-start | bytes 172032 | tf_op jit(solution)/shard_map/psum | solution.py:220
  129.7 16.7 %collective-permute-start.2 = (bf16[384,768]{1,0:T(8,128)(2,1)}, bf16[384,768]{1,0:T(8,128)(2,1)}, u32[]{:S(2)}, u32[]{:S(2)}) collective-permute-start(bf16[384,768]{1,0:T(8,128)(2,1)} %get-tuple-element.45), channel_id=1, source_target_pairs={{0,8},{4,12},{1,9},{5,13},{2,10},{6,14},{3,11},{7,15}} | collective-permute-start | bytes 1769480 | tf_op jit(solution)/shard_map/ppermute | solution.py:104
  133.9 12.5 %collective-permute-start.3 = (bf16[384,768]{1,0:T(8,128)(2,1)}, bf16[384,768]{1,0:T(8,128)(2,1)}, u32[]{:S(2)}, u32[]{:S(2)}) collective-permute-start(bf16[384,768]{1,0:T(8,128)(2,1)} %get-tuple-element.47), channel_id=1, source_target_pairs={{28,20},{24,16},{29,21},{25,17},{30,22},{26,18},{31,23},{27,19}} | collective-permute-start | bytes 1769480 | tf_op jit(solution)/shard_map/ppermute | solution.py:105
  135.4 61.0 %collective-permute-start.8 = (bf16[768,1536]{1,0:T(8,128)(2,1)}, bf16[768,1536]{1,0:T(8,128)(2,1)}, u32[]{:S(2)}, u32[]{:S(2)}) collective-permute-start(bf16[768,1536]{1,0:T(8,128)(2,1)} %multiply_convert_fusion), channel_id=1, source_target_pairs={{0,4},{4,0},{8,12},{12,8},{16,20},{20,16},{24,28},{28,24},{1,5},{5... | collective-permute-start | bytes 7077896 | tf_op jit(solution)/shard_map/ppermute | solution.py:69
  140.6 92.9 %collective-permute-start.12 = (bf16[768,768]{1,0:T(8,128)(2,1)}, bf16[768,768]{1,0:T(8,128)(2,1)}, u32[]{:S(2)}, u32[]{:S(2)}) collective-permute-start(bf16[768,768]{1,0:T(8,128)(2,1)} %multiply_convert_fusion.3), channel_id=1, source_target_pairs={{0,4},{4,0},{8,12},{12,8},{16,20},{20,16},{24,28},{28,24},{1,5},{5... | collective-permute-start | bytes 3538952 | tf_op jit(solution)/shard_map/ppermute | solution.py:69
  148.7 16.6 %collective-permute-start.4 = (bf16[384,768]{1,0:T(8,128)(2,1)S(1)}, bf16[384,768]{1,0:T(8,128)(2,1)S(1)}, u32[]{:S(2)}, u32[]{:S(2)}) collective-permute-start(bf16[384,768]{1,0:T(8,128)(2,1)S(1)} %get-tuple-element.51), channel_id=1, source_target_pairs={{0,8},{4,12},{8,16},{12,20},{1,9},{5,13},{9,17},{13,21},{2,10},{6,... | collective-permute-start | bytes 1769480 | tf_op jit(solution)/shard_map/ppermute | solution.py:104
  153.0 12.3 %collective-permute-start.5 = (bf16[384,768]{1,0:T(8,128)(2,1)S(1)}, bf16[384,768]{1,0:T(8,128)(2,1)S(1)}, u32[]{:S(2)}, u32[]{:S(2)}) collective-permute-start(bf16[384,768]{1,0:T(8,128)(2,1)S(1)} %get-tuple-element.52), channel_id=1, source_target_pairs={{28,20},{24,16},{20,12},{16,8},{29,21},{25,17},{21,13},{17,9},{30,... | collective-permute-start | bytes 1769480 | tf_op jit(solution)/shard_map/ppermute | solution.py:105
  168.1 74.8 %collective-permute-start.9 = (bf16[384,768]{1,0:T(8,128)(2,1)}, bf16[384,768]{1,0:T(8,128)(2,1)}, u32[]{:S(2)}, u32[]{:S(2)}) collective-permute-start(bf16[384,768]{1,0:T(8,128)(2,1)} %get-tuple-element.55), channel_id=1, source_target_pairs={{0,8},{4,12},{8,16},{12,20},{16,24},{20,28},{1,9},{5,13},{9,17},{1... | collective-permute-start | bytes 1769480 | tf_op jit(solution)/shard_map/ppermute | solution.py:104
  177.7 65.2 %collective-permute-start.10 = (bf16[384,768]{1,0:T(8,128)(2,1)S(1)}, bf16[384,768]{1,0:T(8,128)(2,1)}, u32[]{:S(2)}, u32[]{:S(2)}) collective-permute-start(bf16[384,768]{1,0:T(8,128)(2,1)S(1)} %get-tuple-element.61), channel_id=1, source_target_pairs={{28,20},{24,16},{20,12},{16,8},{12,4},{8,0},{29,21},{25,17},{21,13... | collective-permute-start | bytes 1769480 | tf_op jit(solution)/shard_map/ppermute | solution.py:105
  187.2 31.5 %collective-permute-start.7 = (bf16[3,48,384]{2,1,0:T(8,128)(2,1)S(1)}, bf16[3,48,384]{2,1,0:T(8,128)(2,1)S(1)}, u32[]{:S(2)}, u32[]{:S(2)}) collective-permute-start(bf16[3,48,384]{2,1,0:T(8,128)(2,1)S(1)} %get-tuple-element.207), channel_id=1, source_target_pairs={{4,0},{8,4},{12,8},{16,12},{20,16},{24,20},{28,24},{0,28},{5,1},{9... | collective-permute-start | bytes 331784 | tf_op jit(solution)/shard_map/ppermute | solution.py:24
  196.4 23.7 %collective-permute-start.6 = (bf16[3,48,384]{2,1,0:T(8,128)(2,1)S(1)}, bf16[3,48,384]{2,1,0:T(8,128)(2,1)S(1)}, u32[]{:S(2)}, u32[]{:S(2)}) collective-permute-start(bf16[3,48,384]{2,1,0:T(8,128)(2,1)S(1)} %get-tuple-element.206), channel_id=1, source_target_pairs={{0,4},{4,8},{8,12},{12,16},{16,20},{20,24},{24,28},{28,0},{1,5},{5... | collective-permute-start | bytes 331784 | tf_op jit(solution)/shard_map/ppermute | solution.py:23
  200.1 32.0 %copy-start.2 = (f32[768,1536]{1,0:T(8,128)}, f32[768,1536]{1,0:T(8,128)S(1)}, u32[]{:S(2)}) copy-start(f32[768,1536]{1,0:T(8,128)S(1)} %convert_add_fusion) | copy-start | bytes 14155780
  200.3 20.7 %copy-start.11 = (f32[384]{0:T(512)S(1)}, f32[384]{0:T(512)}, u32[]{:S(2)}) copy-start(f32[384]{0:T(512)} %copy-done.10) | copy-start | bytes 4612
  200.3 20.7 %copy-start.13 = (f32[384]{0:T(512)S(1)}, f32[384]{0:T(512)}, u32[]{:S(2)}) copy-start(f32[384]{0:T(512)} %copy-done.12) | copy-start | bytes 4612
  200.3 20.7 %copy-start.15 = (f32[384]{0:T(512)S(1)}, f32[384]{0:T(512)}, u32[]{:S(2)}) copy-start(f32[384]{0:T(512)} %copy-done.14) | copy-start | bytes 4612
  200.3 20.7 %copy-start.17 = (f32[384]{0:T(512)S(1)}, f32[384]{0:T(512)}, u32[]{:S(2)}) copy-start(f32[384]{0:T(512)} %copy-done.16) | copy-start | bytes 4612
  200.3 20.7 %copy-start.19 = (f32[384]{0:T(512)S(1)}, f32[384]{0:T(512)}, u32[]{:S(2)}) copy-start(f32[384]{0:T(512)} %copy-done.18) | copy-start | bytes 4612
  200.4 20.7 %copy-start.21 = (f32[384]{0:T(512)S(1)}, f32[384]{0:T(512)}, u32[]{:S(2)}) copy-start(f32[384]{0:T(512)} %copy-done.20) | copy-start | bytes 4612
  200.4 20.7 %copy-start.23 = (f32[384]{0:T(512)S(1)}, f32[384]{0:T(512)}, u32[]{:S(2)}) copy-start(f32[384]{0:T(512)} %copy-done.22) | copy-start | bytes 4612
  200.4 20.7 %copy-start.25 = (f32[384]{0:T(512)S(1)}, f32[384]{0:T(512)}, u32[]{:S(2)}) copy-start(f32[384]{0:T(512)} %copy-done.24) | copy-start | bytes 4612
  200.4 20.7 %copy-start.27 = (f32[384]{0:T(512)S(1)}, f32[384]{0:T(512)}, u32[]{:S(2)}) copy-start(f32[384]{0:T(512)} %copy-done.26) | copy-start | bytes 4612
  200.4 20.7 %copy-start.29 = (f32[384]{0:T(512)S(1)}, f32[384]{0:T(512)}, u32[]{:S(2)}) copy-start(f32[384]{0:T(512)} %copy-done.28) | copy-start | bytes 4612
  200.4 20.7 %copy-start.31 = (f32[384]{0:T(512)S(1)}, f32[384]{0:T(512)}, u32[]{:S(2)}) copy-start(f32[384]{0:T(512)} %copy-done.30) | copy-start | bytes 4612
  200.4 20.7 %copy-start.33 = (f32[384]{0:T(512)S(1)}, f32[384]{0:T(512)}, u32[]{:S(2)}) copy-start(f32[384]{0:T(512)} %copy-done.32) | copy-start | bytes 4612
  200.4 20.7 %copy-start.35 = (f32[384]{0:T(512)S(1)}, f32[384]{0:T(512)}, u32[]{:S(2)}) copy-start(f32[384]{0:T(512)} %copy-done.34) | copy-start | bytes 4612
  218.7 13.4 %collective-permute-start.13 = (bf16[192,1536]{1,0:T(8,128)(2,1)S(1)}, bf16[192,1536]{1,0:T(8,128)(2,1)S(1)}, u32[]{:S(2)}, u32[]{:S(2)}) collective-permute-start(bf16[192,1536]{1,0:T(8,128)(2,1)S(1)} %get-tuple-element.59), channel_id=1, source_target_pairs={{0,8},{4,12},{1,9},{5,13},{2,10},{6,14},{3,11},{7,15}} | collective-permute-start | bytes 1769480 | tf_op jit(solution)/shard_map/ppermute | solution.py:104
  220.0 12.1 %collective-permute-start.14 = (bf16[192,1536]{1,0:T(8,128)(2,1)S(1)}, bf16[192,1536]{1,0:T(8,128)(2,1)S(1)}, u32[]{:S(2)}, u32[]{:S(2)}) collective-permute-start(bf16[192,1536]{1,0:T(8,128)(2,1)S(1)} %get-tuple-element.64), channel_id=1, source_target_pairs={{28,20},{24,16},{29,21},{25,17},{30,22},{26,18},{31,23},{27,19}} | collective-permute-start | bytes 1769480 | tf_op jit(solution)/shard_map/ppermute | solution.py:105
  233.5 40.3 %slice-start = ((s8[4718592]{0:T(1024)(128)(4,1)}), s8[524288]{0:T(1024)(128)(4,1)S(1)}, s32[]{:S(2)}) async-start(s8[4718592]{0:T(1024)(128)(4,1)} %bitcast.143), calls=%async_computation.7 | async-start | bytes 1048576
  236.1 9.1 %collective-permute-start.16 = (bf16[192,768]{1,0:T(8,128)(2,1)}, bf16[192,768]{1,0:T(8,128)(2,1)}, u32[]{:S(2)}, u32[]{:S(2)}) collective-permute-start(bf16[192,768]{1,0:T(8,128)(2,1)} %get-tuple-element.70), channel_id=1, source_target_pairs={{28,20},{24,16},{29,21},{25,17},{30,22},{26,18},{31,23},{27,19}} | collective-permute-start | bytes 884744 | tf_op jit(solution)/shard_map/ppermute | solution.py:105
  237.7 12.4 %collective-permute-start.15 = (bf16[192,768]{1,0:T(8,128)(2,1)}, bf16[192,768]{1,0:T(8,128)(2,1)}, u32[]{:S(2)}, u32[]{:S(2)}) collective-permute-start(bf16[192,768]{1,0:T(8,128)(2,1)} %get-tuple-element.69), channel_id=1, source_target_pairs={{0,8},{4,12},{1,9},{5,13},{2,10},{6,14},{3,11},{7,15}} | collective-permute-start | bytes 884744 | tf_op jit(solution)/shard_map/ppermute | solution.py:104
  242.8 31.0 %slice-start.1 = ((s8[4718592]{0:T(1024)(128)(4,1)}), s8[4194304]{0:T(1024)(128)(4,1)S(1)}, s32[]{:S(2)}) async-start(s8[4718592]{0:T(1024)(128)(4,1)} %bitcast.143), calls=%async_computation.8 | async-start | bytes 8388608
  242.8 31.0 %collective-permute-start.21 = (bf16[192,1536]{1,0:T(8,128)(2,1)}, bf16[192,1536]{1,0:T(8,128)(2,1)S(1)}, u32[]{:S(2)}, u32[]{:S(2)}) collective-permute-start(bf16[192,1536]{1,0:T(8,128)(2,1)} %get-tuple-element.67), channel_id=1, source_target_pairs={{0,8},{4,12},{8,16},{12,20},{1,9},{5,13},{9,17},{13,21},{2,10},{6,... | collective-permute-start | bytes 1769480 | tf_op jit(solution)/shard_map/ppermute | solution.py:104
  244.4 29.4 %collective-permute-start.22 = (bf16[192,1536]{1,0:T(8,128)(2,1)}, bf16[192,1536]{1,0:T(8,128)(2,1)S(1)}, u32[]{:S(2)}, u32[]{:S(2)}) collective-permute-start(bf16[192,1536]{1,0:T(8,128)(2,1)} %get-tuple-element.75), channel_id=1, source_target_pairs={{28,20},{24,16},{20,12},{16,8},{29,21},{25,17},{21,13},{17,9},{30,... | collective-permute-start | bytes 1769480 | tf_op jit(solution)/shard_map/ppermute | solution.py:105
  251.3 7.6 %collective-permute-start.18 = (bf16[192,768]{1,0:T(8,128)(2,1)S(1)}, bf16[192,768]{1,0:T(8,128)(2,1)S(1)}, u32[]{:S(2)}, u32[]{:S(2)}) collective-permute-start(bf16[192,768]{1,0:T(8,128)(2,1)S(1)} %get-tuple-element.72), channel_id=1, source_target_pairs={{28,20},{24,16},{20,12},{16,8},{29,21},{25,17},{21,13},{17,9},{30,... | collective-permute-start | bytes 884744 | tf_op jit(solution)/shard_map/ppermute | solution.py:105
  252.0 15.3 %collective-permute-start.17 = (bf16[192,768]{1,0:T(8,128)(2,1)S(1)}, bf16[192,768]{1,0:T(8,128)(2,1)S(1)}, u32[]{:S(2)}, u32[]{:S(2)}) collective-permute-start(bf16[192,768]{1,0:T(8,128)(2,1)S(1)} %get-tuple-element.71), channel_id=1, source_target_pairs={{0,8},{4,12},{8,16},{12,20},{1,9},{5,13},{9,17},{13,21},{2,10},{6,... | collective-permute-start | bytes 884744 | tf_op jit(solution)/shard_map/ppermute | solution.py:104
  258.9 21.3 %collective-permute-start.11 = (bf16[192,768]{1,0:T(8,128)(2,1)S(1)}, bf16[192,768]{1,0:T(8,128)(2,1)S(1)}, u32[]{:S(2)}, u32[]{:S(2)}) collective-permute-start(bf16[192,768]{1,0:T(8,128)(2,1)S(1)} %fusion.129), channel_id=1, source_target_pairs={{0,4},{4,0},{8,12},{12,8},{16,20},{20,16},{24,28},{28,24},{1,5},{5... | collective-permute-start | bytes 884744 | tf_op jit(solution)/shard_map/ppermute | solution.py:69
  267.5 12.7 %collective-permute-start.20 = (bf16[192,768]{1,0:T(8,128)(2,1)S(1)}, bf16[192,768]{1,0:T(8,128)(2,1)S(1)}, u32[]{:S(2)}, u32[]{:S(2)}) collective-permute-start(bf16[192,768]{1,0:T(8,128)(2,1)S(1)} %get-tuple-element.74), channel_id=1, source_target_pairs={{28,20},{24,16},{20,12},{16,8},{12,4},{8,0},{29,21},{25,17},{21,13... | collective-permute-start | bytes 884744 | tf_op jit(solution)/shard_map/ppermute | solution.py:105
  268.7 11.5 %collective-permute-start.19 = (bf16[192,768]{1,0:T(8,128)(2,1)S(1)}, bf16[192,768]{1,0:T(8,128)(2,1)S(1)}, u32[]{:S(2)}, u32[]{:S(2)}) collective-permute-start(bf16[192,768]{1,0:T(8,128)(2,1)S(1)} %get-tuple-element.73), channel_id=1, source_target_pairs={{0,8},{4,12},{8,16},{12,20},{16,24},{20,28},{1,9},{5,13},{9,17},{1... | collective-permute-start | bytes 884744 | tf_op jit(solution)/shard_map/ppermute | solution.py:104
  274.2 15.4 %collective-permute-start.24 = (bf16[192,1536]{1,0:T(8,128)(2,1)S(1)}, bf16[192,1536]{1,0:T(8,128)(2,1)S(1)}, u32[]{:S(2)}, u32[]{:S(2)}) collective-permute-start(bf16[192,1536]{1,0:T(8,128)(2,1)S(1)} %get-tuple-element.77), channel_id=1, source_target_pairs={{28,20},{24,16},{20,12},{16,8},{12,4},{8,0},{29,21},{25,17},{21,13... | collective-permute-start | bytes 1769480 | tf_op jit(solution)/shard_map/ppermute | solution.py:105
  275.5 15.5 %collective-permute-start.23 = (bf16[192,1536]{1,0:T(8,128)(2,1)S(1)}, bf16[192,1536]{1,0:T(8,128)(2,1)S(1)}, u32[]{:S(2)}, u32[]{:S(2)}) collective-permute-start(bf16[192,1536]{1,0:T(8,128)(2,1)S(1)} %get-tuple-element.76), channel_id=1, source_target_pairs={{0,8},{4,12},{8,16},{12,20},{16,24},{20,28},{1,9},{5,13},{9,17},{1... | collective-permute-start | bytes 1769480 | tf_op jit(solution)/shard_map/ppermute | solution.py:104
  280.3 32.8 %copy-start.1 = (bf16[1152,384]{1,0:T(8,128)(2,1)S(1)}, bf16[1152,384]{1,0:T(8,128)(2,1)}, u32[]{:S(2)}) copy-start(bf16[1152,384]{1,0:T(8,128)(2,1)} %param.10) | copy-start | bytes 2654212
  (70 other events, 743.6 us)
Sparse Core Ops, SparseCore 0:
  48.1 19.5 all-gather.6
  76.8 19.2 all-gather.4
  129.7 30.6 reduce-scatter.3
  242.9 68.5 all-reduce.5

commit v3 on v1

v3 whole, which is shorter than its diff:
```python
import functools
import math

import jax
import jax.numpy as jnp
from jax import lax
from jax.experimental import pallas as pl
from jax.experimental.pallas import tpu as pltpu
from jax.sharding import PartitionSpec as P

C = 1536
KSIZE = 7
PAGE_SIDE = 48


EPS = 1e-06


def extended_2(value, sides, width):
    for axis, dim in sides:
        peers, length = (lax.axis_size(axis), value.shape[dim])
        up = [(i, (i + 1) % peers) for i in range(peers)]
        down = [(j, i) for i, j in up]
        last = lax.slice_in_dim(value, length - width, length, axis=dim)
        first = lax.slice_in_dim(value, 0, width, axis=dim)
        before = lax.ppermute(last, axis, up)
        after = lax.ppermute(first, axis, down)
        value = jnp.concatenate([before, value, after], axis=dim)
    return value


def gelu_parts(preact):
    normal_cdf = 0.5 * (1.0 + jax.scipy.special.erf(preact * 0.7071067811865476))
    density = jnp.exp(-0.5 * preact * preact) * 0.3989422804014327
    return (preact * normal_cdf, normal_cdf + preact * density)


def depthwise(padded, kernel, rows, cols):
    total = jnp.zeros((rows, cols, padded.shape[2]), jnp.float32)
    for row_off in range(KSIZE):
        for col_off in range(KSIZE):
            window = padded[row_off : row_off + rows, col_off : col_off + cols, :]
            total = total + kernel[row_off * KSIZE + col_off] * window
    return total


def page_edges(extended, band_index, tiles_page, reach):
    height = extended.shape[0]
    row_ids = lax.broadcasted_iota(jnp.int32, (height, 1, 1), 0)
    first = band_index % tiles_page == 0
    final = band_index % tiles_page == tiles_page - 1
    dropped = (row_ids < reach) & first | (row_ids >= height - reach) & final
    kept = jnp.where(dropped, jnp.zeros_like(extended), extended)
    return jnp.pad(kept, ((0, 0), (reach, reach), (0, 0)))


def after(value, *others):
    return lax.optimization_barrier((value, *others))[0]


LINES = 4
CHUNK = 256
MESH = pl.DeviceIdType.MESH


def sum_kernel(
    factor, columns, values, out, pair_out, pair_in, parts, up_out, up_in, down_out, down_in,
    pair_sent, pair_got, up_sent, up_got, down_sent, down_got,
):
    me = lax.axis_index("tile")
    side, place = me % 2, me // 2
    rows = columns.shape[0] // (2 * LINES)
    chunks = values.shape[1] // CHUNK
    pair = me + 1 - 2 * side
    has_up, has_down = place < LINES - 1, place > 0

    barrier = pltpu.get_barrier_semaphore()
    pl.semaphore_signal(barrier, inc=1, device_id={"tile": pair}, device_id_type=MESH)

    @pl.when(has_up)
    def _():
        pl.semaphore_signal(barrier, inc=1, device_id={"tile": me + 2}, device_id_type=MESH)

    @pl.when(has_down)
    def _():
        pl.semaphore_signal(barrier, inc=1, device_id={"tile": me - 2}, device_id_type=MESH)

    @pl.when(has_up & has_down)
    def _():
        pl.semaphore_wait(barrier, 3)

    @pl.when(jnp.logical_not(has_up & has_down))
    def _():
        pl.semaphore_wait(barrier, 2)

    def swap(j):
        return pltpu.make_async_remote_copy(
            src_ref=pair_out.at[j],
            dst_ref=pair_in.at[j],
            send_sem=pair_sent.at[j],
            recv_sem=pair_got.at[j],
            device_id={"tile": pair},
            device_id_type=MESH,
        )

    def hop(upward, j, step):
        src, dst, sent, got, peer = (
            (up_out, up_in, up_sent, up_got, me + 2)
            if upward
            else (down_out, down_in, down_sent, down_got, me - 2)
        )
        return pltpu.make_async_remote_copy(
            src_ref=src.at[j, step],
            dst_ref=dst.at[j, step],
            send_sem=sent.at[j, step],
            recv_sem=got.at[j, step],
            device_id={"tile": peer},
            device_id_type=MESH,
        )

    def block(line, which, j):
        start = pl.multiple_of((2 * line + which) * rows, rows)
        return (
            jnp.dot(
                columns[pl.ds(start, rows), :],
                values[:, j * CHUNK : (j + 1) * CHUNK],
                preferred_element_type=jnp.float32,
            )
            * factor
        )

    for j in range(chunks):
        for line in range(LINES):
            pair_out[j, line] = block(line, 1 - side, j).astype(jnp.bfloat16)
        swap(j).start()
    for j in range(chunks):
        for line in range(LINES):
            parts[j, line] = block(line, side, j)

    def take(j):
        swap(j).wait_recv()
        parts[j] = parts[j] + pair_in[j].astype(jnp.float32)

    def send(j, step):
        for upward in (True, False):
            back = place if upward else LINES - 1 - place

            @pl.when(back <= step)
            def _(upward=upward, back=back):
                dest = LINES - 1 - step + place if upward else step - back
                total = up_out if upward else down_out
                total[j, step] = parts[j, dest].astype(jnp.bfloat16)

                if step:

                    @pl.when(back > 0)
                    def _():
                        hop(upward, j, step - 1).wait_recv()
                        got = up_in if upward else down_in
                        total[j, step] = (
                            parts[j, dest] + got[j, step - 1].astype(jnp.float32)
                        ).astype(jnp.bfloat16)

                hop(upward, j, step).start()

    def finish(j):
        where = pl.ds(j * CHUNK, CHUNK)
        out[:, where] = parts[j, place]

        @pl.when(has_down)
        def _():
            hop(True, j, LINES - 2).wait_recv()
            out[:, where] += up_in[j, LINES - 2].astype(jnp.float32)

        @pl.when(has_up)
        def _():
            hop(False, j, LINES - 2).wait_recv()
            out[:, where] += down_in[j, LINES - 2].astype(jnp.float32)

    for turn in range(chunks + 1):
        if turn < chunks:
            take(turn)
            send(turn, 0)
        if turn > 0:
            send(turn - 1, 2)
        if turn < chunks:
            send(turn, 1)
        if turn > 0:
            finish(turn - 1)
    for j in range(chunks):
        swap(j).wait_send()
        for step in range(LINES - 1):

            @pl.when(place <= step)
            def _(j=j, step=step):
                hop(True, j, step).wait_send()

            @pl.when(LINES - 1 - place <= step)
            def _(j=j, step=step):
                hop(False, j, step).wait_send()


def summed_product(columns, values, factor, ident):
    tiles = lax.axis_size("tile")
    (tokens, width), depth = columns.shape, values.shape[1]
    rows = width // tiles
    if tiles != 2 * LINES or rows % 16 or depth % CHUNK:
        whole = lax.dot_general(
            columns, values, (((0,), (0,)), ((), ())), preferred_element_type=jnp.float32
        )
        return lax.psum_scatter(whole * factor, "tile", scatter_dimension=0, tiled=True)
    chunks, hops = depth // CHUNK, LINES - 1
    line_buffer = pltpu.VMEM((chunks, hops, rows, CHUNK), jnp.bfloat16)
    pair_buffer = pltpu.VMEM((chunks, LINES, rows, CHUNK), jnp.bfloat16)
    return pl.pallas_call(
        functools.partial(sum_kernel, factor),
        out_shape=jax.ShapeDtypeStruct((rows, depth), jnp.float32),
        in_specs=[pl.BlockSpec(memory_space=pltpu.VMEM)] * 2,
        out_specs=pl.BlockSpec(memory_space=pltpu.VMEM),
        scratch_shapes=[
            pair_buffer,
            pair_buffer,
            pltpu.VMEM((chunks, LINES, rows, CHUNK), jnp.float32),
            *([line_buffer] * 4),
            *([pltpu.SemaphoreType.DMA((chunks,))] * 2),
            *([pltpu.SemaphoreType.DMA((chunks, hops))] * 4),
        ],
        compiler_params=pltpu.CompilerParams(
            collective_id=ident, has_side_effects=True, vmem_limit_bytes=36 * 1024 * 1024
        ),
        cost_estimate=pl.CostEstimate(
            flops=2 * tokens * width * depth,
            bytes_accessed=100_000_000,
            transcendentals=0,
        ),
    )(columns.T, values)


def shards(
    seq_grad, token_slot, pixels, dw_kernel, ln_gain, ln_bias, w_in, b_in, w_out, layer_scale
):
    tiles = lax.axis_size("tile")
    position = lax.axis_index("tile")
    band_index = (position + 1) % tiles
    slots = seq_grad.shape[0]
    capacity = slots // tiles
    tok_dev, chan_dev = pixels.shape
    reach = KSIZE // 2
    source = token_slot // slots
    local_slot = token_slot % slots
    onehot = (source[:, None] == jnp.arange(tiles, dtype=jnp.int32)[None, :]).astype(jnp.int32)
    ranks = jnp.sum((jnp.cumsum(onehot, axis=0) - onehot) * onehot, axis=1)
    seat = source * capacity + ranks
    seats = jnp.arange(tiles * capacity, dtype=jnp.int32)
    placed = seat[:, None] == seats[None, :]
    request = jnp.sum(jnp.where(placed, local_slot[:, None], 0), axis=0).reshape(tiles, capacity)
    asked = lax.all_to_all(request, "tile", split_axis=0, concat_axis=0, tiled=True)
    wanted = asked.reshape(-1, 1) == jnp.arange(slots, dtype=jnp.int32)[None, :]
    found = jnp.dot(
        wanted.astype(jnp.bfloat16), seq_grad, preferred_element_type=jnp.float32
    ).astype(jnp.bfloat16)
    arrived = lax.all_to_all(
        found.reshape(tiles, capacity, chan_dev), "tile", split_axis=0, concat_axis=0, tiled=True
    )
    rows = tok_dev // PAGE_SIDE
    tiles_page = PAGE_SIDE // rows
    grid = pixels.reshape(rows, PAGE_SIDE, chan_dev)
    extended = extended_2(grid, (("tile", 0),), reach)
    extended = after(extended, found)
    padded = page_edges(extended.astype(jnp.float32), band_index, tiles_page, reach)
    mixed = depthwise(padded, dw_kernel, rows, PAGE_SIDE).reshape(tok_dev, chan_dev)
    own_mean = jnp.mean(mixed, axis=1)
    own_center = mixed - own_mean[:, None]
    own_spread = jnp.sum(own_center * own_center, axis=1)
    stats = lax.all_gather(jnp.stack([own_mean, own_spread]), "chan")
    mean = jnp.mean(stats[:, 0], axis=0)
    shift = stats[:, 0] - mean
    spread = jnp.sum(stats[:, 1] + chan_dev * shift * shift, axis=0)
    center = mixed - mean[:, None]
    inv_std = lax.rsqrt(spread / C + EPS)[:, None]
    normed = center * inv_std
    ln_part = (normed * ln_gain + ln_bias).astype(jnp.bfloat16)
    ln_out = lax.all_gather(ln_part, "chan", axis=1, tiled=True)
    arrived = after(arrived, ln_part)
    upstream = jnp.dot(
        placed.astype(jnp.bfloat16),
        arrived.reshape(tiles * capacity, chan_dev),
        preferred_element_type=jnp.float32,
    ).astype(jnp.bfloat16)
    upstream_all = lax.all_gather(upstream, "chan", axis=1, tiled=True)
    scaled = (upstream_all.astype(jnp.float32) * layer_scale).astype(jnp.bfloat16)
    preact = jnp.dot(ln_out, w_in, preferred_element_type=jnp.float32) + b_in
    act_val, act_slope = gelu_parts(preact)
    hidden = act_val.astype(jnp.bfloat16)
    factor = 1.0 / math.sqrt(tok_dev * tiles)
    back_hidden = lax.dot_general(
        scaled, w_out, (((1,), (1,)), ((), ())), preferred_element_type=jnp.float32
    )
    back_pre = (back_hidden * act_slope).astype(jnp.bfloat16)
    partial_sum = lax.dot_general(
        back_pre, w_in, (((1,), (1,)), ((), ())), preferred_element_type=jnp.float32
    ).astype(jnp.bfloat16)
    back_norm = lax.psum_scatter(partial_sum, "chan", scatter_dimension=1, tiled=True)
    grad_w_out = summed_product(scaled, after(hidden, partial_sum), factor, 0)
    back_norm = after(back_norm, grad_w_out).astype(jnp.float32)
    grad_normed = back_norm * ln_gain
    sum_grad, sum_cross = lax.psum(
        (jnp.sum(grad_normed, axis=1), jnp.sum(grad_normed * normed, axis=1)), "chan"
    )
    grad_mixed = inv_std * (
        grad_normed - (sum_grad / C)[:, None] - normed * (sum_cross / C)[:, None]
    )
    grad_grid = grad_mixed.reshape(rows, PAGE_SIDE, chan_dev)
    taps = []
    for row_off in range(KSIZE):
        for col_off in range(KSIZE):
            window = padded[row_off : row_off + rows, col_off : col_off + PAGE_SIDE, :]
            taps.append(jnp.sum(window * grad_grid, axis=(0, 1)))
    taps = jnp.stack(taps) * factor
    grad_kernel = lax.psum(taps, "tile")
    grad_ext = extended_2(grad_grid.astype(jnp.bfloat16), (("tile", 0),), reach)
    grad_w_in = summed_product(ln_out, after(back_pre, taps, grad_mixed), factor, 1)
    grad_pad = page_edges(
        after(grad_ext, grad_w_in).astype(jnp.float32), band_index, tiles_page, reach
    )
    back_conv = depthwise(grad_pad, dw_kernel[::-1], rows, PAGE_SIDE).reshape(tok_dev, chan_dev)
    grad_input = (upstream.astype(jnp.float32) + back_conv).astype(jnp.bfloat16)
    return (grad_input, grad_w_in, grad_w_out.T, grad_kernel)


def solution(mesh):
    placed = (
        P("tile", "chan"),
        P("tile"),
        P("tile", "chan"),
        P(None, "chan"),
        P("chan"),
        P("chan"),
        P(None, "chan"),
        P("chan"),
        P("chan", None),
        P(),
    )
    return jax.shard_map(
        shards,
        mesh=mesh,
        in_specs=placed,
        out_specs=(P("tile", "chan"), P("tile", "chan"), P("chan", "tile"), P(None, "chan")),
        check_vma=False,
    )
```

time: 354 us -> 301 us (0.85)
  waiting for transfers between devices: 146 us -> 11.7 us
  Pallas kernels: 0 us -> 134 us
  starting transfers between devices: 44.8 us -> 17.2 us
  local copies, waits for them, and re-layouts: 41.1 us -> 21.8 us
  blocking collectives: 21.1 us -> 38.4 us
  other arithmetic: 51.4 us -> 36.3 us
  matrix products: 32.1 us -> 25.9 us
    pallas_call x0 -> x2, Pallas kernels: none -> 134 us  [summed_product(): pl.pallas_call(functools.partial(sum_kernel, factor), out_shape=jax.Shape...]
    ppermute x14 -> x0, waiting for transfers between devices: 107 us -> none  [the longest x2 77.3 us: pair_products(): arrived = lax.ppermute(product(1 - side).astype(jnp.bfloat16), 'tile', swap)]
    ppermute x14 -> x0, starting transfers between devices: 30 us -> none  [the longest x6 21 us: line_sum(): ups = lax.ppermute(up.astype(jnp.bfloat16), 'tile', up_pairs)]
    all_to_all x1, waiting for transfers between devices: 21 us -> 0.01 us  [shards(): lax.all_to_all(request, 'tile', split_axis=0, concat_axis=0, tiled=True)]
    all_to_all x1, blocking collectives: 9.55 us -> 26.9 us  [shards(): lax.all_to_all(found.reshape(tiles, capacity, chan_dev), 'tile', split_ax...]
    convert_element_type x8 -> x1, other arithmetic: 12.7 us -> 0.05 us  [shards(): grad_ext = extended_2(grad_grid.astype(jnp.bfloat16), (('tile', 0),), reach)]
    dot_general x4 -> x2, matrix products: 15 us -> 4.44 us  [the longest x1 2.58 us: shards(): jnp.dot(wanted.astype(jnp.bfloat16), seq_grad, preferred_element_type=jnp...]
    psum x1, waiting for transfers between devices: 10.6 us -> 0.01 us  [shards(): grad_kernel = lax.psum(taps, 'tile')]
  transfers between devices with their start and end apart: 23 -> 9, of which waited for: 8 -> 1; matrix products, arithmetic and copies ran while one was open for 27% -> 12% of each run, Pallas kernels for 0% -> 45%
where the time goes in v3:
time: 301 us
  Pallas kernels  134 us (45%)
  blocking collectives  38.4 us (13%)
  other arithmetic  36.3 us (12%)
  matrix products  25.9 us (9%)
  local copies, waits for them, and re-layouts  21.8 us (7%)
  starting transfers between devices  17.2 us (6%)
  between operations  15.4 us (5%)
  waiting for transfers between devices  11.7 us (4%)
    pallas_call x2, Pallas kernels, summed_product(): pl.pallas_call(functools.partial(sum_kernel, factor), out_shape=jax.Shape...  134 us
    all_to_all x1, blocking collectives, shards(): lax.all_to_all(found.reshape(tiles, capacity, chan_dev), 'tile', split_ax...  26.9 us
    all_gather x1, waiting for transfers between devices, shards(): upstream_all = lax.all_gather(upstream, 'chan', axis=1, tiled=True)  11.5 us
    unnamed x152, local copies, waits for them, and re-layouts  9.26 us
    dot_general x1, matrix products, shards(): preact = jnp.dot(ln_out, w_in, preferred_element_type=jnp.float32) + b_in  8.7 us
    dot_general x1, matrix products, shards(): lax.dot_general(scaled, w_out, (((1,), (1,)), ((), ())), preferred_elemen...  7.66 us
    add x1, other arithmetic, depthwise(): total = total + kernel[row_off * KSIZE + col_off] * window  7.34 us
    all_to_all x1, starting transfers between devices, shards(): lax.all_to_all(request, 'tile', split_axis=0, concat_axis=0, tiled=True)  7.28 us
  transfers between devices with their start and end apart: 9, of which 1 were waited for; matrix products, arithmetic and copies ran while one was open for 12% of the time, Pallas kernels for 45%

profile of v3, /device:TPU:0, one launch (start us, length us, event | category | flops | bytes accessed | tf_op | source)
XLA Modules:
  0.0 300.5 jit_solution(3314480858499819132)
XLA Ops:
  7.2 0.8 add_select_fusion.1
  8.0 1.4 reduce-window.6
  10.0 0.7 multiply_add_fusion.1
  10.7 0.3 select_reduce_fusion
  11.0 0.7 all_to_all.9
  11.7 7.3 %all-to-all-start = ((s32[8,1,144]{2,1,0:T(1,128)}), s32[8,1,144]{2,1,0:T(1,128)S(1)}, u32[]{:S(2)}, u32[]{:S(2)}) async-start(s32[8,1,144]{2,1,0:T(1,128)} %all_to_all.9), calls=%async_computation | async-start | bytes 16384 | tf_op jit(solution)/shard_map/all_to_all | solution.py:257
  19.0 1.0 fusion.111
  20.0 2.0 collective-permute-start
  22.1 2.8 collective-permute-start.1
  24.8 1.2 slice_reduce_fusion.48
  26.0 1.2 slice_reduce_fusion.47
  27.4 1.1 slice_reduce_fusion.46
  28.9 2.6 fusion.7
  32.0 6.6 %fusion.109 = (f32[12,48]{1,0:T(8,128)S(1)}, f32[12,48,384]{2,1,0:T(8,128)S(1)}) fusion(f32[384]{0:T(512)S(1)} %get-tuple-element.130, f32[384]{0:T(512)S(1)} %get-tuple-element.131, f32[384]{0:T(512)S(1)} %get-tuple-element.84, f32[18,48,384]{2,1,0:T(8,128)S(1)} %convert_select_fusion.1, f32[384]{0:T(512)S(1)} %get-tuple-element.85, ...), kind=kLoop, calls=%fused_computation.341 | loop fusion | flops 21675456 | bytes 8507648 | tf_op jit(solution)/shard_map/reduce_sum | solution.py:272
  38.7 0.3 multiply_reduce_fusion.50
  39.0 5.2 %all-gather.1 = f32[4,2,576]{2,1,0:T(2,128)S(1)} all-gather(f32[1,2,576]{2,1,0:T(2,128)S(1)} %maximum_bitcast_fusion), channel_id=2, replica_groups=mesh['tile'=8,'chan'=4] {'chan'}, dimensions={0}, use_global_device_ids=true | all-gather | bytes 23040 | tf_op jit(solution)/shard_map/all_gather | solution.py:275
  44.3 1.5 copy.43
  45.9 1.1 add_convert_fusion.1
  47.0 26.9 %all_to_all.14 = bf16[8,144,384]{2,1,0:T(8,128)(2,1)S(1)} all-to-all(bf16[8,144,384]{2,1,0:T(8,128)(2,1)} %bitcast.46), channel_id=1, replica_groups=mesh['tile'=8,'chan'=4] {'tile'}, dimensions={0} | all-to-all | bytes 1769472 | tf_op jit(solution)/shard_map/all_to_all | solution.py:262
  73.9 1.9 fusion.11
  76.1 8.7 %multiply_convert_fusion.1 = (bf16[576,1536]{1,0:T(8,128)(2,1)}, f32[576,1536]{1,0:T(8,128)}) fusion(f32[1536]{0:T(1024)S(1)} %copy-done.71, bf16[576,1536]{0,1:T(8,128)(2,1)} %all-gather.7.cloned.1.call-done, bf16[1536,1536]{1,0:T(8,128)(2,1)} %param.16), kind=kOutput, calls=%fused_computation.10 | convolution fusion | flops 2723217408 | bytes 11802624 | tf_op jit(solution)/shard_map/dot_general | solution.py:292
  84.8 11.5 %all-gather.5.cloned.1.call-done = bf16[576,1536]{0,1:T(8,128)(2,1)} async-done(((bf16[576,384]{0,1:T(8,128)(2,1)}), bf16[576,1536]{0,1:T(8,128)(2,1)}) %all-gather.5.cloned.1.call-update) | async-done | bytes 1769488 | tf_op jit(solution)/shard_map/all_gather | solution.py:290
  96.4 7.7 %fusion.6.values = bf16[576,1536]{1,0:T(8,128)(2,1)S(1)} fusion(f32[576,1536]{1,0:T(8,128)} %get-tuple-element.146, bf16[1536,1536]{1,0:T(8,128)(2,1)} %param.18, bf16[576,1536]{0,1:T(8,128)(2,1)} %all-gather.5.cloned.1.call-done, f32[1536]{0:T(1024)S(1)} %copy-done.67), kind=kOutput, calls=%fused_computation.9 | convolution fusion | flops 2729410560 | bytes 11802624 | tf_op jit(solution)/shard_map/dot_general | solution.py:296
  104.1 5.1 %convolution_convert_fusion = bf16[576,1536]{0,1:T(8,128)(2,1)} fusion(bf16[576,1536]{1,0:T(8,128)(2,1)S(1)} %fusion.6.values, bf16[1536,1536]{1,0:T(8,128)(2,1)S(1)} %bitcast.53), kind=kOutput, calls=%fused_computation.13 | convolution fusion | flops 2718793728 | bytes 8257536 | tf_op jit(solution)/shard_map/dot_general | solution.py:300
  109.1 1.3 copy-done.3
  110.5 2.1 fusion.103.columns
  112.6 68.2 %shard_map.129 = f32[192,1536]{1,0:T(8,128)S(1)} custom-call(bf16[1536,576]{1,0:T(8,128)(2,1)S(1)} %fusion.103.columns, bf16[576,1536]{1,0:T(8,128)(2,1)S(1)} %copy-done.2), custom_call_target="tpu_custom_call" | custom-call | flops 2717908992 | bytes 100000000 | tf_op jit(solution)/shard_map/pallas_call | solution.py:215
  180.8 1.6 fusion.12
  182.4 6.3 %all-reduce.3 = (f32[576]{0:T(1024)S(1)}, f32[576]{0:T(1024)S(1)}) all-reduce(f32[576]{0:T(1024)S(1)} %get-tuple-element.82, f32[576]{0:T(1024)S(1)} %get-tuple-element.81), channel_id=1, replica_groups=mesh['tile'=8,'chan'=4] {'chan'}, use_global_device_ids=true, to_apply=%region_12.13 | all-reduce | flops 1152 | bytes 9216 | tf_op jit(solution)/shard_map/psum | solution.py:307
  188.8 2.6 subtract_multiply_fusion
  191.4 2.4 copy.47
  193.8 3.1 %multiply_reduce_fusion.1 = (f32[384]{0:T(512)S(1)}, f32[384]{0:T(512)S(1)}, f32[384]{0:T(512)S(1)}, f32[384]{0:T(512)S(1)}, f32[384]{0:T(512)S(1)}, /*index=5*/...) fusion(f32[12,48,384]{2,1,0:T(8,128)} %bitcast.39, ...), kind=kLoop, calls=%fused_computation.211 | loop fusion | flops 7955712 | bytes 4893696 | tf_op jit(solution)/shard_map/reduce_sum | solution.py:318
  196.9 2.1 multiply_reduce_fusion.19
  199.0 1.5 multiply_reduce_fusion.37
  201.4 0.7 broadcast_multiply_fusion
  202.0 1.5 collective-permute-start.2
  203.5 3.3 %collective-permute-start.3 = (bf16[3,48,384]{2,1,0:T(8,128)(2,1)S(1)}, bf16[3,48,384]{2,1,0:T(8,128)(2,1)}, u32[]{:S(2)}, u32[]{:S(2)}) collective-permute-start(bf16[3,48,384]{2,1,0:T(8,128)(2,1)S(1)} %get-tuple-element.137), channel_id=1, source_target_pairs={{4,0},{8,4},{12,8},{16,12},{20,16},{24,20},{28,24},{0,28},{5,1},{9... | collective-permute-start | bytes 331784 | tf_op jit(solution)/shard_map/ppermute | solution.py:27
  206.9 1.5 copy-done.1
  208.4 1.5 copy-done.4
  209.9 65.7 %shard_map.130 = f32[192,1536]{1,0:T(8,128)S(1)} custom-call(bf16[1536,576]{1,0:T(8,128)(2,1)S(1)} %bitcast.38, bf16[576,1536]{1,0:T(8,128)(2,1)S(1)} %copy-done.4), custom_call_target="tpu_custom_call" | custom-call | flops 2717908992 | bytes 100000000 | tf_op jit(solution)/shard_map/pallas_call | solution.py:215
  275.9 1.0 pad_maximum_fusion.1
  277.4 7.3 %fusion.99 = f32[12,48,384]{2,1,0:T(8,128)} fusion(f32[18,48,384]{2,1,0:T(8,128)S(1)} %convert_select_fusion, f32[384]{0:T(512)S(1)} %copy-done.64, f32[384]{0:T(512)S(1)} %copy-done.66, f32[384]{0:T(512)S(1)} %get-tuple-element.84, f32[384]{0:T(512)S(1)} %get-tuple-element.85, f32[384]{0:T(512)S(1)} %get-tuple-element.86, f32[384]{0:T(512)S(1)} %get-tuple-element.87, ...), kind=kLoop, calls=%fused_computation.200 | loop fusion | flops 21454848 | bytes 8505344 | tf_op jit(solution)/shard_map/add | solution.py:43
  284.7 2.4 copy.48
  287.2 2.2 add_convert_fusion
  289.4 2.0 copy.49
  291.3 1.0 copy.61
  292.4 1.0 copy.62
  293.4 0.6 copy.63
  (237 shorter events, 2.5 us)
Async XLA Ops:
  7.2 21.7 %copy-start = (bf16[1152,384]{1,0:T(8,128)(2,1)S(1)}, bf16[1152,384]{1,0:T(8,128)(2,1)}, u32[]{:S(2)}) copy-start(bf16[1152,384]{1,0:T(8,128)(2,1)} %param.10) | copy-start | bytes 2654212
  11.7 17.0 %all-to-all-start = ((s32[8,1,144]{2,1,0:T(1,128)}), s32[8,1,144]{2,1,0:T(1,128)S(1)}, u32[]{:S(2)}, u32[]{:S(2)}) async-start(s32[8,1,144]{2,1,0:T(1,128)} %all_to_all.9), calls=%async_computation | async-start | bytes 16384 | tf_op jit(solution)/shard_map/all_to_all | solution.py:257
  19.0 57.1 %all-gather.7.cloned.1.call-start = ((), (), s32[]{:S(2)}) async-start(), calls=%async_computation.4 | async-start | bytes 2457600 | tf_op jit(solution)/shard_map/all_gather | solution.py:283
  20.0 11.4 %collective-permute-start = (bf16[3,48,384]{2,1,0:T(8,128)(2,1)S(1)}, bf16[3,48,384]{2,1,0:T(8,128)(2,1)S(1)}, u32[]{:S(2)}, u32[]{:S(2)}) collective-permute-start(bf16[3,48,384]{2,1,0:T(8,128)(2,1)S(1)} %bitcast.49), channel_id=1, source_target_pairs={{0,4},{4,8},{8,12},{12,16},{16,20},{20,24},{24,28},{28,0},{1,5},{5... | collective-permute-start | bytes 331784 | tf_op jit(solution)/shard_map/ppermute | solution.py:26
  22.1 9.4 %collective-permute-start.1 = (bf16[3,48,384]{2,1,0:T(8,128)(2,1)S(1)}, bf16[3,48,384]{2,1,0:T(8,128)(2,1)S(1)}, u32[]{:S(2)}, u32[]{:S(2)}) collective-permute-start(bf16[3,48,384]{2,1,0:T(8,128)(2,1)S(1)} %bitcast.48), channel_id=1, source_target_pairs={{4,0},{8,4},{12,8},{16,12},{20,16},{24,20},{28,24},{0,28},{5,1},{9... | collective-permute-start | bytes 331784 | tf_op jit(solution)/shard_map/ppermute | solution.py:27
  27.3 4.4 %copy-start.13 = (f32[384]{0:T(512)}, f32[384]{0:T(512)S(1)}, u32[]{:S(2)}) copy-start(f32[384]{0:T(512)S(1)} %get-tuple-element.105) | copy-start | bytes 4612
  27.3 4.4 %copy-start.15 = (f32[384]{0:T(512)}, f32[384]{0:T(512)S(1)}, u32[]{:S(2)}) copy-start(f32[384]{0:T(512)S(1)} %get-tuple-element.106) | copy-start | bytes 4612
  27.3 4.4 %copy-start.17 = (f32[384]{0:T(512)}, f32[384]{0:T(512)S(1)}, u32[]{:S(2)}) copy-start(f32[384]{0:T(512)S(1)} %get-tuple-element.107) | copy-start | bytes 4612
  27.3 4.4 %copy-start.19 = (f32[384]{0:T(512)}, f32[384]{0:T(512)S(1)}, u32[]{:S(2)}) copy-start(f32[384]{0:T(512)S(1)} %get-tuple-element.108) | copy-start | bytes 4612
  27.3 4.4 %copy-start.21 = (f32[384]{0:T(512)}, f32[384]{0:T(512)S(1)}, u32[]{:S(2)}) copy-start(f32[384]{0:T(512)S(1)} %get-tuple-element.109) | copy-start | bytes 4612
  27.3 4.4 %copy-start.23 = (f32[384]{0:T(512)}, f32[384]{0:T(512)S(1)}, u32[]{:S(2)}) copy-start(f32[384]{0:T(512)S(1)} %get-tuple-element.110) | copy-start | bytes 4612
  27.3 4.4 %copy-start.25 = (f32[384]{0:T(512)}, f32[384]{0:T(512)S(1)}, u32[]{:S(2)}) copy-start(f32[384]{0:T(512)S(1)} %get-tuple-element.111) | copy-start | bytes 4612
  27.4 4.4 %copy-start.27 = (f32[384]{0:T(512)}, f32[384]{0:T(512)S(1)}, u32[]{:S(2)}) copy-start(f32[384]{0:T(512)S(1)} %get-tuple-element.112) | copy-start | bytes 4612
  27.4 4.4 %copy-start.29 = (f32[384]{0:T(512)}, f32[384]{0:T(512)S(1)}, u32[]{:S(2)}) copy-start(f32[384]{0:T(512)S(1)} %get-tuple-element.113) | copy-start | bytes 4612
  27.4 4.4 %copy-start.31 = (f32[384]{0:T(512)}, f32[384]{0:T(512)S(1)}, u32[]{:S(2)}) copy-start(f32[384]{0:T(512)S(1)} %get-tuple-element.114) | copy-start | bytes 4612
  27.4 4.4 %copy-start.33 = (f32[384]{0:T(512)}, f32[384]{0:T(512)S(1)}, u32[]{:S(2)}) copy-start(f32[384]{0:T(512)S(1)} %get-tuple-element.115) | copy-start | bytes 4612
  27.4 4.4 %copy-start.35 = (f32[384]{0:T(512)}, f32[384]{0:T(512)S(1)}, u32[]{:S(2)}) copy-start(f32[384]{0:T(512)S(1)} %get-tuple-element.116) | copy-start | bytes 4612
  27.4 4.4 %copy-start.37 = (f32[384]{0:T(512)}, f32[384]{0:T(512)S(1)}, u32[]{:S(2)}) copy-start(f32[384]{0:T(512)S(1)} %get-tuple-element.117) | copy-start | bytes 4612
  27.4 4.4 %copy-start.39 = (f32[384]{0:T(512)}, f32[384]{0:T(512)S(1)}, u32[]{:S(2)}) copy-start(f32[384]{0:T(512)S(1)} %get-tuple-element.118) | copy-start | bytes 4612
  27.4 4.4 %copy-start.41 = (f32[384]{0:T(512)}, f32[384]{0:T(512)S(1)}, u32[]{:S(2)}) copy-start(f32[384]{0:T(512)S(1)} %get-tuple-element.119) | copy-start | bytes 4612
  27.4 4.4 %copy-start.43 = (f32[384]{0:T(512)}, f32[384]{0:T(512)S(1)}, u32[]{:S(2)}) copy-start(f32[384]{0:T(512)S(1)} %get-tuple-element.120) | copy-start | bytes 4612
  28.6 3.3 %copy-start.45 = (f32[384]{0:T(512)}, f32[384]{0:T(512)S(1)}, u32[]{:S(2)}) copy-start(f32[384]{0:T(512)S(1)} %get-tuple-element.121) | copy-start | bytes 4612
  28.6 3.3 %copy-start.47 = (f32[384]{0:T(512)}, f32[384]{0:T(512)S(1)}, u32[]{:S(2)}) copy-start(f32[384]{0:T(512)S(1)} %get-tuple-element.122) | copy-start | bytes 4612
  28.6 3.3 %copy-start.49 = (f32[384]{0:T(512)}, f32[384]{0:T(512)S(1)}, u32[]{:S(2)}) copy-start(f32[384]{0:T(512)S(1)} %get-tuple-element.123) | copy-start | bytes 4612
  28.6 3.3 %copy-start.51 = (f32[384]{0:T(512)}, f32[384]{0:T(512)S(1)}, u32[]{:S(2)}) copy-start(f32[384]{0:T(512)S(1)} %get-tuple-element.124) | copy-start | bytes 4612
  28.6 3.3 %copy-start.53 = (f32[384]{0:T(512)}, f32[384]{0:T(512)S(1)}, u32[]{:S(2)}) copy-start(f32[384]{0:T(512)S(1)} %get-tuple-element.125) | copy-start | bytes 4612
  28.6 3.3 %copy-start.55 = (f32[384]{0:T(512)}, f32[384]{0:T(512)S(1)}, u32[]{:S(2)}) copy-start(f32[384]{0:T(512)S(1)} %get-tuple-element.126) | copy-start | bytes 4612
  28.6 3.3 %copy-start.57 = (f32[384]{0:T(512)}, f32[384]{0:T(512)S(1)}, u32[]{:S(2)}) copy-start(f32[384]{0:T(512)S(1)} %get-tuple-element.127) | copy-start | bytes 4612
  28.6 3.3 %copy-start.59 = (f32[384]{0:T(512)}, f32[384]{0:T(512)S(1)}, u32[]{:S(2)}) copy-start(f32[384]{0:T(512)S(1)} %get-tuple-element.128) | copy-start | bytes 4612
  28.6 3.3 %copy-start.61 = (f32[384]{0:T(512)}, f32[384]{0:T(512)S(1)}, u32[]{:S(2)}) copy-start(f32[384]{0:T(512)S(1)} %get-tuple-element.129) | copy-start | bytes 4612
  28.7 3.3 %copy-start.63 = (f32[384]{0:T(512)}, f32[384]{0:T(512)S(1)}, u32[]{:S(2)}) copy-start(f32[384]{0:T(512)S(1)} %get-tuple-element.130) | copy-start | bytes 4612
  28.7 3.3 %copy-start.65 = (f32[384]{0:T(512)}, f32[384]{0:T(512)S(1)}, u32[]{:S(2)}) copy-start(f32[384]{0:T(512)S(1)} %get-tuple-element.131) | copy-start | bytes 4612
  38.6 5.8 %copy-start.7 = (f32[12,48,384]{2,1,0:T(8,128)}, f32[12,48,384]{2,1,0:T(8,128)S(1)}, u32[]{:S(2)}) copy-start(f32[12,48,384]{2,1,0:T(8,128)S(1)} %get-tuple-element.135) | copy-start | bytes 2654212
  38.6 7.3 %copy-start.12 = (f32[384]{0:T(512)S(1)}, f32[384]{0:T(512)}, u32[]{:S(2)}) copy-start(f32[384]{0:T(512)} %param.14) | copy-start | bytes 4612
  38.6 7.3 %copy-start.68 = (f32[384]{0:T(512)S(1)}, f32[384]{0:T(512)}, u32[]{:S(2)}) copy-start(f32[384]{0:T(512)} %param.15) | copy-start | bytes 4612
  45.8 30.0 %copy-start.6 = (f32[576,384]{0,1:T(8,128)}, f32[576,384]{0,1:T(8,128)S(1)}, u32[]{:S(2)}) copy-start(f32[576,384]{0,1:T(8,128)S(1)} %copy.43) | copy-start | bytes 2654212
  47.0 49.4 %all-gather.5.cloned.1.call-start = ((), (), s32[]{:S(2)}) async-start(), calls=%async_computation.3 | async-start | bytes 2457600 | tf_op jit(solution)/shard_map/all_gather | solution.py:290
  75.8 20.5 %copy-start.67 = (f32[1536]{0:T(1024)S(1)}, f32[1536]{0:T(1024)}, u32[]{:S(2)}) copy-start(f32[1536]{0:T(1024)} %param.19) | copy-start | bytes 18436
  75.8 104.9 %reduce-scatter.2.cloned.1.call-start = ((), (), s32[]{:S(2)}) async-start(), calls=%async_computation.5 | async-start | bytes 2457600 | tf_op jit(solution)/shard_map/reduce_scatter | solution.py:303
  76.1 27.9 %slice-start = ((s8[4718592]{0:T(1024)(128)(4,1)}), s8[524288]{0:T(1024)(128)(4,1)S(1)}, s32[]{:S(2)}) async-start(s8[4718592]{0:T(1024)(128)(4,1)} %bitcast.52), calls=%async_computation.7 | async-start | bytes 1048576
  96.4 7.7 %slice-start.1 = ((s8[4718592]{0:T(1024)(128)(4,1)}), s8[4194304]{0:T(1024)(128)(4,1)S(1)}, s32[]{:S(2)}) async-start(s8[4718592]{0:T(1024)(128)(4,1)} %bitcast.52), calls=%async_computation.8 | async-start | bytes 8388608
  110.4 180.9 %all-reduce.6.cloned.1.call-start = ((), (), s32[]{:S(2)}) async-start(), calls=%async_computation.6 | async-start | bytes 172032 | tf_op jit(solution)/shard_map/psum | solution.py:320
  193.8 3.1 %copy-start.5 = (f32[576,384]{1,0:T(8,128)S(1)}, f32[576,384]{1,0:T(8,128)}, u32[]{:S(2)}) copy-start(f32[576,384]{1,0:T(8,128)} %copy.47) | copy-start | bytes 2654212
  200.6 6.2 %copy-start.8 = (bf16[12,48,384]{2,1,0:T(8,128)(2,1)}, bf16[12,48,384]{2,1,0:T(8,128)(2,1)S(1)}, u32[]{:S(2)}) copy-start(bf16[12,48,384]{2,1,0:T(8,128)(2,1)S(1)} %convert_element_type.63) | copy-start | bytes 1327108
  202.0 73.8 %collective-permute-start.2 = (bf16[3,48,384]{2,1,0:T(8,128)(2,1)S(1)}, bf16[3,48,384]{2,1,0:T(8,128)(2,1)}, u32[]{:S(2)}, u32[]{:S(2)}) collective-permute-start(bf16[3,48,384]{2,1,0:T(8,128)(2,1)S(1)} %get-tuple-element.136), channel_id=1, source_target_pairs={{0,4},{4,8},{8,12},{12,16},{16,20},{20,24},{24,28},{28,0},{1,5},{5... | collective-permute-start | bytes 331784 | tf_op jit(solution)/shard_map/ppermute | solution.py:26
  203.5 72.3 %collective-permute-start.3 = (bf16[3,48,384]{2,1,0:T(8,128)(2,1)S(1)}, bf16[3,48,384]{2,1,0:T(8,128)(2,1)}, u32[]{:S(2)}, u32[]{:S(2)}) collective-permute-start(bf16[3,48,384]{2,1,0:T(8,128)(2,1)S(1)} %get-tuple-element.137), channel_id=1, source_target_pairs={{4,0},{8,4},{12,8},{16,12},{20,16},{24,20},{28,24},{0,28},{5,1},{9... | collective-permute-start | bytes 331784 | tf_op jit(solution)/shard_map/ppermute | solution.py:27
  209.9 66.0 %copy-start.9 = (bf16[12,48,384]{2,1,0:T(8,128)(2,1)S(1)}, bf16[12,48,384]{2,1,0:T(8,128)(2,1)}, u32[]{:S(2)}) copy-start(bf16[12,48,384]{2,1,0:T(8,128)(2,1)} %copy-done.8) | copy-start | bytes 1327108
  209.9 67.1 %copy-start.70 = (pred[18]{0:T(512)(128)(4,1)S(1)}, pred[18]{0:T(512)(128)(4,1)}, u32[]{:S(2)}) copy-start(pred[18]{0:T(512)(128)(4,1)} %copy-done.69) | copy-start | bytes 58
  (35 other events, 57.4 us)
Sparse Core Ops, SparseCore 0:
  47.1 20.4 all-gather.6
  76.0 20.3 all-gather.4
  110.6 30.6 reduce-scatter.1
  207.0 65.4 all-reduce.5

commit v4 on v3

--- a/solution.py
+++ b/solution.py
@@ -272,10 +272,14 @@
     own_mean = jnp.mean(mixed, axis=1)
     own_center = mixed - own_mean[:, None]
     own_spread = jnp.sum(own_center * own_center, axis=1)
-    stats = lax.all_gather(jnp.stack([own_mean, own_spread]), "chan")
-    mean = jnp.mean(stats[:, 0], axis=0)
-    shift = stats[:, 0] - mean
-    spread = jnp.sum(stats[:, 1] + chan_dev * shift * shift, axis=0)
+    own_stats = jnp.stack([own_mean, own_spread])
+    chans = lax.axis_size("chan")
+    stats = [own_stats] + [
+        lax.ppermute(own_stats, "chan", [(i, (i + turn) % chans) for i in range(chans)])
+        for turn in range(1, chans)
+    ]
+    mean = sum(one[0] for one in stats) / chans
+    spread = sum(one[1] + chan_dev * (one[0] - mean) * (one[0] - mean) for one in stats)
     center = mixed - mean[:, None]
     inv_std = lax.rsqrt(spread / C + EPS)[:, None]
     normed = center * inv_std

time: 301 us -> 299 us (level)
  blocking collectives: 38.4 us -> 33.2 us
    all_gather x1 -> x0, blocking collectives: 5.19 us -> none  [shards(): stats = lax.all_gather(jnp.stack([own_mean, own_spread]), 'chan')]
  transfers between devices with their start and end apart: 9 -> 12, of which waited for: 1 -> 1; matrix products, arithmetic and copies ran while one was open for 12% -> 12% of each run, Pallas kernels for 45% -> 45%
where the time goes in v4:
time: 299 us; the launch traced here: 298 us
  Pallas kernels  134 us (45%)
  other arithmetic  36.2 us (12%)
  blocking collectives  33.2 us (11%)
  matrix products  25.9 us (9%)
  local copies, waits for them, and re-layouts  22 us (7%)
  starting transfers between devices  20.2 us (7%)
  between operations  15.5 us (5%)
  waiting for transfers between devices  11.5 us (4%)
    pallas_call x2, Pallas kernels, summed_product(): pl.pallas_call(functools.partial(sum_kernel, factor), out_shape=jax.Shape...  134 us
    all_to_all x1, blocking collectives, shards(): lax.all_to_all(found.reshape(tiles, capacity, chan_dev), 'tile', split_ax...  26.8 us
    all_gather x1, waiting for transfers between devices, shards(): upstream_all = lax.all_gather(upstream, 'chan', axis=1, tiled=True)  11.4 us
    unnamed x152, local copies, waits for them, and re-layouts  9.26 us
    dot_general x1, matrix products, shards(): preact = jnp.dot(ln_out, w_in, preferred_element_type=jnp.float32) + b_in  8.7 us
    dot_general x1, matrix products, shards(): lax.dot_general(scaled, w_out, (((1,), (1,)), ((), ())), preferred_elemen...  7.66 us
    add x1, other arithmetic, depthwise(): total = total + kernel[row_off * KSIZE + col_off] * window  7.35 us
    all_to_all x1, starting transfers between devices, shards(): lax.all_to_all(request, 'tile', split_axis=0, concat_axis=0, tiled=True)  7.28 us
  transfers between devices with their start and end apart: 12, of which 1 were waited for; matrix products, arithmetic and copies ran while one was open for 12% of the time, Pallas kernels for 45%

profile of v4, /device:TPU:0, one launch (start us, length us, event | category | flops | bytes accessed | tf_op | source)
XLA Modules:
  0.0 298.1 jit_solution(17886452158537994131)
XLA Ops:
  7.2 0.8 add_select_fusion.1
  8.0 1.4 reduce-window.6
  10.0 0.7 multiply_add_fusion.1
  10.7 0.3 select_reduce_fusion
  11.0 0.7 all_to_all.9
  11.7 7.3 %all-to-all-start = ((s32[8,1,144]{2,1,0:T(1,128)}), s32[8,1,144]{2,1,0:T(1,128)S(1)}, u32[]{:S(2)}, u32[]{:S(2)}) async-start(s32[8,1,144]{2,1,0:T(1,128)} %all_to_all.9), calls=%async_computation | async-start | bytes 16384 | tf_op jit(solution)/shard_map/all_to_all | solution.py:257
  19.0 1.0 fusion.119
  20.0 2.0 collective-permute-start
  22.1 2.8 collective-permute-start.1
  24.8 1.2 slice_reduce_fusion.53
  26.1 1.2 slice_reduce_fusion.54
  27.4 1.1 slice_reduce_fusion.52
  28.9 2.6 fusion.7
  32.0 6.6 %fusion.117 = (f32[12,48]{1,0:T(8,128)S(1)}, f32[12,48,384]{2,1,0:T(8,128)S(1)}) fusion(f32[384]{0:T(512)S(1)} %get-tuple-element.126, f32[384]{0:T(512)S(1)} %get-tuple-element.127, f32[384]{0:T(512)S(1)} %get-tuple-element.80, f32[18,48,384]{2,1,0:T(8,128)S(1)} %convert_select_fusion.1, f32[384]{0:T(512)S(1)} %get-tuple-element.81, ...), kind=kLoop, calls=%fused_computation.354 | loop fusion | flops 21675456 | bytes 8507648 | tf_op jit(solution)/shard_map/reduce_sum | solution.py:272
  39.1 1.5 collective-permute-start.3
  40.7 1.4 collective-permute-start.4
  42.2 1.5 copy.32
  43.9 1.0 add_convert_fusion.1
  44.9 26.8 %all_to_all.14 = bf16[8,144,384]{2,1,0:T(8,128)(2,1)S(1)} all-to-all(bf16[8,144,384]{2,1,0:T(8,128)(2,1)} %bitcast.36), channel_id=1, replica_groups=mesh['tile'=8,'chan'=4] {'tile'}, dimensions={0} | all-to-all | bytes 1769472 | tf_op jit(solution)/shard_map/all_to_all | solution.py:262
  71.7 1.9 fusion.11
  73.9 8.7 %multiply_convert_fusion.1 = (bf16[576,1536]{1,0:T(8,128)(2,1)}, f32[576,1536]{1,0:T(8,128)}) fusion(f32[1536]{0:T(1024)S(1)} %copy-done.71, bf16[576,1536]{0,1:T(8,128)(2,1)} %all-gather.5.cloned.1.call-done, bf16[1536,1536]{1,0:T(8,128)(2,1)} %param.16), kind=kOutput, calls=%fused_computation.10 | convolution fusion | flops 2723217408 | bytes 11802624 | tf_op jit(solution)/shard_map/dot_general | solution.py:296
  82.6 11.4 %all-gather.3.cloned.1.call-done = bf16[576,1536]{0,1:T(8,128)(2,1)} async-done(((bf16[576,384]{0,1:T(8,128)(2,1)}), bf16[576,1536]{0,1:T(8,128)(2,1)}) %all-gather.3.cloned.1.call-update) | async-done | bytes 1769488 | tf_op jit(solution)/shard_map/all_gather | solution.py:294
  94.0 7.7 %fusion.6.values = bf16[576,1536]{1,0:T(8,128)(2,1)S(1)} fusion(f32[576,1536]{1,0:T(8,128)} %get-tuple-element.147, bf16[1536,1536]{1,0:T(8,128)(2,1)} %param.18, bf16[576,1536]{0,1:T(8,128)(2,1)} %all-gather.3.cloned.1.call-done, f32[1536]{0:T(1024)S(1)} %copy-done.67), kind=kOutput, calls=%fused_computation.9 | convolution fusion | flops 2729410560 | bytes 11802624 | tf_op jit(solution)/shard_map/dot_general | solution.py:300
  101.7 5.1 %convolution_convert_fusion = bf16[576,1536]{0,1:T(8,128)(2,1)} fusion(bf16[576,1536]{1,0:T(8,128)(2,1)S(1)} %fusion.6.values, bf16[1536,1536]{1,0:T(8,128)(2,1)S(1)} %bitcast.43), kind=kOutput, calls=%fused_computation.13 | convolution fusion | flops 2718793728 | bytes 8257536 | tf_op jit(solution)/shard_map/dot_general | solution.py:304
  106.8 1.3 copy-done.3
  108.1 2.1 fusion.103.columns
  110.2 68.1 %shard_map.129 = f32[192,1536]{1,0:T(8,128)S(1)} custom-call(bf16[1536,576]{1,0:T(8,128)(2,1)S(1)} %fusion.103.columns, bf16[576,1536]{1,0:T(8,128)(2,1)S(1)} %copy-done.2), custom_call_target="tpu_custom_call" | custom-call | flops 2717908992 | bytes 100000000 | tf_op jit(solution)/shard_map/pallas_call | solution.py:215
  178.4 1.6 fusion.12
  180.0 6.4 %all-reduce.3 = (f32[576]{0:T(1024)S(1)}, f32[576]{0:T(1024)S(1)}) all-reduce(f32[576]{0:T(1024)S(1)} %get-tuple-element.78, f32[576]{0:T(1024)S(1)} %get-tuple-element.77), channel_id=1, replica_groups=mesh['tile'=8,'chan'=4] {'chan'}, use_global_device_ids=true, to_apply=%region_10.11 | all-reduce | flops 1152 | bytes 9216 | tf_op jit(solution)/shard_map/psum | solution.py:311
  186.4 2.6 subtract_multiply_fusion
  189.0 2.4 copy.35
  191.4 3.1 %multiply_reduce_fusion.1 = (f32[384]{0:T(512)S(1)}, f32[384]{0:T(512)S(1)}, f32[384]{0:T(512)S(1)}, f32[384]{0:T(512)S(1)}, f32[384]{0:T(512)S(1)}, /*index=5*/...) fusion(f32[12,48,384]{2,1,0:T(8,128)} %bitcast.29, ...), kind=kLoop, calls=%fused_computation.211 | loop fusion | flops 7955712 | bytes 4893696 | tf_op jit(solution)/shard_map/reduce_sum | solution.py:322
  194.6 2.1 multiply_reduce_fusion.19
  196.7 1.5 multiply_reduce_fusion.37
  199.0 0.7 broadcast_multiply_fusion
  199.7 1.4 collective-permute-start.5
  201.1 3.3 %collective-permute-start.6 = (bf16[3,48,384]{2,1,0:T(8,128)(2,1)S(1)}, bf16[3,48,384]{2,1,0:T(8,128)(2,1)}, u32[]{:S(2)}, u32[]{:S(2)}) collective-permute-start(bf16[3,48,384]{2,1,0:T(8,128)(2,1)S(1)} %get-tuple-element.139), channel_id=1, source_target_pairs={{4,0},{8,4},{12,8},{16,12},{20,16},{24,20},{28,24},{0,28},{5,1},{9... | collective-permute-start | bytes 331784 | tf_op jit(solution)/shard_map/ppermute | solution.py:27
  204.5 1.5 copy-done.1
  206.0 1.5 copy-done.4
  207.5 65.6 %shard_map.130 = f32[192,1536]{1,0:T(8,128)S(1)} custom-call(bf16[1536,576]{1,0:T(8,128)(2,1)S(1)} %bitcast.28, bf16[576,1536]{1,0:T(8,128)(2,1)S(1)} %copy-done.4), custom_call_target="tpu_custom_call" | custom-call | flops 2717908992 | bytes 100000000 | tf_op jit(solution)/shard_map/pallas_call | solution.py:215
  273.4 1.0 pad_maximum_fusion.1
  274.9 7.4 %fusion.99 = f32[12,48,384]{2,1,0:T(8,128)} fusion(f32[18,48,384]{2,1,0:T(8,128)S(1)} %convert_select_fusion, f32[384]{0:T(512)S(1)} %copy-done.64, f32[384]{0:T(512)S(1)} %copy-done.66, f32[384]{0:T(512)S(1)} %get-tuple-element.80, f32[384]{0:T(512)S(1)} %get-tuple-element.81, f32[384]{0:T(512)S(1)} %copy-done.14, f32[384]{0:T(512)S(1)} %copy-done.16, ...), kind=kLoop, calls=%fused_computation.200 | loop fusion | flops 21454848 | bytes 8505344 | tf_op jit(solution)/shard_map/add | solution.py:43
  282.3 2.4 copy.36
  284.7 2.2 add_convert_fusion
  286.9 2.0 copy.37
  288.9 1.0 copy.43
  289.9 1.0 copy.44
  290.9 0.6 copy.45
  (244 shorter events, 3.1 us)
Async XLA Ops:
  7.2 21.7 %copy-start = (bf16[1152,384]{1,0:T(8,128)(2,1)S(1)}, bf16[1152,384]{1,0:T(8,128)(2,1)}, u32[]{:S(2)}) copy-start(bf16[1152,384]{1,0:T(8,128)(2,1)} %param.10) | copy-start | bytes 2654212
  11.7 17.0 %all-to-all-start = ((s32[8,1,144]{2,1,0:T(1,128)}), s32[8,1,144]{2,1,0:T(1,128)S(1)}, u32[]{:S(2)}, u32[]{:S(2)}) async-start(s32[8,1,144]{2,1,0:T(1,128)} %all_to_all.9), calls=%async_computation | async-start | bytes 16384 | tf_op jit(solution)/shard_map/all_to_all | solution.py:257
  19.0 54.9 %all-gather.5.cloned.1.call-start = ((), (), s32[]{:S(2)}) async-start(), calls=%async_computation.4 | async-start | bytes 2457600 | tf_op jit(solution)/shard_map/all_gather | solution.py:287
  20.0 11.4 %collective-permute-start = (bf16[3,48,384]{2,1,0:T(8,128)(2,1)S(1)}, bf16[3,48,384]{2,1,0:T(8,128)(2,1)S(1)}, u32[]{:S(2)}, u32[]{:S(2)}) collective-permute-start(bf16[3,48,384]{2,1,0:T(8,128)(2,1)S(1)} %bitcast.39), channel_id=1, source_target_pairs={{0,4},{4,8},{8,12},{12,16},{16,20},{20,24},{24,28},{28,0},{1,5},{5... | collective-permute-start | bytes 331784 | tf_op jit(solution)/shard_map/ppermute | solution.py:26
  22.1 9.4 %collective-permute-start.1 = (bf16[3,48,384]{2,1,0:T(8,128)(2,1)S(1)}, bf16[3,48,384]{2,1,0:T(8,128)(2,1)S(1)}, u32[]{:S(2)}, u32[]{:S(2)}) collective-permute-start(bf16[3,48,384]{2,1,0:T(8,128)(2,1)S(1)} %bitcast.38), channel_id=1, source_target_pairs={{4,0},{8,4},{12,8},{16,12},{20,16},{24,20},{28,24},{0,28},{5,1},{9... | collective-permute-start | bytes 331784 | tf_op jit(solution)/shard_map/ppermute | solution.py:27
  27.3 4.4 %copy-start.13 = (f32[384]{0:T(512)}, f32[384]{0:T(512)S(1)}, u32[]{:S(2)}) copy-start(f32[384]{0:T(512)S(1)} %get-tuple-element.82) | copy-start | bytes 4612
  27.3 4.4 %copy-start.15 = (f32[384]{0:T(512)}, f32[384]{0:T(512)S(1)}, u32[]{:S(2)}) copy-start(f32[384]{0:T(512)S(1)} %get-tuple-element.83) | copy-start | bytes 4612
  27.3 4.4 %copy-start.17 = (f32[384]{0:T(512)}, f32[384]{0:T(512)S(1)}, u32[]{:S(2)}) copy-start(f32[384]{0:T(512)S(1)} %get-tuple-element.84) | copy-start | bytes 4612
  27.3 4.4 %copy-start.19 = (f32[384]{0:T(512)}, f32[384]{0:T(512)S(1)}, u32[]{:S(2)}) copy-start(f32[384]{0:T(512)S(1)} %get-tuple-element.85) | copy-start | bytes 4612
  27.3 4.4 %copy-start.21 = (f32[384]{0:T(512)}, f32[384]{0:T(512)S(1)}, u32[]{:S(2)}) copy-start(f32[384]{0:T(512)S(1)} %get-tuple-element.86) | copy-start | bytes 4612
  27.3 4.4 %copy-start.23 = (f32[384]{0:T(512)}, f32[384]{0:T(512)S(1)}, u32[]{:S(2)}) copy-start(f32[384]{0:T(512)S(1)} %get-tuple-element.87) | copy-start | bytes 4612
  27.3 4.4 %copy-start.25 = (f32[384]{0:T(512)}, f32[384]{0:T(512)S(1)}, u32[]{:S(2)}) copy-start(f32[384]{0:T(512)S(1)} %get-tuple-element.88) | copy-start | bytes 4612
  27.4 4.4 %copy-start.27 = (f32[384]{0:T(512)}, f32[384]{0:T(512)S(1)}, u32[]{:S(2)}) copy-start(f32[384]{0:T(512)S(1)} %get-tuple-element.89) | copy-start | bytes 4612
  27.4 4.4 %copy-start.29 = (f32[384]{0:T(512)}, f32[384]{0:T(512)S(1)}, u32[]{:S(2)}) copy-start(f32[384]{0:T(512)S(1)} %get-tuple-element.90) | copy-start | bytes 4612
  27.4 4.4 %copy-start.31 = (f32[384]{0:T(512)}, f32[384]{0:T(512)S(1)}, u32[]{:S(2)}) copy-start(f32[384]{0:T(512)S(1)} %get-tuple-element.91) | copy-start | bytes 4612
  27.4 4.4 %copy-start.33 = (f32[384]{0:T(512)}, f32[384]{0:T(512)S(1)}, u32[]{:S(2)}) copy-start(f32[384]{0:T(512)S(1)} %get-tuple-element.92) | copy-start | bytes 4612
  27.4 4.4 %copy-start.35 = (f32[384]{0:T(512)}, f32[384]{0:T(512)S(1)}, u32[]{:S(2)}) copy-start(f32[384]{0:T(512)S(1)} %get-tuple-element.93) | copy-start | bytes 4612
  27.4 4.4 %copy-start.37 = (f32[384]{0:T(512)}, f32[384]{0:T(512)S(1)}, u32[]{:S(2)}) copy-start(f32[384]{0:T(512)S(1)} %get-tuple-element.94) | copy-start | bytes 4612
  27.4 4.4 %copy-start.39 = (f32[384]{0:T(512)}, f32[384]{0:T(512)S(1)}, u32[]{:S(2)}) copy-start(f32[384]{0:T(512)S(1)} %get-tuple-element.95) | copy-start | bytes 4612
  27.4 4.4 %copy-start.41 = (f32[384]{0:T(512)}, f32[384]{0:T(512)S(1)}, u32[]{:S(2)}) copy-start(f32[384]{0:T(512)S(1)} %get-tuple-element.96) | copy-start | bytes 4612
  27.4 4.4 %copy-start.43 = (f32[384]{0:T(512)}, f32[384]{0:T(512)S(1)}, u32[]{:S(2)}) copy-start(f32[384]{0:T(512)S(1)} %get-tuple-element.97) | copy-start | bytes 4612
  28.6 3.3 %copy-start.45 = (f32[384]{0:T(512)}, f32[384]{0:T(512)S(1)}, u32[]{:S(2)}) copy-start(f32[384]{0:T(512)S(1)} %get-tuple-element.117) | copy-start | bytes 4612
  28.6 3.3 %copy-start.47 = (f32[384]{0:T(512)}, f32[384]{0:T(512)S(1)}, u32[]{:S(2)}) copy-start(f32[384]{0:T(512)S(1)} %get-tuple-element.118) | copy-start | bytes 4612
  28.6 3.3 %copy-start.49 = (f32[384]{0:T(512)}, f32[384]{0:T(512)S(1)}, u32[]{:S(2)}) copy-start(f32[384]{0:T(512)S(1)} %get-tuple-element.119) | copy-start | bytes 4612
  28.6 3.3 %copy-start.51 = (f32[384]{0:T(512)}, f32[384]{0:T(512)S(1)}, u32[]{:S(2)}) copy-start(f32[384]{0:T(512)S(1)} %get-tuple-element.120) | copy-start | bytes 4612
  28.6 3.3 %copy-start.53 = (f32[384]{0:T(512)}, f32[384]{0:T(512)S(1)}, u32[]{:S(2)}) copy-start(f32[384]{0:T(512)S(1)} %get-tuple-element.121) | copy-start | bytes 4612
  28.6 3.3 %copy-start.55 = (f32[384]{0:T(512)}, f32[384]{0:T(512)S(1)}, u32[]{:S(2)}) copy-start(f32[384]{0:T(512)S(1)} %get-tuple-element.122) | copy-start | bytes 4612
  28.6 3.3 %copy-start.57 = (f32[384]{0:T(512)}, f32[384]{0:T(512)S(1)}, u32[]{:S(2)}) copy-start(f32[384]{0:T(512)S(1)} %get-tuple-element.123) | copy-start | bytes 4612
  28.6 3.3 %copy-start.59 = (f32[384]{0:T(512)}, f32[384]{0:T(512)S(1)}, u32[]{:S(2)}) copy-start(f32[384]{0:T(512)S(1)} %get-tuple-element.124) | copy-start | bytes 4612
  28.6 3.3 %copy-start.61 = (f32[384]{0:T(512)}, f32[384]{0:T(512)S(1)}, u32[]{:S(2)}) copy-start(f32[384]{0:T(512)S(1)} %get-tuple-element.125) | copy-start | bytes 4612
  38.6 3.6 %copy-start.7 = (f32[12,48,384]{2,1,0:T(8,128)}, f32[12,48,384]{2,1,0:T(8,128)S(1)}, u32[]{:S(2)}) copy-start(f32[12,48,384]{2,1,0:T(8,128)S(1)} %get-tuple-element.137) | copy-start | bytes 2654212
  38.6 5.3 %copy-start.12 = (f32[384]{0:T(512)S(1)}, f32[384]{0:T(512)}, u32[]{:S(2)}) copy-start(f32[384]{0:T(512)} %param.14) | copy-start | bytes 4612
  38.6 5.3 %copy-start.68 = (f32[384]{0:T(512)S(1)}, f32[384]{0:T(512)}, u32[]{:S(2)}) copy-start(f32[384]{0:T(512)} %param.15) | copy-start | bytes 4612
  39.0 4.7 %collective-permute-start.2 = (f32[2,576]{1,0:T(2,128)S(1)}, f32[2,576]{1,0:T(2,128)S(1)}, u32[]{:S(2)}, u32[]{:S(2)}) collective-permute-start(f32[2,576]{1,0:T(2,128)S(1)} %pad_maximum_fusion.2), channel_id=1, source_target_pairs={{0,1},{1,2},{2,3},{3,0},{4,5},{5,6},{6,7},{7,4},{8,9},{9,10},{10,1... | collective-permute-start | bytes 13832 | tf_op jit(solution)/shard_map/ppermute | solution.py:278
  39.1 4.6 %collective-permute-start.3 = (f32[2,576]{1,0:T(2,128)S(1)}, f32[2,576]{1,0:T(2,128)S(1)}, u32[]{:S(2)}, u32[]{:S(2)}) collective-permute-start(f32[2,576]{1,0:T(2,128)S(1)} %pad_maximum_fusion.2), channel_id=1, source_target_pairs={{0,2},{1,3},{2,0},{3,1},{4,6},{5,7},{6,4},{7,5},{8,10},{9,11},{10,... | collective-permute-start | bytes 13832 | tf_op jit(solution)/shard_map/ppermute | solution.py:278
  40.7 3.1 %collective-permute-start.4 = (f32[2,576]{1,0:T(2,128)S(1)}, f32[2,576]{1,0:T(2,128)S(1)}, u32[]{:S(2)}, u32[]{:S(2)}) collective-permute-start(f32[2,576]{1,0:T(2,128)S(1)} %pad_maximum_fusion.2), channel_id=1, source_target_pairs={{0,3},{1,0},{2,1},{3,2},{4,7},{5,4},{6,5},{7,6},{8,11},{9,8},{10,9... | collective-permute-start | bytes 13832 | tf_op jit(solution)/shard_map/ppermute | solution.py:278
  43.7 29.9 %copy-start.6 = (f32[576,384]{0,1:T(8,128)}, f32[576,384]{0,1:T(8,128)S(1)}, u32[]{:S(2)}) copy-start(f32[576,384]{0,1:T(8,128)S(1)} %copy.32) | copy-start | bytes 2654212
  44.9 49.1 %all-gather.3.cloned.1.call-start = ((), (), s32[]{:S(2)}) async-start(), calls=%async_computation.3 | async-start | bytes 2457600 | tf_op jit(solution)/shard_map/all_gather | solution.py:294
  73.6 20.4 %copy-start.67 = (f32[1536]{0:T(1024)S(1)}, f32[1536]{0:T(1024)}, u32[]{:S(2)}) copy-start(f32[1536]{0:T(1024)} %param.19) | copy-start | bytes 18436
  73.6 104.7 %reduce-scatter.2.cloned.1.call-start = ((), (), s32[]{:S(2)}) async-start(), calls=%async_computation.5 | async-start | bytes 2457600 | tf_op jit(solution)/shard_map/reduce_scatter | solution.py:307
  73.9 27.8 %slice-start = ((s8[4718592]{0:T(1024)(128)(4,1)}), s8[524288]{0:T(1024)(128)(4,1)S(1)}, s32[]{:S(2)}) async-start(s8[4718592]{0:T(1024)(128)(4,1)} %bitcast.42), calls=%async_computation.7 | async-start | bytes 1048576
  94.0 7.7 %slice-start.1 = ((s8[4718592]{0:T(1024)(128)(4,1)}), s8[4194304]{0:T(1024)(128)(4,1)S(1)}, s32[]{:S(2)}) async-start(s8[4718592]{0:T(1024)(128)(4,1)} %bitcast.42), calls=%async_computation.8 | async-start | bytes 8388608
  108.1 180.8 %all-reduce.6.cloned.1.call-start = ((), (), s32[]{:S(2)}) async-start(), calls=%async_computation.6 | async-start | bytes 172032 | tf_op jit(solution)/shard_map/psum | solution.py:324
  198.2 6.2 %copy-start.8 = (bf16[12,48,384]{2,1,0:T(8,128)(2,1)}, bf16[12,48,384]{2,1,0:T(8,128)(2,1)S(1)}, u32[]{:S(2)}) copy-start(bf16[12,48,384]{2,1,0:T(8,128)(2,1)S(1)} %convert_element_type.63) | copy-start | bytes 1327108
  199.7 73.7 %collective-permute-start.5 = (bf16[3,48,384]{2,1,0:T(8,128)(2,1)S(1)}, bf16[3,48,384]{2,1,0:T(8,128)(2,1)}, u32[]{:S(2)}, u32[]{:S(2)}) collective-permute-start(bf16[3,48,384]{2,1,0:T(8,128)(2,1)S(1)} %get-tuple-element.138), channel_id=1, source_target_pairs={{0,4},{4,8},{8,12},{12,16},{16,20},{20,24},{24,28},{28,0},{1,5},{5... | collective-permute-start | bytes 331784 | tf_op jit(solution)/shard_map/ppermute | solution.py:26
  201.1 72.3 %collective-permute-start.6 = (bf16[3,48,384]{2,1,0:T(8,128)(2,1)S(1)}, bf16[3,48,384]{2,1,0:T(8,128)(2,1)}, u32[]{:S(2)}, u32[]{:S(2)}) collective-permute-start(bf16[3,48,384]{2,1,0:T(8,128)(2,1)S(1)} %get-tuple-element.139), channel_id=1, source_target_pairs={{4,0},{8,4},{12,8},{16,12},{20,16},{24,20},{28,24},{0,28},{5,1},{9... | collective-permute-start | bytes 331784 | tf_op jit(solution)/shard_map/ppermute | solution.py:27
  207.5 65.9 %copy-start.9 = (bf16[12,48,384]{2,1,0:T(8,128)(2,1)S(1)}, bf16[12,48,384]{2,1,0:T(8,128)(2,1)}, u32[]{:S(2)}) copy-start(bf16[12,48,384]{2,1,0:T(8,128)(2,1)} %copy-done.8) | copy-start | bytes 1327108
  207.5 67.0 %copy-start.70 = (pred[18]{0:T(512)(128)(4,1)S(1)}, pred[18]{0:T(512)(128)(4,1)}, u32[]{:S(2)}) copy-start(pred[18]{0:T(512)(128)(4,1)} %copy-done.69) | copy-start | bytes 58
  (38 other events, 67.2 us)
Sparse Core Ops, SparseCore 0:
  45.0 20.3 all-gather.4
  73.7 20.1 all-gather.2
  108.2 30.6 reduce-scatter.1
  204.6 65.4 all-reduce.5

commit v5 on v4

--- a/solution.py
+++ b/solution.py
@@ -65,7 +65,7 @@
 
 def sum_kernel(
     factor, columns, values, out, pair_out, pair_in, parts, up_out, up_in, down_out, down_in,
-    pair_sent, pair_got, up_sent, up_got, down_sent, down_got,
+    lead_parts, lead_up_out, lead_up_in, lead_down_out, lead_down_in, pair_sent, pair_got, up_sent, up_got, down_sent, down_got,
 ):
     me = lax.axis_index("tile")
     side, place = me % 2, me // 2
@@ -95,26 +95,29 @@
 
     def swap(j):
         return pltpu.make_async_remote_copy(
-            src_ref=pair_out.at[j],
-            dst_ref=pair_in.at[j],
+            src_ref=pair_out.at[j] if j else pair_out.at[0, 0],
+            dst_ref=pair_in.at[j] if j else pair_in.at[0, 0],
             send_sem=pair_sent.at[j],
             recv_sem=pair_got.at[j],
             device_id={"tile": pair},
             device_id_type=MESH,
         )
 
+    def buffers(upward, j):
+        if j == 0:
+            return (lead_up_out, lead_up_in) if upward else (lead_down_out, lead_down_in)
+        out_ref, in_ref = (up_out, up_in) if upward else (down_out, down_in)
+        return out_ref.at[j], in_ref.at[j]
+
     def hop(upward, j, step):
-        src, dst, sent, got, peer = (
-            (up_out, up_in, up_sent, up_got, me + 2)
-            if upward
-            else (down_out, down_in, down_sent, down_got, me - 2)
-        )
+        src, dst = buffers(upward, j)
+        sent, got = (up_sent, up_got) if upward else (down_sent, down_got)
         return pltpu.make_async_remote_copy(
-            src_ref=src.at[j, step],
-            dst_ref=dst.at[j, step],
+            src_ref=src.at[step],
+            dst_ref=dst.at[step],
             send_sem=sent.at[j, step],
             recv_sem=got.at[j, step],
-            device_id={"tile": peer},
+            device_id={"tile": me + 2 if upward else me - 2},
             device_id_type=MESH,
         )
 
@@ -129,14 +132,6 @@
             * factor
         )
 
-    for j in range(chunks):
-        for line in range(LINES):
-            pair_out[j, line] = block(line, 1 - side, j).astype(jnp.bfloat16)
-        swap(j).start()
-    for j in range(chunks):
-        for line in range(LINES):
-            parts[j, line] = block(line, side, j)
-
     def take(j):
         swap(j).wait_recv()
         parts[j] = parts[j] + pair_in[j].astype(jnp.float32)
@@ -148,17 +143,17 @@
             @pl.when(back <= step)
             def _(upward=upward, back=back):
                 dest = LINES - 1 - step + place if upward else step - back
-                total = up_out if upward else down_out
-                total[j, step] = parts[j, dest].astype(jnp.bfloat16)
+                total, got = buffers(upward, j)
+                held = parts.at[j] if j else lead_parts
+                total[step] = held[dest].astype(jnp.bfloat16)
 
                 if step:
 
                     @pl.when(back > 0)
                     def _():
                         hop(upward, j, step - 1).wait_recv()
-                        got = up_in if upward else down_in
-                        total[j, step] = (
-                            parts[j, dest] + got[j, step - 1].astype(jnp.float32)
+                        total[step] = (
+                            held[dest] + got[step - 1].astype(jnp.float32)
                         ).astype(jnp.bfloat16)
 
                 hop(upward, j, step).start()
@@ -177,16 +172,50 @@
             hop(False, j, LINES - 2).wait_recv()
             out[:, where] += down_in[j, LINES - 2].astype(jnp.float32)
 
-    for turn in range(chunks + 1):
+    def offer(j):
+        for line in range(LINES):
+            pair_out[j, line] = block(line, 1 - side, j).astype(jnp.bfloat16)
+        swap(j).start()
+
+    offer(1)
+    for line in range(LINES):
+        for which in range(2):
+            lead_parts[line, which * rows : (which + 1) * rows] = block(line, which, 0)
+    send(0, 0)
+    for j in range(2, chunks):
+        offer(j)
+    send(0, 1)
+    for j in range(1, chunks):
+        for line in range(LINES):
+            parts[j, line] = block(line, side, j)
+    send(0, 2)
+
+    @pl.when(has_down)
+    def _():
+        hop(True, 0, LINES - 2).wait_recv()
+        lead_parts[place] += lead_up_in[LINES - 2].astype(jnp.float32)
+
+    @pl.when(has_up)
+    def _():
+        hop(False, 0, LINES - 2).wait_recv()
+        lead_parts[place] += lead_down_in[LINES - 2].astype(jnp.float32)
+
+    theirs = pl.ds(pl.multiple_of((1 - side) * rows, rows), rows)
+    ours = pl.ds(pl.multiple_of(side * rows, rows), rows)
+    pair_out[0, 0] = lead_parts[place, theirs].astype(jnp.bfloat16)
+    swap(0).start()
+    for turn in range(1, chunks + 1):
         if turn < chunks:
             take(turn)
             send(turn, 0)
-        if turn > 0:
+        if turn > 1:
             send(turn - 1, 2)
         if turn < chunks:
             send(turn, 1)
-        if turn > 0:
+        if turn > 1:
             finish(turn - 1)
+    swap(0).wait_recv()
+    out[:, 0:CHUNK] = lead_parts[place, ours] + pair_in[0, 0].astype(jnp.float32)
     for j in range(chunks):
         swap(j).wait_send()
         for step in range(LINES - 1):
@@ -222,6 +251,8 @@
             pair_buffer,
             pltpu.VMEM((chunks, LINES, rows, CHUNK), jnp.float32),
             *([line_buffer] * 4),
+            pltpu.VMEM((LINES, 2 * rows, CHUNK), jnp.float32),
+            *([pltpu.VMEM((hops, 2 * rows, CHUNK), jnp.bfloat16)] * 4),
             *([pltpu.SemaphoreType.DMA((chunks,))] * 2),
             *([pltpu.SemaphoreType.DMA((chunks, hops))] * 4),
         ],

time: 299 us -> 284 us (0.950)
  Pallas kernels: 134 us -> 119 us
    pallas_call x2, Pallas kernels: 134 us -> 119 us  [summed_product(): pl.pallas_call(functools.partial(sum_kernel, factor), out_shape=jax.Shape...]
  transfers between devices with their start and end apart: 12 -> 12, of which waited for: 1 -> 1; matrix products, arithmetic and copies ran while one was open for 12% -> 13% of each run, Pallas kernels for 45% -> 42%
where the time goes in v5:
time: 284 us; the launch traced here: 283 us
  Pallas kernels  119 us (42%)
  other arithmetic  36.2 us (13%)
  blocking collectives  32.9 us (12%)
  matrix products  25.9 us (9%)
  local copies, waits for them, and re-layouts  22 us (8%)
  starting transfers between devices  20.2 us (7%)
  between operations  15.5 us (5%)
  waiting for transfers between devices  11.5 us (4%)
    pallas_call x2, Pallas kernels, summed_product(): pl.pallas_call(functools.partial(sum_kernel, factor), out_shape=jax.Shape...  119 us
    all_to_all x1, blocking collectives, shards(): lax.all_to_all(found.reshape(tiles, capacity, chan_dev), 'tile', split_ax...  26.8 us
    all_gather x1, waiting for transfers between devices, shards(): upstream_all = lax.all_gather(upstream, 'chan', axis=1, tiled=True)  11.4 us
    unnamed x152, local copies, waits for them, and re-layouts  9.26 us
    dot_general x1, matrix products, shards(): preact = jnp.dot(ln_out, w_in, preferred_element_type=jnp.float32) + b_in  8.7 us
    dot_general x1, matrix products, shards(): lax.dot_general(scaled, w_out, (((1,), (1,)), ((), ())), preferred_elemen...  7.66 us
    add x1, other arithmetic, depthwise(): total = total + kernel[row_off * KSIZE + col_off] * window  7.35 us
    all_to_all x1, starting transfers between devices, shards(): lax.all_to_all(request, 'tile', split_axis=0, concat_axis=0, tiled=True)  7.28 us
  transfers between devices with their start and end apart: 12, of which 1 were waited for; matrix products, arithmetic and copies ran while one was open for 13% of the time, Pallas kernels for 42%

profile of v5, /device:TPU:0, one launch (start us, length us, event | category | flops | bytes accessed | tf_op | source)
XLA Modules:
  0.0 282.9 jit_solution(6665959808271129661)
XLA Ops:
  7.2 0.8 add_select_fusion.1
  8.0 1.4 reduce-window.6
  10.0 0.7 multiply_add_fusion.1
  10.7 0.3 select_reduce_fusion
  11.0 0.7 all_to_all.9
  11.7 7.3 %all-to-all-start = ((s32[8,1,144]{2,1,0:T(1,128)}), s32[8,1,144]{2,1,0:T(1,128)S(1)}, u32[]{:S(2)}, u32[]{:S(2)}) async-start(s32[8,1,144]{2,1,0:T(1,128)} %all_to_all.9), calls=%async_computation | async-start | bytes 16384 | tf_op jit(solution)/shard_map/all_to_all | solution.py:288
  19.0 1.0 fusion.119
  20.0 2.0 collective-permute-start
  22.1 2.8 collective-permute-start.1
  24.8 1.2 slice_reduce_fusion.53
  26.1 1.2 slice_reduce_fusion.54
  27.4 1.1 slice_reduce_fusion.52
  28.9 2.6 fusion.7
  32.0 6.6 %fusion.117 = (f32[12,48]{1,0:T(8,128)S(1)}, f32[12,48,384]{2,1,0:T(8,128)S(1)}) fusion(f32[384]{0:T(512)S(1)} %get-tuple-element.126, f32[384]{0:T(512)S(1)} %get-tuple-element.127, f32[384]{0:T(512)S(1)} %get-tuple-element.80, f32[18,48,384]{2,1,0:T(8,128)S(1)} %convert_select_fusion.1, f32[384]{0:T(512)S(1)} %get-tuple-element.81, ...), kind=kLoop, calls=%fused_computation.354 | loop fusion | flops 21675456 | bytes 8507648 | tf_op jit(solution)/shard_map/reduce_sum | solution.py:303
  39.1 1.5 collective-permute-start.3
  40.7 1.4 collective-permute-start.4
  42.2 1.5 copy.32
  43.9 1.0 add_convert_fusion.1
  44.9 26.8 %all_to_all.14 = bf16[8,144,384]{2,1,0:T(8,128)(2,1)S(1)} all-to-all(bf16[8,144,384]{2,1,0:T(8,128)(2,1)} %bitcast.36), channel_id=1, replica_groups=mesh['tile'=8,'chan'=4] {'tile'}, dimensions={0} | all-to-all | bytes 1769472 | tf_op jit(solution)/shard_map/all_to_all | solution.py:293
  71.7 1.9 fusion.11
  73.9 8.7 %multiply_convert_fusion.1 = (bf16[576,1536]{1,0:T(8,128)(2,1)}, f32[576,1536]{1,0:T(8,128)}) fusion(f32[1536]{0:T(1024)S(1)} %copy-done.71, bf16[576,1536]{0,1:T(8,128)(2,1)} %all-gather.5.cloned.1.call-done, bf16[1536,1536]{1,0:T(8,128)(2,1)} %param.16), kind=kOutput, calls=%fused_computation.10 | convolution fusion | flops 2723217408 | bytes 11802624 | tf_op jit(solution)/shard_map/dot_general | solution.py:327
  82.6 11.4 %all-gather.3.cloned.1.call-done = bf16[576,1536]{0,1:T(8,128)(2,1)} async-done(((bf16[576,384]{0,1:T(8,128)(2,1)}), bf16[576,1536]{0,1:T(8,128)(2,1)}) %all-gather.3.cloned.1.call-update) | async-done | bytes 1769488 | tf_op jit(solution)/shard_map/all_gather | solution.py:325
  94.0 7.7 %fusion.6.values = bf16[576,1536]{1,0:T(8,128)(2,1)S(1)} fusion(f32[576,1536]{1,0:T(8,128)} %get-tuple-element.147, bf16[1536,1536]{1,0:T(8,128)(2,1)} %param.18, bf16[576,1536]{0,1:T(8,128)(2,1)} %all-gather.3.cloned.1.call-done, f32[1536]{0:T(1024)S(1)} %copy-done.67), kind=kOutput, calls=%fused_computation.9 | convolution fusion | flops 2729410560 | bytes 11802624 | tf_op jit(solution)/shard_map/dot_general | solution.py:331
  101.7 5.1 %convolution_convert_fusion = bf16[576,1536]{0,1:T(8,128)(2,1)} fusion(bf16[576,1536]{1,0:T(8,128)(2,1)S(1)} %fusion.6.values, bf16[1536,1536]{1,0:T(8,128)(2,1)S(1)} %bitcast.43), kind=kOutput, calls=%fused_computation.13 | convolution fusion | flops 2718793728 | bytes 8257536 | tf_op jit(solution)/shard_map/dot_general | solution.py:335
  106.8 1.3 copy-done.3
  108.1 2.1 fusion.103.columns
  110.2 61.3 %shard_map.129 = f32[192,1536]{1,0:T(8,128)S(1)} custom-call(bf16[1536,576]{1,0:T(8,128)(2,1)S(1)} %fusion.103.columns, bf16[576,1536]{1,0:T(8,128)(2,1)S(1)} %copy-done.2), custom_call_target="tpu_custom_call" | custom-call | flops 2717908992 | bytes 100000000 | tf_op jit(solution)/shard_map/pallas_call | solution.py:244
  171.6 1.6 fusion.12
  173.2 6.0 %all-reduce.3 = (f32[576]{0:T(1024)S(1)}, f32[576]{0:T(1024)S(1)}) all-reduce(f32[576]{0:T(1024)S(1)} %get-tuple-element.78, f32[576]{0:T(1024)S(1)} %get-tuple-element.77), channel_id=1, replica_groups=mesh['tile'=8,'chan'=4] {'chan'}, use_global_device_ids=true, to_apply=%region_10.11 | all-reduce | flops 1152 | bytes 9216 | tf_op jit(solution)/shard_map/psum | solution.py:342
  179.3 2.6 subtract_multiply_fusion
  181.9 2.4 copy.35
  184.3 3.1 %multiply_reduce_fusion.1 = (f32[384]{0:T(512)S(1)}, f32[384]{0:T(512)S(1)}, f32[384]{0:T(512)S(1)}, f32[384]{0:T(512)S(1)}, f32[384]{0:T(512)S(1)}, /*index=5*/...) fusion(f32[12,48,384]{2,1,0:T(8,128)} %bitcast.29, ...), kind=kLoop, calls=%fused_computation.211 | loop fusion | flops 7955712 | bytes 4893696 | tf_op jit(solution)/shard_map/reduce_sum | solution.py:353
  187.5 2.1 multiply_reduce_fusion.19
  189.5 1.5 multiply_reduce_fusion.37
  191.9 0.7 broadcast_multiply_fusion
  192.5 1.6 collective-permute-start.5
  194.1 3.2 %collective-permute-start.6 = (bf16[3,48,384]{2,1,0:T(8,128)(2,1)S(1)}, bf16[3,48,384]{2,1,0:T(8,128)(2,1)}, u32[]{:S(2)}, u32[]{:S(2)}) collective-permute-start(bf16[3,48,384]{2,1,0:T(8,128)(2,1)S(1)} %get-tuple-element.139), channel_id=1, source_target_pairs={{4,0},{8,4},{12,8},{16,12},{20,16},{24,20},{28,24},{0,28},{5,1},{9... | collective-permute-start | bytes 331784 | tf_op jit(solution)/shard_map/ppermute | solution.py:27
  197.4 1.5 copy-done.1
  198.9 1.5 copy-done.4
  200.4 57.5 %shard_map.130 = f32[192,1536]{1,0:T(8,128)S(1)} custom-call(bf16[1536,576]{1,0:T(8,128)(2,1)S(1)} %bitcast.28, bf16[576,1536]{1,0:T(8,128)(2,1)S(1)} %copy-done.4), custom_call_target="tpu_custom_call" | custom-call | flops 2717908992 | bytes 100000000 | tf_op jit(solution)/shard_map/pallas_call | solution.py:244
  258.2 1.0 pad_maximum_fusion.1
  259.7 7.4 %fusion.99 = f32[12,48,384]{2,1,0:T(8,128)} fusion(f32[18,48,384]{2,1,0:T(8,128)S(1)} %convert_select_fusion, f32[384]{0:T(512)S(1)} %copy-done.64, f32[384]{0:T(512)S(1)} %copy-done.66, f32[384]{0:T(512)S(1)} %get-tuple-element.80, f32[384]{0:T(512)S(1)} %get-tuple-element.81, f32[384]{0:T(512)S(1)} %copy-done.14, f32[384]{0:T(512)S(1)} %copy-done.16, ...), kind=kLoop, calls=%fused_computation.200 | loop fusion | flops 21454848 | bytes 8505344 | tf_op jit(solution)/shard_map/add | solution.py:43
  267.0 2.4 copy.36
  269.5 2.2 add_convert_fusion
  271.7 2.0 copy.37
  273.7 1.0 copy.43
  274.7 1.0 copy.44
  275.7 0.6 copy.45
  (244 shorter events, 3.1 us)
Async XLA Ops:
  7.2 21.7 %copy-start = (bf16[1152,384]{1,0:T(8,128)(2,1)S(1)}, bf16[1152,384]{1,0:T(8,128)(2,1)}, u32[]{:S(2)}) copy-start(bf16[1152,384]{1,0:T(8,128)(2,1)} %param.10) | copy-start | bytes 2654212
  11.7 17.0 %all-to-all-start = ((s32[8,1,144]{2,1,0:T(1,128)}), s32[8,1,144]{2,1,0:T(1,128)S(1)}, u32[]{:S(2)}, u32[]{:S(2)}) async-start(s32[8,1,144]{2,1,0:T(1,128)} %all_to_all.9), calls=%async_computation | async-start | bytes 16384 | tf_op jit(solution)/shard_map/all_to_all | solution.py:288
  19.0 54.9 %all-gather.5.cloned.1.call-start = ((), (), s32[]{:S(2)}) async-start(), calls=%async_computation.4 | async-start | bytes 2457600 | tf_op jit(solution)/shard_map/all_gather | solution.py:318
  20.0 11.4 %collective-permute-start = (bf16[3,48,384]{2,1,0:T(8,128)(2,1)S(1)}, bf16[3,48,384]{2,1,0:T(8,128)(2,1)S(1)}, u32[]{:S(2)}, u32[]{:S(2)}) collective-permute-start(bf16[3,48,384]{2,1,0:T(8,128)(2,1)S(1)} %bitcast.39), channel_id=1, source_target_pairs={{0,4},{4,8},{8,12},{12,16},{16,20},{20,24},{24,28},{28,0},{1,5},{5... | collective-permute-start | bytes 331784 | tf_op jit(solution)/shard_map/ppermute | solution.py:26
  22.1 9.4 %collective-permute-start.1 = (bf16[3,48,384]{2,1,0:T(8,128)(2,1)S(1)}, bf16[3,48,384]{2,1,0:T(8,128)(2,1)S(1)}, u32[]{:S(2)}, u32[]{:S(2)}) collective-permute-start(bf16[3,48,384]{2,1,0:T(8,128)(2,1)S(1)} %bitcast.38), channel_id=1, source_target_pairs={{4,0},{8,4},{12,8},{16,12},{20,16},{24,20},{28,24},{0,28},{5,1},{9... | collective-permute-start | bytes 331784 | tf_op jit(solution)/shard_map/ppermute | solution.py:27
  27.3 4.4 %copy-start.13 = (f32[384]{0:T(512)}, f32[384]{0:T(512)S(1)}, u32[]{:S(2)}) copy-start(f32[384]{0:T(512)S(1)} %get-tuple-element.82) | copy-start | bytes 4612
  27.3 4.4 %copy-start.15 = (f32[384]{0:T(512)}, f32[384]{0:T(512)S(1)}, u32[]{:S(2)}) copy-start(f32[384]{0:T(512)S(1)} %get-tuple-element.83) | copy-start | bytes 4612
  27.3 4.4 %copy-start.17 = (f32[384]{0:T(512)}, f32[384]{0:T(512)S(1)}, u32[]{:S(2)}) copy-start(f32[384]{0:T(512)S(1)} %get-tuple-element.84) | copy-start | bytes 4612
  27.3 4.4 %copy-start.19 = (f32[384]{0:T(512)}, f32[384]{0:T(512)S(1)}, u32[]{:S(2)}) copy-start(f32[384]{0:T(512)S(1)} %get-tuple-element.85) | copy-start | bytes 4612
  27.3 4.4 %copy-start.21 = (f32[384]{0:T(512)}, f32[384]{0:T(512)S(1)}, u32[]{:S(2)}) copy-start(f32[384]{0:T(512)S(1)} %get-tuple-element.86) | copy-start | bytes 4612
  27.3 4.4 %copy-start.23 = (f32[384]{0:T(512)}, f32[384]{0:T(512)S(1)}, u32[]{:S(2)}) copy-start(f32[384]{0:T(512)S(1)} %get-tuple-element.87) | copy-start | bytes 4612
  27.3 4.4 %copy-start.25 = (f32[384]{0:T(512)}, f32[384]{0:T(512)S(1)}, u32[]{:S(2)}) copy-start(f32[384]{0:T(512)S(1)} %get-tuple-element.88) | copy-start | bytes 4612
  27.4 4.4 %copy-start.27 = (f32[384]{0:T(512)}, f32[384]{0:T(512)S(1)}, u32[]{:S(2)}) copy-start(f32[384]{0:T(512)S(1)} %get-tuple-element.89) | copy-start | bytes 4612
  27.4 4.4 %copy-start.29 = (f32[384]{0:T(512)}, f32[384]{0:T(512)S(1)}, u32[]{:S(2)}) copy-start(f32[384]{0:T(512)S(1)} %get-tuple-element.90) | copy-start | bytes 4612
  27.4 4.4 %copy-start.31 = (f32[384]{0:T(512)}, f32[384]{0:T(512)S(1)}, u32[]{:S(2)}) copy-start(f32[384]{0:T(512)S(1)} %get-tuple-element.91) | copy-start | bytes 4612
  27.4 4.4 %copy-start.33 = (f32[384]{0:T(512)}, f32[384]{0:T(512)S(1)}, u32[]{:S(2)}) copy-start(f32[384]{0:T(512)S(1)} %get-tuple-element.92) | copy-start | bytes 4612
  27.4 4.4 %copy-start.35 = (f32[384]{0:T(512)}, f32[384]{0:T(512)S(1)}, u32[]{:S(2)}) copy-start(f32[384]{0:T(512)S(1)} %get-tuple-element.93) | copy-start | bytes 4612
  27.4 4.4 %copy-start.37 = (f32[384]{0:T(512)}, f32[384]{0:T(512)S(1)}, u32[]{:S(2)}) copy-start(f32[384]{0:T(512)S(1)} %get-tuple-element.94) | copy-start | bytes 4612
  27.4 4.4 %copy-start.39 = (f32[384]{0:T(512)}, f32[384]{0:T(512)S(1)}, u32[]{:S(2)}) copy-start(f32[384]{0:T(512)S(1)} %get-tuple-element.95) | copy-start | bytes 4612
  27.4 4.4 %copy-start.41 = (f32[384]{0:T(512)}, f32[384]{0:T(512)S(1)}, u32[]{:S(2)}) copy-start(f32[384]{0:T(512)S(1)} %get-tuple-element.96) | copy-start | bytes 4612
  27.4 4.4 %copy-start.43 = (f32[384]{0:T(512)}, f32[384]{0:T(512)S(1)}, u32[]{:S(2)}) copy-start(f32[384]{0:T(512)S(1)} %get-tuple-element.97) | copy-start | bytes 4612
  28.6 3.3 %copy-start.45 = (f32[384]{0:T(512)}, f32[384]{0:T(512)S(1)}, u32[]{:S(2)}) copy-start(f32[384]{0:T(512)S(1)} %get-tuple-element.117) | copy-start | bytes 4612
  28.6 3.3 %copy-start.47 = (f32[384]{0:T(512)}, f32[384]{0:T(512)S(1)}, u32[]{:S(2)}) copy-start(f32[384]{0:T(512)S(1)} %get-tuple-element.118) | copy-start | bytes 4612
  28.6 3.3 %copy-start.49 = (f32[384]{0:T(512)}, f32[384]{0:T(512)S(1)}, u32[]{:S(2)}) copy-start(f32[384]{0:T(512)S(1)} %get-tuple-element.119) | copy-start | bytes 4612
  28.6 3.3 %copy-start.51 = (f32[384]{0:T(512)}, f32[384]{0:T(512)S(1)}, u32[]{:S(2)}) copy-start(f32[384]{0:T(512)S(1)} %get-tuple-element.120) | copy-start | bytes 4612
  28.6 3.3 %copy-start.53 = (f32[384]{0:T(512)}, f32[384]{0:T(512)S(1)}, u32[]{:S(2)}) copy-start(f32[384]{0:T(512)S(1)} %get-tuple-element.121) | copy-start | bytes 4612
  28.6 3.3 %copy-start.55 = (f32[384]{0:T(512)}, f32[384]{0:T(512)S(1)}, u32[]{:S(2)}) copy-start(f32[384]{0:T(512)S(1)} %get-tuple-element.122) | copy-start | bytes 4612
  28.6 3.3 %copy-start.57 = (f32[384]{0:T(512)}, f32[384]{0:T(512)S(1)}, u32[]{:S(2)}) copy-start(f32[384]{0:T(512)S(1)} %get-tuple-element.123) | copy-start | bytes 4612
  28.6 3.3 %copy-start.59 = (f32[384]{0:T(512)}, f32[384]{0:T(512)S(1)}, u32[]{:S(2)}) copy-start(f32[384]{0:T(512)S(1)} %get-tuple-element.124) | copy-start | bytes 4612
  28.6 3.3 %copy-start.61 = (f32[384]{0:T(512)}, f32[384]{0:T(512)S(1)}, u32[]{:S(2)}) copy-start(f32[384]{0:T(512)S(1)} %get-tuple-element.125) | copy-start | bytes 4612
  38.6 3.6 %copy-start.7 = (f32[12,48,384]{2,1,0:T(8,128)}, f32[12,48,384]{2,1,0:T(8,128)S(1)}, u32[]{:S(2)}) copy-start(f32[12,48,384]{2,1,0:T(8,128)S(1)} %get-tuple-element.137) | copy-start | bytes 2654212
  38.6 5.3 %copy-start.12 = (f32[384]{0:T(512)S(1)}, f32[384]{0:T(512)}, u32[]{:S(2)}) copy-start(f32[384]{0:T(512)} %param.14) | copy-start | bytes 4612
  38.6 5.3 %copy-start.68 = (f32[384]{0:T(512)S(1)}, f32[384]{0:T(512)}, u32[]{:S(2)}) copy-start(f32[384]{0:T(512)} %param.15) | copy-start | bytes 4612
  39.0 4.7 %collective-permute-start.2 = (f32[2,576]{1,0:T(2,128)S(1)}, f32[2,576]{1,0:T(2,128)S(1)}, u32[]{:S(2)}, u32[]{:S(2)}) collective-permute-start(f32[2,576]{1,0:T(2,128)S(1)} %pad_maximum_fusion.2), channel_id=1, source_target_pairs={{0,1},{1,2},{2,3},{3,0},{4,5},{5,6},{6,7},{7,4},{8,9},{9,10},{10,1... | collective-permute-start | bytes 13832 | tf_op jit(solution)/shard_map/ppermute | solution.py:309
  39.1 4.6 %collective-permute-start.3 = (f32[2,576]{1,0:T(2,128)S(1)}, f32[2,576]{1,0:T(2,128)S(1)}, u32[]{:S(2)}, u32[]{:S(2)}) collective-permute-start(f32[2,576]{1,0:T(2,128)S(1)} %pad_maximum_fusion.2), channel_id=1, source_target_pairs={{0,2},{1,3},{2,0},{3,1},{4,6},{5,7},{6,4},{7,5},{8,10},{9,11},{10,... | collective-permute-start | bytes 13832 | tf_op jit(solution)/shard_map/ppermute | solution.py:309
  40.7 3.1 %collective-permute-start.4 = (f32[2,576]{1,0:T(2,128)S(1)}, f32[2,576]{1,0:T(2,128)S(1)}, u32[]{:S(2)}, u32[]{:S(2)}) collective-permute-start(f32[2,576]{1,0:T(2,128)S(1)} %pad_maximum_fusion.2), channel_id=1, source_target_pairs={{0,3},{1,0},{2,1},{3,2},{4,7},{5,4},{6,5},{7,6},{8,11},{9,8},{10,9... | collective-permute-start | bytes 13832 | tf_op jit(solution)/shard_map/ppermute | solution.py:309
  43.7 29.9 %copy-start.6 = (f32[576,384]{0,1:T(8,128)}, f32[576,384]{0,1:T(8,128)S(1)}, u32[]{:S(2)}) copy-start(f32[576,384]{0,1:T(8,128)S(1)} %copy.32) | copy-start | bytes 2654212
  44.9 49.1 %all-gather.3.cloned.1.call-start = ((), (), s32[]{:S(2)}) async-start(), calls=%async_computation.3 | async-start | bytes 2457600 | tf_op jit(solution)/shard_map/all_gather | solution.py:325
  73.6 20.4 %copy-start.67 = (f32[1536]{0:T(1024)S(1)}, f32[1536]{0:T(1024)}, u32[]{:S(2)}) copy-start(f32[1536]{0:T(1024)} %param.19) | copy-start | bytes 18436
  73.6 97.9 %reduce-scatter.2.cloned.1.call-start = ((), (), s32[]{:S(2)}) async-start(), calls=%async_computation.5 | async-start | bytes 2457600 | tf_op jit(solution)/shard_map/reduce_scatter | solution.py:338
  73.9 27.8 %slice-start = ((s8[4718592]{0:T(1024)(128)(4,1)}), s8[524288]{0:T(1024)(128)(4,1)S(1)}, s32[]{:S(2)}) async-start(s8[4718592]{0:T(1024)(128)(4,1)} %bitcast.42), calls=%async_computation.7 | async-start | bytes 1048576
  94.0 7.7 %slice-start.1 = ((s8[4718592]{0:T(1024)(128)(4,1)}), s8[4194304]{0:T(1024)(128)(4,1)S(1)}, s32[]{:S(2)}) async-start(s8[4718592]{0:T(1024)(128)(4,1)} %bitcast.42), calls=%async_computation.8 | async-start | bytes 8388608
  108.1 165.6 %all-reduce.6.cloned.1.call-start = ((), (), s32[]{:S(2)}) async-start(), calls=%async_computation.6 | async-start | bytes 172032 | tf_op jit(solution)/shard_map/psum | solution.py:355
  191.1 6.2 %copy-start.8 = (bf16[12,48,384]{2,1,0:T(8,128)(2,1)}, bf16[12,48,384]{2,1,0:T(8,128)(2,1)S(1)}, u32[]{:S(2)}) copy-start(bf16[12,48,384]{2,1,0:T(8,128)(2,1)S(1)} %convert_element_type.63) | copy-start | bytes 1327108
  192.5 65.6 %collective-permute-start.5 = (bf16[3,48,384]{2,1,0:T(8,128)(2,1)S(1)}, bf16[3,48,384]{2,1,0:T(8,128)(2,1)}, u32[]{:S(2)}, u32[]{:S(2)}) collective-permute-start(bf16[3,48,384]{2,1,0:T(8,128)(2,1)S(1)} %get-tuple-element.138), channel_id=1, source_target_pairs={{0,4},{4,8},{8,12},{12,16},{16,20},{20,24},{24,28},{28,0},{1,5},{5... | collective-permute-start | bytes 331784 | tf_op jit(solution)/shard_map/ppermute | solution.py:26
  194.1 64.0 %collective-permute-start.6 = (bf16[3,48,384]{2,1,0:T(8,128)(2,1)S(1)}, bf16[3,48,384]{2,1,0:T(8,128)(2,1)}, u32[]{:S(2)}, u32[]{:S(2)}) collective-permute-start(bf16[3,48,384]{2,1,0:T(8,128)(2,1)S(1)} %get-tuple-element.139), channel_id=1, source_target_pairs={{4,0},{8,4},{12,8},{16,12},{20,16},{24,20},{28,24},{0,28},{5,1},{9... | collective-permute-start | bytes 331784 | tf_op jit(solution)/shard_map/ppermute | solution.py:27
  200.4 57.8 %copy-start.9 = (bf16[12,48,384]{2,1,0:T(8,128)(2,1)S(1)}, bf16[12,48,384]{2,1,0:T(8,128)(2,1)}, u32[]{:S(2)}) copy-start(bf16[12,48,384]{2,1,0:T(8,128)(2,1)} %copy-done.8) | copy-start | bytes 1327108
  200.4 58.9 %copy-start.70 = (pred[18]{0:T(512)(128)(4,1)S(1)}, pred[18]{0:T(512)(128)(4,1)}, u32[]{:S(2)}) copy-start(pred[18]{0:T(512)(128)(4,1)} %copy-done.69) | copy-start | bytes 58
  (38 other events, 67.2 us)
Sparse Core Ops, SparseCore 0:
  45.0 20.3 all-gather.4
  73.7 20.1 all-gather.2
  108.2 30.6 reduce-scatter.1
  197.5 65.5 all-reduce.5
